TPU v7x, 32 devices: a whole 2x2x4 slice. The times are simulated.
32 devices in a mesh: tm: 4 (over z), row: 2 (over x), col: 4 (over y, core).
Axes of the slice: x: 2, y: 2, z: 4, core: 2. Of those that a mesh axis runs over, the one named last changes fastest.
Arguments:
- occ_rows: float32 [1024, 512], P('row', ('tm', 'col')), may hold values from -1.2613447 to 1.2613447
- emp_rows: float32 [1024, 1536], P('row', ('tm', 'col')), may hold values from -0.9584147 to 0.9584147
- occ_cols: float32 [2048, 512], P('col', ('tm', 'row')), may hold values from -1.2613447 to 1.2613447
- emp_cols: float32 [2048, 1536], P('col', ('tm', 'row')), may hold values from -0.9584147 to 0.9584147
- occ_energy: float32 [1, 512], P(None, ('tm', 'col')), may hold values from 0.05 to 2
- emp_energy: float32 [1, 1536], P(None, ('tm', 'col')), may hold values from 0.05 to 2
- times: float32 [4], P('tm'), may hold values from 0.1 to 1.5
- freq_weight: float32 [4, 4], replicated, may hold values from -3 to 3
Outputs:
- spectrum: float32 [4, 2048, 1024], P('tm', 'col', 'row')
All inputs are finite; a program needn't handle non-finite values.
Results may differ from a plain program's by a relative error of at most 0.00019.
Values sent between devices are 32-bit elements; how exact they have to be, the bound alone decides.
No kernel may reach another device: no remote copies, remote signals or barrier semaphores. Data moves between devices by JAX's collectives and lax.ppermute only.
A program may use at most 64 MiB of HBM per device.

v0:
```python
import jax
import jax.numpy as jnp
from jax import lax
from jax.sharding import PartitionSpec as P

GP = 2048


precise = lax.Precision.HIGHEST


def cosine_table(first_col, number_cols, number_modes):
    column = first_col + jnp.arange(number_cols, dtype=jnp.int32)
    wave = jnp.arange(number_modes, dtype=jnp.int32)
    phase = (2 * column[:, None] + 1) * wave[None, :] % (4 * GP)
    return jnp.sqrt(2.0 / GP) * jnp.cos(jnp.pi * phase.astype(jnp.float32) / (2.0 * GP))


def make_folder(times, row_orbitals, energies, piece):
    breadth = piece.shape[1]
    decays = jnp.exp(-(times[:, None] * energies))
    scaled = (row_orbitals[None, :, :] * decays[:, None, :]).reshape(-1, breadth)
    return lax.dot_general(scaled, piece, (((1,), (1,)), ((), ())), precision=precise)


def per_device(occ_rows, emp_rows, occ_cols, emp_cols, occ_energy, emp_energy, times, freq_weight):
    number_times = times.shape[0]
    number_rows = occ_rows.shape[0]
    number_cols = occ_cols.shape[0]
    mode_share = GP // lax.axis_size("col")
    gathered_occ, gathered_emp, energy_occ, energy_emp = (
        lax.all_gather(occ_rows, ("tm", "col"), axis=1, tiled=True),
        lax.all_gather(emp_rows, ("tm", "col"), axis=1, tiled=True),
        lax.all_gather(occ_energy, ("tm", "col"), axis=1, tiled=True),
        lax.all_gather(emp_energy, ("tm", "col"), axis=1, tiled=True),
    )
    green_occ = make_folder(
        times, gathered_occ, energy_occ, lax.all_gather(occ_cols, ("tm", "row"), axis=1, tiled=True)
    )
    green_emp = make_folder(
        times, gathered_emp, energy_emp, lax.all_gather(emp_cols, ("tm", "row"), axis=1, tiled=True)
    )
    product = green_occ * green_emp
    col_first = lax.axis_index("col") * number_cols
    mode_rows = lax.psum_scatter(
        lax.dot_general(
            cosine_table(col_first, number_cols, mode_share * lax.axis_size("col")),
            product,
            (((0,), (1,)), ((), ())),
            precision=precise,
        ),
        "col",
        scatter_dimension=0,
        tiled=True,
    )
    series = mode_rows.reshape(mode_share, number_times, number_rows)
    own_weights = lax.dynamic_slice_in_dim(
        freq_weight, lax.axis_index("tm") * number_times, number_times, 1
    )
    return lax.psum_scatter(
        jnp.einsum("wt,gtr->wgr", own_weights, series, precision=precise),
        "tm",
        scatter_dimension=0,
        tiled=True,
    )


def solution(mesh):
    return jax.shard_map(
        per_device,
        mesh=mesh,
        in_specs=(
            P("row", ("tm", "col")),
            P("row", ("tm", "col")),
            P("col", ("tm", "row")),
            P("col", ("tm", "row")),
            P(None, ("tm", "col")),
            P(None, ("tm", "col")),
            P("tm"),
            P(),
        ),
        out_specs=P("tm", "col", "row"),
        check_vma=False,
    )
```

profile of v0, /device:TPU:0, one launch (start us, length us, event | category | flops | bytes accessed | tf_op | source)
XLA Modules:
  0.0 368.2 jit_solution(15174462070523814575)
XLA Ops:
  6.5 0.0 copy-start
  6.5 0.0 all-gather.7.cloned.1.call-start
  6.5 0.7 all-gather.7.cloned.1.call-update
  7.3 0.0 all-gather.5.cloned.1.call-start
  7.3 0.7 all-gather.5.cloned.1.call-update
  8.0 0.0 all-gather.11.cloned.1.call-start
  8.1 0.7 all-gather.11.cloned.1.call-update
  8.7 0.0 all-gather.9.cloned.1.call-start
  8.8 0.5 all-gather.9.cloned.1.call-update
  9.3 0.0 reduce-scatter.3.cloned.1.call-start
  9.4 1.2 dynamic-slice
  12.6 0.8 bitcast_dynamic-update-slice_fusion
  13.4 0.7 bitcast_dynamic-update-slice_fusion.1
  14.1 63.1 %all-reduce.2 = (f32[512]{0:T(512)S(1)}, f32[1536]{0:T(1024)S(1)}) all-reduce(f32[512]{0:T(512)S(1)} %bitcast_dynamic-update-slice_fusion.1, f32[1536]{0:T(1024)S(1)} %bitcast_dynamic-update-slice_fusion), channel_id=1, replica_groups=mesh['tm'=4,'row'=2,'col'=4] {'tm','col'}, use_global_device_ids=true, to_apply=%add | all-reduce | flops 2048 | bytes 16384
  77.3 0.0 all-gather.7.cloned.1.call-done
  77.3 14.0 %all-gather.5.cloned.1.call-done = f32[512,512]{0,1:T(8,128)} async-done(((f32[512,32]{0,1:T(8,128)}), f32[512,512]{0,1:T(8,128)}) %all-gather.5.cloned.1.call-update) | async-done | bytes 1048592 | tf_op jit(solution)/shard_map/all_gather | solution.py:32
  91.3 3.5 fusion.24
  94.8 58.1 %all-gather.11.cloned.1.call-done = f32[512,1536]{0,1:T(8,128)} async-done(((f32[512,192]{0,1:T(8,128)}), f32[512,1536]{0,1:T(8,128)}) %all-gather.11.cloned.1.call-update) | async-done | bytes 3145744 | tf_op jit(solution)/shard_map/all_gather | solution.py:41
  152.8 46.0 %all-gather.9.cloned.1.call-done = f32[512,1536]{0,1:T(8,128)} async-done(((f32[512,96]{0,1:T(8,128)}), f32[512,1536]{0,1:T(8,128)}) %all-gather.9.cloned.1.call-update) | async-done | bytes 3145744 | tf_op jit(solution)/shard_map/all_gather | solution.py:33
  198.8 8.4 %fusion.21 = f32[512,512]{1,0:T(8,128)S(1)} fusion(f32[512,512]{1,0:T(8,128)S(1)} %fusion.24, f32[512,1536]{0,1:T(8,128)} %all-gather.11.cloned.1.call-done, f32[512,1536]{0,1:T(8,128)} %all-gather.9.cloned.1.call-done, f32[1536]{0:T(1024)S(1)} %negate_exponential_fusion), kind=kOutput, calls=%fused_computation.22 | convolution fusion | flops 4832886784 | bytes 8394752 | tf_op jit(solution)/shard_map/dot_general | solution.py:23
  207.2 29.9 %fusion.5 = f32[2048,512]{1,0:T(8,128)} fusion(f32[512,512]{1,0:T(8,128)S(1)} %fusion.21, s32[512]{0:T(512)S(1)} %multiply_add_fusion), kind=kOutput, calls=%fused_computation.8 | convolution fusion | flops 6458179584 | bytes 5244928 | tf_op jit(solution)/shard_map/dot_general | solution.py:46
  237.1 0.0 reduce-scatter.3.cloned.1.call-update
  237.2 0.0 reduce-scatter.5.cloned.1.call-start
  237.2 0.0 copy-done
  237.2 0.2 dynamic-slice_reduce_fusion
  237.4 43.2 %reduce-scatter.3.cloned.1.call-done = f32[512,512]{1,0:T(8,128)} async-done(((f32[2048,512]{1,0:T(8,128)}), f32[512,512]{1,0:T(8,128)}) %reduce-scatter.3.cloned.1.call-update) | async-done | bytes 1048592 | tf_op jit(solution)/shard_map/reduce_scatter | solution.py:45
  280.6 3.8 %broadcast_multiply_fusion = f32[4,512,512]{2,1,0:T(8,128)} fusion(f32[512,512]{1,0:T(8,128)} %reduce-scatter.3.cloned.1.call-done, f32[4]{0:T(128)S(1)} %dynamic-slice_reduce_fusion), kind=kLoop, calls=%fused_computation.14 | loop fusion | flops 1048576 | bytes 5242896 | tf_op jit(solution)/shard_map/wt,gtr->wgr/dot_general | solution.py:61
  284.5 0.0 reduce-scatter.5.cloned.1.call-update
  284.5 76.9 %reduce-scatter.5.cloned.1.call-done = f32[1,512,512]{2,1,0:T(8,128)} async-done(((f32[4,512,512]{2,1,0:T(8,128)}), f32[1,512,512]{2,1,0:T(8,128)}) %reduce-scatter.5.cloned.1.call-update) | async-done | bytes 1048592 | tf_op jit(solution)/shard_map/reduce_scatter | solution.py:60
  (5 shorter events, 0.0 us)
Async XLA Ops:
  6.5 230.7 %copy-start = (f32[4,4]{1,0:T(4,128)S(1)}, f32[4,4]{1,0:T(4,128)}, u32[]{:S(2)}) copy-start(f32[4,4]{1,0:T(4,128)} %param.15) | copy-start | bytes 196
  6.5 70.7 %all-gather.7.cloned.1.call-start = ((), (), s32[]{:S(2)}) async-start(), calls=%async_computation.3 | async-start | bytes 1179648 | tf_op jit(solution)/shard_map/all_gather | solution.py:38
  7.3 84.0 %all-gather.5.cloned.1.call-start = ((), (), s32[]{:S(2)}) async-start(), calls=%async_computation.2 | async-start | bytes 1114112 | tf_op jit(solution)/shard_map/all_gather | solution.py:32
  8.0 144.8 %all-gather.11.cloned.1.call-start = ((), (), s32[]{:S(2)}) async-start(), calls=%async_computation.5 | async-start | bytes 3538944 | tf_op jit(solution)/shard_map/all_gather | solution.py:41
  8.7 190.1 %all-gather.9.cloned.1.call-start = ((), (), s32[]{:S(2)}) async-start(), calls=%async_computation.4 | async-start | bytes 3342336 | tf_op jit(solution)/shard_map/all_gather | solution.py:33
  9.3 271.3 %reduce-scatter.3.cloned.1.call-start = ((), (), s32[]{:S(2)}) async-start(), calls=%async_computation.6 | async-start | bytes 5242880 | tf_op jit(solution)/shard_map/reduce_scatter | solution.py:45
  237.2 124.2 %reduce-scatter.5.cloned.1.call-start = ((), (), s32[]{:S(2)}) async-start(), calls=%async_computation.7 | async-start | bytes 5242880 | tf_op jit(solution)/shard_map/reduce_scatter | solution.py:60
Sparse Core Ops, SparseCore 0:
  9.5 42.8 all-gather.6
  54.5 36.6 all-gather.4
  93.5 59.3 all-gather.10
  155.0 43.8 all-gather.8
  237.3 43.2 reduce-scatter.2
  284.6 76.7 reduce-scatter.4
where the time goes:
time: 368 us
  waiting for transfers between devices  241 us (65%)
  blocking collectives  63.1 us (17%)
  matrix products  41.8 us (11%)
  between operations  15.5 us (4%)
  other arithmetic  3.85 us (1%)
    reduce_scatter x1, waiting for transfers between devices, per_device(): lax.psum_scatter(jnp.einsum('wt,gtr->wgr', own_weights, series, precision...  76.9 us
    unnamed x1, blocking collectives  63.1 us
    all_gather x1, waiting for transfers between devices, per_device(): lax.all_gather(emp_cols, ('tm', 'row'), axis=1, tiled=True)  58.1 us
    all_gather x1, waiting for transfers between devices, per_device(): lax.all_gather(emp_rows, ('tm', 'col'), axis=1, tiled=True)  46 us
    reduce_scatter x1, waiting for transfers between devices, per_device(): lax.psum_scatter(lax.dot_general(cosine_table(col_first, number_cols, mod...  43.2 us
    dot_general x1, matrix products, per_device(): lax.dot_general(cosine_table(col_first, number_cols, mode_share * lax.axi...  29.9 us
    all_gather x1, waiting for transfers between devices, per_device(): lax.all_gather(occ_rows, ('tm', 'col'), axis=1, tiled=True)  14 us
    dot_general x2, matrix products, make_folder(): lax.dot_general(scaled, piece, (((1,), (1,)), ((), ())), precision=precise)  11.9 us
  transfers between devices with their start and end apart: 6, of which 5 were waited for; matrix products, arithmetic and copies ran while one was open for 2% of the time, Pallas kernels for 0%

commit v1 on v0

v1 whole, which is shorter than its diff:
```python
import functools

import jax
import jax.numpy as jnp
from jax import lax
from jax.experimental import pallas as pl
from jax.experimental.pallas import tpu as pltpu
from jax.sharding import PartitionSpec as P

GP = 2048
f32, bf16 = jnp.float32, jnp.bfloat16
VMEM_LIMIT = 32 * 1024 * 1024
EXTRA = 8
CHUNKS = 2
FINE = 32


def bits_of(size):
    return [1 << b for b in range(size.bit_length() - 1)][::-1]


def swap(value, axis, bit):
    size = lax.axis_size(axis)
    return lax.ppermute(value, axis, [(i, i ^ bit) for i in range(size)])


def unrelate(blocks, axis, dim):
    size, me = lax.axis_size(axis), lax.axis_index(axis)
    for bit in bits_of(size):
        shape = blocks.shape
        cut = blocks.reshape(*shape[:dim], -1, 2, bit, *shape[dim + 1 :])
        cut = jnp.where((me // bit) % 2 == 1, jnp.flip(cut, dim + 1), cut)
        blocks = cut.reshape(shape)
    return blocks


def pick(pieces, at):
    return lax.dynamic_index_in_dim(pieces, at, 0, False)


def exchange(pieces, axis, bits):
    me, low = lax.axis_index(axis), bits[-1] if bits else 1
    size, rest = pieces.shape[0], pieces.shape[1:]
    got = pieces[None]
    for bit in bits:
        got = got.reshape(got.shape[0], 2, -1, *rest)
        mine = (me // bit) % 2
        keep = lax.dynamic_index_in_dim(got, mine, 1, False)
        send = lax.dynamic_index_in_dim(got, 1 - mine, 1, False)
        got = jnp.stack([keep, swap(send, axis, bit)], 1)
        got = got.reshape(-1, *got.shape[2:])
    return got.reshape(size, *rest)


def split(value):
    high = value.astype(bf16)
    return high, (value - high.astype(f32)).astype(bf16)


def dot(a, b):
    return lax.dot_general(a, b, (((1,), (0,)), ((), ())), preferred_element_type=f32)


def green_kernel(chunk, slots, half, T, X, C, counts, *refs):
    occ_r, emp_r, occ_c, emp_c = counts
    place, weights, decay_occ, decay_emp = refs[:4]
    rows = refs[4 : 4 + 2 * T]
    cols = refs[4 + 2 * T : 6 + 2 * T]
    outs = refs[6 + 2 * T : 6 + 3 * T]
    flat, columns, s_high, s_low = refs[6 + 3 * T :]
    x, q = place[0], place[1]
    k_occ, k_emp = decay_occ.shape[1], decay_emp.shape[1]
    breadth = flat.shape[1]
    piece = cols[0].shape[-1]
    for s in range(T):
        for core in range(2):
            for d in range(C // 2):
                at = s * C + (q ^ (2 * d + core))
                block = rows[2 * s + core]
                flat[pl.ds(pl.multiple_of(at * occ_r, 8), occ_r), :] = block[d, chunk, 0:occ_r, :]
                flat[pl.ds(pl.multiple_of(k_occ + at * emp_r, 8), emp_r), :] = block[d, chunk, occ_r : occ_r + emp_r, :]
    for part in range(2):
        for i, (dx, dq) in enumerate(slots[part]):
            lanes = slice((dq // 2) * piece, (dq // 2) * piece + piece)
            for h in range(half):
                at = (part * half + h) * X + (x ^ dx)
                columns[pl.ds(pl.multiple_of(at * occ_c, 8), occ_c), lanes] = cols[part][i, h, 0:occ_c, :]
                columns[pl.ds(pl.multiple_of(k_occ + at * emp_c, 8), emp_c), lanes] = cols[part][i, h, occ_c : occ_c + emp_c, :]
    step = 128
    for kb in range((k_occ + k_emp) // step):
        at = kb * step
        turned = flat[at : at + step, :].T
        decay = decay_occ if at < k_occ else decay_emp
        first = at if at < k_occ else at - k_occ
        for t in range(T):
            high, low = split(turned * decay[t : t + 1, first : first + step])
            s_high[t * breadth : (t + 1) * breadth, at : at + step] = high
            s_low[t * breadth : (t + 1) * breadth, at : at + step] = low

    def green(lo, hi):
        c_high, c_low = split(columns[lo:hi, :])
        a_high, a_low = s_high[:, lo:hi], s_low[:, lo:hi]
        return dot(a_high, c_high) + dot(a_high, c_low) + dot(a_low, c_high)

    product = green(0, k_occ) * green(k_occ, k_occ + k_emp)
    for w in range(T):
        total = weights[w * T] * product[0:breadth, :]
        for t in range(1, T):
            total += weights[w * T + t] * product[t * breadth : (t + 1) * breadth, :]
        outs[w][...] = total


def table_kernel(near, far, high, low):
    share = far.shape[1]
    for h in range(share):
        c, s = far[0, h : h + 1, :], far[1, h : h + 1, :]
        for odd in range(2):
            value = c * near[2 * odd] - s * near[2 * odd + 1]
            a, b = split(value)
            high[odd, h * FINE : (h + 1) * FINE, :] = a
            low[odd, h * FINE : (h + 1) * FINE, :] = b


def mode_kernel(T, high, low, *refs):
    series = refs[: 2 * T]
    outs = refs[2 * T : -2]
    both, single = refs[-2:]
    breadth, width = series[0].shape
    step = width // 2 if width >= 256 else width
    groups = width // step
    at = 0
    for s in range(T):
        for d in range(groups):
            mine = series[2 * s][:, d * step : (d + 1) * step]
            e = groups - 1 - d
            theirs = series[2 * (s ^ (T - 1)) + 1][:, e * step : (e + 1) * step]
            for odd, value in enumerate((mine + theirs, mine - theirs)):
                a, b = split(value.T)
                both[odd, at : at + step, 0:breadth] = a
                both[odd, at : at + step, breadth:] = b
            at += step
    share = outs[0].shape[0] // 2
    for block, out in enumerate(outs):
        lines = slice(block * share, (block + 1) * share)
        for odd in range(2):
            twice = dot(high[odd, lines, :], both[odd])
            once = dot(low[odd, lines, :], both[odd, :, 0:breadth])
            out[pl.ds(odd, share, stride=2), :] = twice[:, :breadth] + twice[:, breadth:] + once


def place_kernel(place, *refs):
    pieces, out = refs[:-1], refs[-1]
    for i, piece in enumerate(pieces):
        breadth = piece.shape[2]
        for d in range(piece.shape[0]):
            at = ((place[1] // 2) ^ d) * CHUNKS + i
            out[0, :, pl.ds(pl.multiple_of(at * breadth, breadth), breadth)] = piece[d]


def per_device(occ_rows, emp_rows, occ_cols, emp_cols, occ_energy, emp_energy, times, freq_weight):
    T, X, C = lax.axis_size("tm"), lax.axis_size("row"), lax.axis_size("col")
    k, x, q = lax.axis_index("tm"), lax.axis_index("row"), lax.axis_index("col")
    number_rows, number_cols = occ_rows.shape[0], occ_cols.shape[0]
    occ_r, emp_r, occ_c, emp_c = (a.shape[1] for a in (occ_rows, emp_rows, occ_cols, emp_cols))
    n, m = occ_r + emp_r, occ_c + emp_c
    H = C // 2
    rp, jp = number_rows // (H * CHUNKS), number_cols // T
    half = T // 2
    k_occ, k_emp = occ_r * T * C, emp_r * T * C
    high_bits = [("col", b) for b in bits_of(C) if b > 1]
    row_bits = [("row", b) for b in bits_of(X)]

    turn = q >= C // 2
    col_t = jnp.concatenate([occ_cols, emp_cols], 1)
    col_t = jnp.where(turn, jnp.flip(col_t, 0), col_t).T.reshape(m, T, jp).transpose(1, 0, 2)
    mirror = jnp.where(turn, T - 1, 0)
    col_slots = [pick(col_t, k ^ mirror)] + [None] * (T - 1)
    for s in range(1, T):
        col_slots[s] = swap(pick(col_t, k ^ s ^ mirror), "tm", s)

    row_t = jnp.concatenate([occ_rows.T, emp_rows.T], 0).reshape(n, H, CHUNKS, rp).transpose(1, 2, 0, 3)
    energy = jnp.concatenate([occ_energy, emp_energy], 1)
    extra = jnp.zeros((EXTRA, rp), f32).at[0:1, :n].set(energy).at[1, :].set(times[0])
    row_t = jnp.concatenate([row_t, jnp.broadcast_to(extra, (H, CHUNKS, EXTRA, rp))], 2)
    own_rows = exchange(row_t, "col", [b for _, b in high_bits])
    row_slots = []
    for s in range(T):
        got = own_rows if s == 0 else swap(own_rows, "tm", s)
        row_slots += [got, swap(got, "col", 1)]

    cols, slots = [], []
    for first, order in ((0, row_bits + high_bits), (half, high_bits + row_bits)):
        value = jnp.stack(col_slots[first : first + half])[None]
        where = [(0, 0)]
        for axis, bit in order:
            value = jnp.concatenate([value, swap(value, axis, bit)], 0)
            where = where + [(dx ^ bit, dq) if axis == "row" else (dx, dq ^ bit) for dx, dq in where]
        cols.append(value)
        slots.append(where)

    heads = jnp.stack([r[:, 0, n : n + 2, :] for r in row_slots]).reshape(T, 2, H, 2, rp)
    levels = heads[:, :, :, 0, :n].transpose(0, 2, 1, 3).reshape(T, C, n)
    levels = unrelate(levels, "col", 1)
    instants = heads[:, 0, 0, 1, 0]

    def decays(energies):
        return jnp.exp(-(instants[:, None] * energies.reshape(1, -1)))

    decay_occ, decay_emp = decays(levels[:, :, :occ_r]), decays(levels[:, :, occ_r:])
    step = jnp.arange(T)
    weights = freq_weight[k ^ step][:, k ^ step].reshape(-1)
    place = jnp.stack([x, q]).astype(jnp.int32)

    smem = pl.BlockSpec(memory_space=pltpu.SMEM)
    vmem = pl.BlockSpec(memory_space=pltpu.VMEM)
    params = pltpu.CompilerParams(vmem_limit_bytes=VMEM_LIMIT)
    wide = H * jp
    own = []
    for chunk in range(CHUNKS):
        series = pl.pallas_call(
            functools.partial(green_kernel, chunk, slots, half, T, X, C, (occ_r, emp_r, occ_c, emp_c)),
            out_shape=[jax.ShapeDtypeStruct((rp, wide), f32)] * T,
            in_specs=[smem, smem] + [pl.BlockSpec()] * (2 + 2 * T + 2),
            scratch_shapes=[
                pltpu.VMEM((k_occ + k_emp, rp), f32),
                pltpu.VMEM((k_occ + k_emp, wide), f32),
                pltpu.VMEM((T * rp, k_occ + k_emp), bf16),
                pltpu.VMEM((T * rp, k_occ + k_emp), bf16),
            ],
            compiler_params=params,
            name="greens",
        )(place, weights, decay_occ, decay_emp, *row_slots, *cols)
        here = [series[0]] + [None] * (T - 1)
        for s in range(1, T):
            here[s] = swap(series[s], "tm", s)
        own.append(here)

    slot = jnp.arange(T, dtype=jnp.int32)[:, None, None]
    dq = 2 * jnp.arange(H, dtype=jnp.int32)[None, :, None]
    inner = jnp.arange(jp, dtype=jnp.int32)[None, None, :]
    source = q ^ dq
    lane = jnp.where(source >= C // 2, (T - 1 - (k ^ slot)) * 0 + (jp - 1 - inner), inner)
    column = (source * number_cols + (k ^ slot) * jp + lane).reshape(-1)
    odd_column = 2 * column + 1
    share = GP // C

    def angle(wave):
        phase = (odd_column[None, :] * wave[:, None]) % (4 * GP)
        return jnp.pi * phase.astype(f32) / (2.0 * GP)

    scale = jnp.sqrt(2.0 / GP)
    fine = 2 * jnp.arange(FINE, dtype=jnp.int32)
    per_block = share // (2 * FINE)
    blocks = q ^ (2 * jnp.arange(H, dtype=jnp.int32)[::-1])
    coarse = (blocks[:, None] * share + 2 * FINE * jnp.arange(per_block, dtype=jnp.int32)[None, :]).reshape(-1)
    even, odd, far = angle(fine), angle(fine + 1), angle(coarse)
    near = jnp.stack([scale * jnp.cos(even), scale * jnp.sin(even), scale * jnp.cos(odd), scale * jnp.sin(odd)])
    far = jnp.stack([jnp.cos(far), jnp.sin(far)])
    all_cols = T * wide
    t_high, t_low = pl.pallas_call(
        table_kernel,
        out_shape=[jax.ShapeDtypeStruct((2, H * share // 2, all_cols), bf16)] * 2,
        in_specs=[pl.BlockSpec()] * 2,
        out_specs=[vmem] * 2,
        compiler_params=params,
        name="cosines",
    )(near, far)

    pieces = []
    for chunk in range(CHUNKS):
        both = []
        for s in range(T):
            both += [own[chunk][s], swap(own[chunk][s], "col", 1)]
        made = pl.pallas_call(
            functools.partial(mode_kernel, T),
            out_shape=[jax.ShapeDtypeStruct((share, rp), f32)] * H,
            in_specs=[vmem] * 2 + [pl.BlockSpec()] * (2 * T),
            scratch_shapes=[pltpu.VMEM((2, all_cols, 2 * rp), bf16), pltpu.VMEM((8, 128), f32)],
            compiler_params=params,
            name="modes",
        )(t_high, t_low, *both)
        got = [made[H - 1]]
        for d in range(1, H):
            got.append(swap(made[H - 1 - d], "col", 2 * d))
        pieces.append(jnp.stack(got))
    return pl.pallas_call(
        place_kernel,
        out_shape=jax.ShapeDtypeStruct((1, share, number_rows), f32),
        in_specs=[smem] + [pl.BlockSpec()] * CHUNKS,
        compiler_params=params,
        name="assemble",
    )(place, *pieces)


def solution(mesh):
    return jax.shard_map(
        per_device,
        mesh=mesh,
        in_specs=(
            P("row", ("tm", "col")),
            P("row", ("tm", "col")),
            P("col", ("tm", "row")),
            P("col", ("tm", "row")),
            P(None, ("tm", "col")),
            P(None, ("tm", "col")),
            P("tm"),
            P(),
        ),
        out_specs=P("tm", "col", "row"),
        check_vma=False,
    )
```

time: 368 us -> 107 us (0.29)
  waiting for transfers between devices: 241 us -> 40.8 us
  blocking collectives: 63.1 us -> 0 us
  matrix products: 41.8 us -> 0 us
  starting transfers between devices: 0.2 us -> 34.6 us
  between operations: 15.5 us -> 1.16 us
  Pallas kernels: 0 us -> 11.8 us
  local copies, waits for them, and re-layouts: 2.95 us -> 9 us
  other arithmetic: 3.85 us -> 8.88 us
    reduce_scatter x2 -> x0, waiting for transfers between devices: 120 us -> none  [the longest x1 76.9 us: per_device(): lax.psum_scatter(jnp.einsum('wt,gtr->wgr', own_weights, series, precision...]
    all_gather x4 -> x0, waiting for transfers between devices: 118 us -> none  [the longest x1 58.1 us: per_device(): lax.all_gather(emp_cols, ('tm', 'row'), axis=1, tiled=True)]
    unnamed x1 -> x0, blocking collectives: 63.1 us -> none
    dot_general x3 -> x0, matrix products: 41.8 us -> none  [the longest x1 29.9 us: per_device(): lax.dot_general(cosine_table(col_first, number_cols, mode_share * lax.axi...]
    ppermute x0 -> x31, waiting for transfers between devices: none -> 40.8 us  [swap(): return lax.ppermute(value, axis, [(i, i ^ bit) for i in range(size)])]
    ppermute x0 -> x31, starting transfers between devices: none -> 34.6 us  [swap(): return lax.ppermute(value, axis, [(i, i ^ bit) for i in range(size)])]
    pallas_call x0 -> x6, Pallas kernels: none -> 11.8 us  [the longest x2 6.44 us: per_device(): pl.pallas_call(functools.partial(green_kernel, chunk, slots, half, T, X,...]
    concatenate x0 -> x6, other arithmetic: none -> 4.8 us  [the longest x4 3.1 us: per_device(): value = jnp.concatenate([value, swap(value, axis, bit)], 0)]
  transfers between devices with their start and end apart: 6 -> 31, of which waited for: 5 -> 8; matrix products, arithmetic and copies ran while one was open for 2% -> 14% of each run, Pallas kernels for 0% -> 6%
where the time goes in v1:
time: 107 us; the launch traced here: 106 us
  waiting for transfers between devices  40.8 us (38%)
  starting transfers between devices  34.6 us (32%)
  Pallas kernels  11.8 us (11%)
  local copies, waits for them, and re-layouts  9 us (8%)
  other arithmetic  8.88 us (8%)
  between operations  1.16 us (1%)
    ppermute x31, waiting for transfers between devices, swap(): return lax.ppermute(value, axis, [(i, i ^ bit) for i in range(size)])  40.8 us
    ppermute x31, starting transfers between devices, swap(): return lax.ppermute(value, axis, [(i, i ^ bit) for i in range(size)])  34.6 us
    pallas_call x2, Pallas kernels, per_device(): pl.pallas_call(functools.partial(green_kernel, chunk, slots, half, T, X,...  6.44 us
    concatenate x4, other arithmetic, per_device(): value = jnp.concatenate([value, swap(value, axis, bit)], 0)  3.1 us
    pallas_call x2, Pallas kernels, per_device(): pl.pallas_call(functools.partial(mode_kernel, T), out_shape=[jax.ShapeDty...  2.72 us
  transfers between devices with their start and end apart: 31, of which 8 were waited for; matrix products, arithmetic and copies ran while one was open for 14% of the time, Pallas kernels for 6%

profile of v1, /device:TPU:0, one launch (start us, length us, event | category | flops | bytes accessed | tf_op | source)
XLA Modules:
  0.0 106.2 jit_solution(17209250998253061835)
XLA Ops:
  0.7 1.0 pad_maximum_fusion.7
  1.7 0.2 reshape.614
  1.9 0.7 select_maximum_fusion
  2.7 3.1 %collective-permute-start = (f32[1,1,2,136,128]{4,3,2,1,0:T(8,128)S(1)}, f32[1,1,2,136,128]{4,3,2,1,0:T(8,128)S(1)}, u32[]{:S(2)}, u32[]{:S(2)}) collective-permute-start(f32[1,1,2,136,128]{4,3,2,1,0:T(8,128)S(1)} %get-tuple-element.62), channel_id=1, source_target_pairs={{0,2},{1,3},{2,0},{3,1},{4,6},{5,7},{6,4},{7,5},{8,10},{9,11},{10,... | collective-permute-start | bytes 417800 | tf_op jit(solution)/shard_map/ppermute | solution.py:24
  5.8 0.8 rev.12
  6.6 0.1 select_bitcast_fusion
  6.7 0.2 reshape.617
  6.9 0.5 constant_dynamic-slice_fusion.1
  7.4 1.6 %collective-permute-start.8 = (f32[256,128]{1,0:T(8,128)S(1)}, f32[256,128]{1,0:T(8,128)S(1)}, u32[]{:S(2)}, u32[]{:S(2)}) collective-permute-start(f32[256,128]{1,0:T(8,128)S(1)} %bitcast.97), channel_id=1, source_target_pairs={{0,8},{8,0},{16,24},{24,16},{1,9},{9,1},{17,25},{25,17},{2,10},{10... | collective-permute-start | bytes 393224 | tf_op jit(solution)/shard_map/ppermute | solution.py:24
  9.0 2.6 %collective-permute-start.11 = (f32[256,128]{1,0:T(8,128)S(1)}, f32[256,128]{1,0:T(8,128)S(1)}, u32[]{:S(2)}, u32[]{:S(2)}) collective-permute-start(f32[256,128]{1,0:T(8,128)S(1)} %bitcast.99), channel_id=1, source_target_pairs={{0,16},{8,24},{16,0},{24,8},{1,17},{9,25},{17,1},{25,9},{2,18},{10... | collective-permute-start | bytes 393224 | tf_op jit(solution)/shard_map/ppermute | solution.py:24
  11.6 0.2 collective-permute-start.12
  11.9 0.1 rev.11
  12.2 0.5 iota_multiply_fusion.1
  12.8 0.6 add.190
  13.5 0.6 gather_fusion
  14.0 0.1 copy.32
  14.1 0.6 gather_fusion.1
  14.7 0.1 copy.33
  14.8 6.8 %collective-permute-done.11 = f32[256,128]{1,0:T(8,128)S(1)} collective-permute-done((f32[256,128]{1,0:T(8,128)S(1)}, f32[256,128]{1,0:T(8,128)S(1)}, u32[]{:S(2)}, u32[]{:S(2)}) %collective-permute-start.11) | collective-permute-done | bytes 131104 | tf_op jit(solution)/shard_map/ppermute | solution.py:24
  21.7 0.6 collective-permute-start.13
  22.3 1.6 %collective-permute-start.9 = (f32[1,2,256,128]{3,2,1,0:T(8,128)S(1)}, f32[1,2,256,128]{3,2,1,0:T(8,128)S(1)}, u32[]{:S(2)}, u32[]{:S(2)}) collective-permute-start(f32[1,2,256,128]{3,2,1,0:T(8,128)S(1)} %maximum_bitcast_fusion.1), channel_id=1, source_target_pairs={{0,4},{4,0},{1,5},{5,1},{2,6},{6,2},{3,7},{7,3},{8,12},{12,8},{9,1... | collective-permute-start | bytes 786440 | tf_op jit(solution)/shard_map/ppermute | solution.py:24
  23.9 2.5 %collective-permute-start.6 = (f32[2,2,136,128]{3,2,0,1:T(8,128)S(1)}, f32[2,2,136,128]{3,2,0,1:T(8,128)S(1)}, u32[]{:S(2)}, u32[]{:S(2)}) collective-permute-start(f32[2,2,136,128]{3,2,0,1:T(8,128)S(1)} %maximum_bitcast_fusion), channel_id=1, source_target_pairs={{0,24},{8,16},{16,8},{24,0},{1,25},{9,17},{17,9},{25,1},{2,26},{10... | collective-permute-start | bytes 835592 | tf_op jit(solution)/shard_map/ppermute | solution.py:24
  26.4 3.4 %collective-permute-start.2 = (f32[2,2,136,128]{3,2,0,1:T(8,128)S(1)}, f32[2,2,136,128]{3,2,0,1:T(8,128)S(1)}, u32[]{:S(2)}, u32[]{:S(2)}) collective-permute-start(f32[2,2,136,128]{3,2,0,1:T(8,128)S(1)} %maximum_bitcast_fusion), channel_id=1, source_target_pairs={{0,8},{8,0},{16,24},{24,16},{1,9},{9,1},{17,25},{25,17},{2,10},{10... | collective-permute-start | bytes 835592 | tf_op jit(solution)/shard_map/ppermute | solution.py:24
  29.8 1.9 %collective-permute-start.4 = (f32[2,2,136,128]{3,2,0,1:T(8,128)S(1)}, f32[2,2,136,128]{3,2,0,1:T(8,128)S(1)}, u32[]{:S(2)}, u32[]{:S(2)}) collective-permute-start(f32[2,2,136,128]{3,2,0,1:T(8,128)S(1)} %maximum_bitcast_fusion), channel_id=1, source_target_pairs={{0,16},{8,24},{16,0},{24,8},{1,17},{9,25},{17,1},{25,9},{2,18},{10... | collective-permute-start | bytes 835592 | tf_op jit(solution)/shard_map/ppermute | solution.py:24
  31.7 3.8 %collective-permute-start.14 = (f32[2,2,256,128]{3,2,1,0:T(8,128)S(1)}, f32[2,2,256,128]{3,2,1,0:T(8,128)}, u32[]{:S(2)}, u32[]{:S(2)}) collective-permute-start(f32[2,2,256,128]{3,2,1,0:T(8,128)S(1)} %pad_maximum_fusion.4), channel_id=1, source_target_pairs={{0,4},{4,0},{1,5},{5,1},{2,6},{6,2},{3,7},{7,3},{8,12},{12,8},{9,1... | collective-permute-start | bytes 1572872 | tf_op jit(solution)/shard_map/ppermute | solution.py:24
  35.5 0.8 pad_maximum_fusion.3
  36.3 1.1 %collective-permute-done.2 = f32[2,2,136,128]{3,2,0,1:T(8,128)S(1)} collective-permute-done((f32[2,2,136,128]{3,2,0,1:T(8,128)S(1)}, f32[2,2,136,128]{3,2,0,1:T(8,128)S(1)}, u32[]{:S(2)}, u32[]{:S(2)}) %collective-permute-start.2) | collective-permute-done | bytes 278560 | tf_op jit(solution)/shard_map/ppermute | solution.py:24
  37.5 0.5 collective-permute-start.3
  38.0 10.4 %collective-permute-done.4 = f32[2,2,136,128]{3,2,0,1:T(8,128)S(1)} collective-permute-done((f32[2,2,136,128]{3,2,0,1:T(8,128)S(1)}, f32[2,2,136,128]{3,2,0,1:T(8,128)S(1)}, u32[]{:S(2)}, u32[]{:S(2)}) %collective-permute-start.4) | collective-permute-done | bytes 278560 | tf_op jit(solution)/shard_map/ppermute | solution.py:24
  48.6 1.6 %collective-permute-done.5 = f32[2,2,136,128]{3,2,0,1:T(8,128)} collective-permute-done((f32[2,2,136,128]{3,2,0,1:T(8,128)S(1)}, f32[2,2,136,128]{3,2,0,1:T(8,128)}, u32[]{:S(2)}, u32[]{:S(2)}) %collective-permute-start.5) | collective-permute-done | bytes 278560 | tf_op jit(solution)/shard_map/ppermute | solution.py:24
  50.1 0.7 constant_dynamic-update-slice_fusion.2
  50.9 0.6 copy.56
  51.5 0.6 reverse.7
  52.1 0.7 mul.238
  52.8 0.7 negate_exponential_fusion.1.refs_2_
  53.5 0.7 slice.94
  54.2 0.8 mul.242
  55.0 1.0 copy.47.refs_9_
  56.0 0.7 negate_exponential_fusion.refs_3_
  56.7 1.1 %pad_maximum_fusion.1.refs_13_ = f32[4,2,256,128]{3,2,1,0:T(8,128)S(1)} fusion(f32[2,2,256,128]{3,2,1,0:T(8,128)} %collective-permute-done.14, f32[1,2,256,128]{3,2,1,0:T(8,128)S(1)} %collective-permute-done.13, f32[1,2,256,128]{3,2,1,0:T(8,128)S(1)} %maximum_bitcast_fusion.2), kind=kLoop, calls=%fused_computation.3 | loop fusion | flops 524288 | bytes 2097152 | tf_op jit(solution)/shard_map/concatenate | solution.py:196
  57.8 1.1 %pad_maximum_fusion.refs_12_ = f32[4,2,256,128]{3,2,1,0:T(8,128)S(1)} fusion(f32[2,2,256,128]{3,2,1,0:T(8,128)} %collective-permute-done.10, f32[1,2,256,128]{3,2,1,0:T(8,128)S(1)} %collective-permute-done.9, f32[1,2,256,128]{3,2,1,0:T(8,128)S(1)} %maximum_bitcast_fusion.1), kind=kLoop, calls=%fused_computation.2 | loop fusion | flops 524288 | bytes 2097152 | tf_op jit(solution)/shard_map/concatenate | solution.py:196
  59.0 3.2 %greens.3 = (f32[128,256]{1,0:T(8,128)S(1)}, f32[128,256]{1,0:T(8,128)S(1)}, f32[128,256]{1,0:T(8,128)S(1)}, f32[128,256]{1,0:T(8,128)S(1)}) custom-call(s32[2]{0:T(128)S(1)} %pad_add_fusion.refs_0_.place, f32[16]{0:T(128)S(1)} %reshape.613.refs_1_, f32[4,512]{1,0:T(4,128)S(1)} %negate_exponential_fusion.1.refs_2_, ...), custom_call_target="tpu_custom_call" | custom-call | tf_op jit(solution)/shard_map/greens/pallas_call | solution.py:220
  62.3 2.8 %collective-permute-start.26 = (f32[128,256]{1,0:T(8,128)S(1)}, f32[128,256]{1,0:T(8,128)S(1)}, u32[]{:S(2)}, u32[]{:S(2)}) collective-permute-start(f32[128,256]{1,0:T(8,128)S(1)} %get-tuple-element.53), channel_id=1, source_target_pairs={{0,16},{8,24},{16,0},{24,8},{1,17},{9,25},{17,1},{25,9},{2,18},{10... | collective-permute-start | bytes 393224 | tf_op jit(solution)/shard_map/ppermute | solution.py:24
  65.1 1.6 %collective-permute-start.28 = (f32[128,256]{1,0:T(8,128)S(1)}, f32[128,256]{1,0:T(8,128)S(1)}, u32[]{:S(2)}, u32[]{:S(2)}) collective-permute-start(f32[128,256]{1,0:T(8,128)S(1)} %get-tuple-element.54), channel_id=1, source_target_pairs={{0,24},{8,16},{16,8},{24,0},{1,25},{9,17},{17,9},{25,1},{2,26},{10... | collective-permute-start | bytes 393224 | tf_op jit(solution)/shard_map/ppermute | solution.py:24
  66.7 3.2 %greens.2 = (f32[128,256]{1,0:T(8,128)S(1)}, f32[128,256]{1,0:T(8,128)S(1)}, f32[128,256]{1,0:T(8,128)S(1)}, f32[128,256]{1,0:T(8,128)S(1)}) custom-call(s32[2]{0:T(128)S(1)} %pad_add_fusion.refs_0_.place, f32[16]{0:T(128)S(1)} %reshape.613.refs_1_, f32[4,512]{1,0:T(4,128)S(1)} %negate_exponential_fusion.1.refs_2_, ...), custom_call_target="tpu_custom_call" | custom-call | tf_op jit(solution)/shard_map/greens/pallas_call | solution.py:220
  70.0 1.1 %cosine_multiply_fusion.1 = (f32[1,32,1024]{2,1,0:T(8,128)S(1)}, f32[1,32,1024]{2,1,0:T(8,128)S(1)}, f32[1,32,1024]{2,1,0:T(8,128)S(1)}, f32[1,32,1024]{2,1,0:T(8,128)S(1)}) fusion(s32[32]{0:T(128)S(1)} %copy-done.4, s32[1024]{0:T(1024)S(1)} %bitcast.105, s32[32]{0:T(128)S(1)} %copy-done.5), kind=kLoop, calls=%fused_computation.43 | loop fusion | flops 1048576 | bytes 528640 | tf_op jit(solution)/shard_map/mul | solution.py:257
  71.1 2.9 %collective-permute-start.18 = (f32[128,256]{1,0:T(8,128)S(1)}, f32[128,256]{1,0:T(8,128)S(1)}, u32[]{:S(2)}, u32[]{:S(2)}) collective-permute-start(f32[128,256]{1,0:T(8,128)S(1)} %get-tuple-element.47), channel_id=1, source_target_pairs={{0,16},{8,24},{16,0},{24,8},{1,17},{9,25},{17,1},{25,9},{2,18},{10... | collective-permute-start | bytes 393224 | tf_op jit(solution)/shard_map/ppermute | solution.py:24
  74.0 1.6 %collective-permute-start.20 = (f32[128,256]{1,0:T(8,128)S(1)}, f32[128,256]{1,0:T(8,128)S(1)}, u32[]{:S(2)}, u32[]{:S(2)}) collective-permute-start(f32[128,256]{1,0:T(8,128)S(1)} %get-tuple-element.48), channel_id=1, source_target_pairs={{0,24},{8,16},{16,8},{24,0},{1,25},{9,17},{17,9},{25,1},{2,26},{10... | collective-permute-start | bytes 393224 | tf_op jit(solution)/shard_map/ppermute | solution.py:24
  75.5 0.5 collective-permute-start.25
  76.0 1.9 %collective-permute-done.16.refs_2_ = f32[128,256]{1,0:T(8,128)S(1)} collective-permute-done((f32[128,256]{1,0:T(8,128)S(1)}, f32[128,256]{1,0:T(8,128)S(1)}, u32[]{:S(2)}, u32[]{:S(2)}) %collective-permute-start.16) | collective-permute-done | bytes 131104 | tf_op jit(solution)/shard_map/ppermute | solution.py:24
  78.0 0.3 fusion.14
  78.3 8.2 %collective-permute-done.18.refs_4_ = f32[128,256]{1,0:T(8,128)S(1)} collective-permute-done((f32[128,256]{1,0:T(8,128)S(1)}, f32[128,256]{1,0:T(8,128)S(1)}, u32[]{:S(2)}, u32[]{:S(2)}) %collective-permute-start.18) | collective-permute-done | bytes 131104 | tf_op jit(solution)/shard_map/ppermute | solution.py:24
  86.6 0.6 collective-permute-start.15
  87.2 0.1 collective-permute-start.17
  87.3 0.4 collective-permute-start.19
  87.7 0.1 collective-permute-start.21
  87.8 0.9 cosines.1
  88.8 1.4 %modes.3 = (f32[512,128]{1,0:T(8,128)S(1)}, f32[512,128]{1,0:T(8,128)S(1)}) custom-call(bf16[2,512,1024]{2,1,0:T(8,128)(2,1)S(1)} %get-tuple-element.43.high, bf16[2,512,1024]{2,1,0:T(8,128)(2,1)S(1)} %get-tuple-element.44.low, f32[128,256]{1,0:T(8,128)S(1)} %get-tuple-element.51.refs_0_, f32[128,256]{1,0:T(8,128)S(1)} %collective-permute-done.23.refs_1_, ...), custom_call_target="tpu_custom_call" | custom-call | tf_op jit(solution)/shard_map/modes/pallas_call | solution.py:274
  90.1 1.6 %collective-permute-start.30 = (f32[512,128]{1,0:T(8,128)S(1)}, f32[512,128]{1,0:T(8,128)S(1)}, u32[]{:S(2)}, u32[]{:S(2)}) collective-permute-start(f32[512,128]{1,0:T(8,128)S(1)} %get-tuple-element.56), channel_id=1, source_target_pairs={{0,2},{1,3},{2,0},{3,1},{4,6},{5,7},{6,4},{7,5},{8,10},{9,11},{10,... | collective-permute-start | bytes 786440 | tf_op jit(solution)/shard_map/ppermute | solution.py:24
  91.7 1.4 %modes.2 = (f32[512,128]{1,0:T(8,128)S(1)}, f32[512,128]{1,0:T(8,128)S(1)}) custom-call(bf16[2,512,1024]{2,1,0:T(8,128)(2,1)S(1)} %get-tuple-element.43.high, bf16[2,512,1024]{2,1,0:T(8,128)(2,1)S(1)} %get-tuple-element.44.low, f32[128,256]{1,0:T(8,128)S(1)} %get-tuple-element.45.refs_0_, f32[128,256]{1,0:T(8,128)S(1)} %collective-permute-done.15.refs_1_, ...), custom_call_target="tpu_custom_call" | custom-call | tf_op jit(solution)/shard_map/modes/pallas_call | solution.py:274
  93.1 0.6 collective-permute-start.22
  93.7 5.6 %collective-permute-done.30 = f32[512,128]{1,0:T(8,128)S(1)} collective-permute-done((f32[512,128]{1,0:T(8,128)S(1)}, f32[512,128]{1,0:T(8,128)S(1)}, u32[]{:S(2)}, u32[]{:S(2)}) %collective-permute-start.30) | collective-permute-done | bytes 262176 | tf_op jit(solution)/shard_map/ppermute | solution.py:24
  99.3 5.1 %collective-permute-done.22 = f32[512,128]{1,0:T(8,128)S(1)} collective-permute-done((f32[512,128]{1,0:T(8,128)S(1)}, f32[512,128]{1,0:T(8,128)S(1)}, u32[]{:S(2)}, u32[]{:S(2)}) %collective-permute-start.22) | collective-permute-done | bytes 262176 | tf_op jit(solution)/shard_map/ppermute | solution.py:24
  104.5 1.7 %assemble.1 = f32[1,512,512]{2,1,0:T(8,128)} custom-call(s32[2]{0:T(128)S(1)} %pad_add_fusion.refs_0_.place, f32[2,512,128]{2,1,0:T(8,128)S(1)} %pad_maximum_fusion.5.refs_0_, f32[2,512,128]{2,1,0:T(8,128)S(1)} %pad_maximum_fusion.6.refs_1_), custom_call_target="tpu_custom_call" | custom-call | tf_op jit(solution)/shard_map/assemble/pallas_call | solution.py:286
  (90 shorter events, 1.3 us)
Async XLA Ops:
  0.0 13.5 %copy-start = (f32[4,4]{1,0:T(4,128)S(1)}, f32[4,4]{1,0:T(4,128)}, u32[]{:S(2)}) copy-start(f32[4,4]{1,0:T(4,128)} %param.19) | copy-start | bytes 196
  0.0 5.8 %copy-start.2 = (f32[512,64]{0,1:T(8,128)S(1)}, f32[512,64]{0,1:T(8,128)}, u32[]{:S(2)}) copy-start(f32[512,64]{0,1:T(8,128)} %param.14) | copy-start | bytes 393220
  0.0 5.8 %copy-start.1 = (f32[512,192]{0,1:T(8,128)S(1)}, f32[512,192]{0,1:T(8,128)}, u32[]{:S(2)}) copy-start(f32[512,192]{0,1:T(8,128)} %param.15) | copy-start | bytes 1179652
  2.7 21.1 %collective-permute-start = (f32[1,1,2,136,128]{4,3,2,1,0:T(8,128)S(1)}, f32[1,1,2,136,128]{4,3,2,1,0:T(8,128)S(1)}, u32[]{:S(2)}, u32[]{:S(2)}) collective-permute-start(f32[1,1,2,136,128]{4,3,2,1,0:T(8,128)S(1)} %get-tuple-element.62), channel_id=1, source_target_pairs={{0,2},{1,3},{2,0},{3,1},{4,6},{5,7},{6,4},{7,5},{8,10},{9,11},{10,... | collective-permute-start | bytes 417800 | tf_op jit(solution)/shard_map/ppermute | solution.py:24
  7.4 14.9 %collective-permute-start.8 = (f32[256,128]{1,0:T(8,128)S(1)}, f32[256,128]{1,0:T(8,128)S(1)}, u32[]{:S(2)}, u32[]{:S(2)}) collective-permute-start(f32[256,128]{1,0:T(8,128)S(1)} %bitcast.97), channel_id=1, source_target_pairs={{0,8},{8,0},{16,24},{24,16},{1,9},{9,1},{17,25},{25,17},{2,10},{10... | collective-permute-start | bytes 393224 | tf_op jit(solution)/shard_map/ppermute | solution.py:24
  9.0 12.6 %collective-permute-start.11 = (f32[256,128]{1,0:T(8,128)S(1)}, f32[256,128]{1,0:T(8,128)S(1)}, u32[]{:S(2)}, u32[]{:S(2)}) collective-permute-start(f32[256,128]{1,0:T(8,128)S(1)} %bitcast.99), channel_id=1, source_target_pairs={{0,16},{8,24},{16,0},{24,8},{1,17},{9,25},{17,1},{25,9},{2,18},{10... | collective-permute-start | bytes 393224 | tf_op jit(solution)/shard_map/ppermute | solution.py:24
  11.6 10.1 %collective-permute-start.12 = (f32[256,128]{1,0:T(8,128)S(1)}, f32[256,128]{1,0:T(8,128)S(1)}, u32[]{:S(2)}, u32[]{:S(2)}) collective-permute-start(f32[256,128]{1,0:T(8,128)S(1)} %bitcast.98), channel_id=1, source_target_pairs={{0,24},{8,16},{16,8},{24,0},{1,25},{9,17},{17,9},{25,1},{2,26},{10... | collective-permute-start | bytes 393224 | tf_op jit(solution)/shard_map/ppermute | solution.py:24
  21.7 8.1 %collective-permute-start.13 = (f32[1,2,256,128]{3,2,1,0:T(8,128)S(1)}, f32[1,2,256,128]{3,2,1,0:T(8,128)S(1)}, u32[]{:S(2)}, u32[]{:S(2)}) collective-permute-start(f32[1,2,256,128]{3,2,1,0:T(8,128)S(1)} %maximum_bitcast_fusion.2), channel_id=1, source_target_pairs={{0,2},{1,3},{2,0},{3,1},{4,6},{5,7},{6,4},{7,5},{8,10},{9,11},{10,... | collective-permute-start | bytes 786440 | tf_op jit(solution)/shard_map/ppermute | solution.py:24
  22.3 9.4 %collective-permute-start.9 = (f32[1,2,256,128]{3,2,1,0:T(8,128)S(1)}, f32[1,2,256,128]{3,2,1,0:T(8,128)S(1)}, u32[]{:S(2)}, u32[]{:S(2)}) collective-permute-start(f32[1,2,256,128]{3,2,1,0:T(8,128)S(1)} %maximum_bitcast_fusion.1), channel_id=1, source_target_pairs={{0,4},{4,0},{1,5},{5,1},{2,6},{6,2},{3,7},{7,3},{8,12},{12,8},{9,1... | collective-permute-start | bytes 786440 | tf_op jit(solution)/shard_map/ppermute | solution.py:24
  23.9 12.4 %collective-permute-start.6 = (f32[2,2,136,128]{3,2,0,1:T(8,128)S(1)}, f32[2,2,136,128]{3,2,0,1:T(8,128)S(1)}, u32[]{:S(2)}, u32[]{:S(2)}) collective-permute-start(f32[2,2,136,128]{3,2,0,1:T(8,128)S(1)} %maximum_bitcast_fusion), channel_id=1, source_target_pairs={{0,24},{8,16},{16,8},{24,0},{1,25},{9,17},{17,9},{25,1},{2,26},{10... | collective-permute-start | bytes 835592 | tf_op jit(solution)/shard_map/ppermute | solution.py:24
  26.4 11.1 %collective-permute-start.2 = (f32[2,2,136,128]{3,2,0,1:T(8,128)S(1)}, f32[2,2,136,128]{3,2,0,1:T(8,128)S(1)}, u32[]{:S(2)}, u32[]{:S(2)}) collective-permute-start(f32[2,2,136,128]{3,2,0,1:T(8,128)S(1)} %maximum_bitcast_fusion), channel_id=1, source_target_pairs={{0,8},{8,0},{16,24},{24,16},{1,9},{9,1},{17,25},{25,17},{2,10},{10... | collective-permute-start | bytes 835592 | tf_op jit(solution)/shard_map/ppermute | solution.py:24
  29.8 7.7 %collective-permute-start.1 = (f32[2,2,136,128]{3,2,0,1:T(8,128)S(1)}, f32[2,2,136,128]{3,2,0,1:T(8,128)S(1)}, u32[]{:S(2)}, u32[]{:S(2)}) collective-permute-start(f32[2,2,136,128]{3,2,0,1:T(8,128)S(1)} %maximum_bitcast_fusion), channel_id=1, source_target_pairs={{0,1},{1,0},{2,3},{3,2},{4,5},{5,4},{6,7},{7,6},{8,9},{9,8},{10,11... | collective-permute-start | bytes 835592 | tf_op jit(solution)/shard_map/ppermute | solution.py:24
  29.8 18.6 %collective-permute-start.4 = (f32[2,2,136,128]{3,2,0,1:T(8,128)S(1)}, f32[2,2,136,128]{3,2,0,1:T(8,128)S(1)}, u32[]{:S(2)}, u32[]{:S(2)}) collective-permute-start(f32[2,2,136,128]{3,2,0,1:T(8,128)S(1)} %maximum_bitcast_fusion), channel_id=1, source_target_pairs={{0,16},{8,24},{16,0},{24,8},{1,17},{9,25},{17,1},{25,9},{2,18},{10... | collective-permute-start | bytes 835592 | tf_op jit(solution)/shard_map/ppermute | solution.py:24
  31.7 25.0 %collective-permute-start.14 = (f32[2,2,256,128]{3,2,1,0:T(8,128)S(1)}, f32[2,2,256,128]{3,2,1,0:T(8,128)}, u32[]{:S(2)}, u32[]{:S(2)}) collective-permute-start(f32[2,2,256,128]{3,2,1,0:T(8,128)S(1)} %pad_maximum_fusion.4), channel_id=1, source_target_pairs={{0,4},{4,0},{1,5},{5,1},{2,6},{6,2},{3,7},{7,3},{8,12},{12,8},{9,1... | collective-permute-start | bytes 1572872 | tf_op jit(solution)/shard_map/ppermute | solution.py:24
  36.3 21.5 %collective-permute-start.10 = (f32[2,2,256,128]{3,2,1,0:T(8,128)}, f32[2,2,256,128]{3,2,1,0:T(8,128)}, u32[]{:S(2)}, u32[]{:S(2)}) collective-permute-start(f32[2,2,256,128]{3,2,1,0:T(8,128)} %pad_maximum_fusion.3), channel_id=1, source_target_pairs={{0,2},{1,3},{2,0},{3,1},{4,6},{5,7},{6,4},{7,5},{8,10},{9,11},{10,... | collective-permute-start | bytes 1572872 | tf_op jit(solution)/shard_map/ppermute | solution.py:24
  37.5 13.4 %collective-permute-start.7 = (f32[2,2,136,128]{3,2,1,0:T(8,128)S(1)}, f32[2,2,136,128]{3,2,1,0:T(8,128)S(1)}, u32[]{:S(2)}, u32[]{:S(2)}) collective-permute-start(f32[2,2,136,128]{3,2,1,0:T(8,128)S(1)} %copy.35.refs_10_), channel_id=1, source_target_pairs={{0,1},{1,0},{2,3},{3,2},{4,5},{5,4},{6,7},{7,6},{8,9},{9,8},{10,11... | collective-permute-start | bytes 835592 | tf_op jit(solution)/shard_map/ppermute | solution.py:24
  37.5 11.1 %collective-permute-start.3 = (f32[2,2,136,128]{3,2,0,1:T(8,128)S(1)}, f32[2,2,136,128]{3,2,0,1:T(8,128)S(1)}, u32[]{:S(2)}, u32[]{:S(2)}) collective-permute-start(f32[2,2,136,128]{3,2,0,1:T(8,128)S(1)} %collective-permute-done.2), channel_id=1, source_target_pairs={{0,1},{1,0},{2,3},{3,2},{4,5},{5,4},{6,7},{7,6},{8,9},{9,8},{10,11... | collective-permute-start | bytes 835592 | tf_op jit(solution)/shard_map/ppermute | solution.py:24
  48.4 1.8 %collective-permute-start.5 = (f32[2,2,136,128]{3,2,0,1:T(8,128)S(1)}, f32[2,2,136,128]{3,2,0,1:T(8,128)}, u32[]{:S(2)}, u32[]{:S(2)}) collective-permute-start(f32[2,2,136,128]{3,2,0,1:T(8,128)S(1)} %collective-permute-done.4), channel_id=1, source_target_pairs={{0,1},{1,0},{2,3},{3,2},{4,5},{5,4},{6,7},{7,6},{8,9},{9,8},{10,11... | collective-permute-start | bytes 835592 | tf_op jit(solution)/shard_map/ppermute | solution.py:24
  62.2 11.8 %collective-permute-start.24 = (f32[128,256]{1,0:T(8,128)S(1)}, f32[128,256]{1,0:T(8,128)S(1)}, u32[]{:S(2)}, u32[]{:S(2)}) collective-permute-start(f32[128,256]{1,0:T(8,128)S(1)} %get-tuple-element.52), channel_id=1, source_target_pairs={{0,8},{8,0},{16,24},{24,16},{1,9},{9,1},{17,25},{25,17},{2,10},{10... | collective-permute-start | bytes 393224 | tf_op jit(solution)/shard_map/ppermute | solution.py:24
  62.3 13.3 %collective-permute-start.26 = (f32[128,256]{1,0:T(8,128)S(1)}, f32[128,256]{1,0:T(8,128)S(1)}, u32[]{:S(2)}, u32[]{:S(2)}) collective-permute-start(f32[128,256]{1,0:T(8,128)S(1)} %get-tuple-element.53), channel_id=1, source_target_pairs={{0,16},{8,24},{16,0},{24,8},{1,17},{9,25},{17,1},{25,9},{2,18},{10... | collective-permute-start | bytes 393224 | tf_op jit(solution)/shard_map/ppermute | solution.py:24
  65.1 4.9 %copy-start.4 = (s32[32]{0:T(128)S(1)}, s32[32]{0:T(128)}, u32[]{:S(2)}) copy-start(s32[32]{0:T(128)} %get-tuple-element.73) | copy-start | bytes 388
  65.1 4.9 %copy-start.5 = (s32[32]{0:T(128)S(1)}, s32[32]{0:T(128)}, u32[]{:S(2)}) copy-start(s32[32]{0:T(128)} %get-tuple-element.74) | copy-start | bytes 388
  65.1 12.9 %copy-start.3 = (s32[16]{0:T(128)S(1)}, s32[16]{0:T(128)}, u32[]{:S(2)}) copy-start(s32[16]{0:T(128)} %add.190) | copy-start | bytes 196
  65.1 10.4 %collective-permute-start.28 = (f32[128,256]{1,0:T(8,128)S(1)}, f32[128,256]{1,0:T(8,128)S(1)}, u32[]{:S(2)}, u32[]{:S(2)}) collective-permute-start(f32[128,256]{1,0:T(8,128)S(1)} %get-tuple-element.54), channel_id=1, source_target_pairs={{0,24},{8,16},{16,8},{24,0},{1,25},{9,17},{17,9},{25,1},{2,26},{10... | collective-permute-start | bytes 393224 | tf_op jit(solution)/shard_map/ppermute | solution.py:24
  69.9 8.1 %collective-permute-start.16 = (f32[128,256]{1,0:T(8,128)S(1)}, f32[128,256]{1,0:T(8,128)S(1)}, u32[]{:S(2)}, u32[]{:S(2)}) collective-permute-start(f32[128,256]{1,0:T(8,128)S(1)} %get-tuple-element.46), channel_id=1, source_target_pairs={{0,8},{8,0},{16,24},{24,16},{1,9},{9,1},{17,25},{25,17},{2,10},{10... | collective-permute-start | bytes 393224 | tf_op jit(solution)/shard_map/ppermute | solution.py:24
  71.1 15.5 %collective-permute-start.18 = (f32[128,256]{1,0:T(8,128)S(1)}, f32[128,256]{1,0:T(8,128)S(1)}, u32[]{:S(2)}, u32[]{:S(2)}) collective-permute-start(f32[128,256]{1,0:T(8,128)S(1)} %get-tuple-element.47), channel_id=1, source_target_pairs={{0,16},{8,24},{16,0},{24,8},{1,17},{9,25},{17,1},{25,9},{2,18},{10... | collective-permute-start | bytes 393224 | tf_op jit(solution)/shard_map/ppermute | solution.py:24
  74.0 12.6 %collective-permute-start.20 = (f32[128,256]{1,0:T(8,128)S(1)}, f32[128,256]{1,0:T(8,128)S(1)}, u32[]{:S(2)}, u32[]{:S(2)}) collective-permute-start(f32[128,256]{1,0:T(8,128)S(1)} %get-tuple-element.48), channel_id=1, source_target_pairs={{0,24},{8,16},{16,8},{24,0},{1,25},{9,17},{17,9},{25,1},{2,26},{10... | collective-permute-start | bytes 393224 | tf_op jit(solution)/shard_map/ppermute | solution.py:24
  75.5 11.7 %collective-permute-start.23 = (f32[128,256]{1,0:T(8,128)S(1)}, f32[128,256]{1,0:T(8,128)S(1)}, u32[]{:S(2)}, u32[]{:S(2)}) collective-permute-start(f32[128,256]{1,0:T(8,128)S(1)} %get-tuple-element.51.refs_0_), channel_id=1, source_target_pairs={{0,1},{1,0},{2,3},{3,2},{4,5},{5,4},{6,7},{7,6},{8,9},{9,8},{10,11... | collective-permute-start | bytes 393224 | tf_op jit(solution)/shard_map/ppermute | solution.py:24
  75.5 11.7 %collective-permute-start.25 = (f32[128,256]{1,0:T(8,128)S(1)}, f32[128,256]{1,0:T(8,128)S(1)}, u32[]{:S(2)}, u32[]{:S(2)}) collective-permute-start(f32[128,256]{1,0:T(8,128)S(1)} %collective-permute-done.24.refs_2_), channel_id=1, source_target_pairs={{0,1},{1,0},{2,3},{3,2},{4,5},{5,4},{6,7},{7,6},{8,9},{9,8},{10,11... | collective-permute-start | bytes 393224 | tf_op jit(solution)/shard_map/ppermute | solution.py:24
  77.9 9.8 %collective-permute-start.27 = (f32[128,256]{1,0:T(8,128)S(1)}, f32[128,256]{1,0:T(8,128)S(1)}, u32[]{:S(2)}, u32[]{:S(2)}) collective-permute-start(f32[128,256]{1,0:T(8,128)S(1)} %collective-permute-done.26.refs_4_), channel_id=1, source_target_pairs={{0,1},{1,0},{2,3},{3,2},{4,5},{5,4},{6,7},{7,6},{8,9},{9,8},{10,11... | collective-permute-start | bytes 393224 | tf_op jit(solution)/shard_map/ppermute | solution.py:24
  86.5 2.2 %collective-permute-start.29 = (f32[128,256]{1,0:T(8,128)S(1)}, f32[128,256]{1,0:T(8,128)S(1)}, u32[]{:S(2)}, u32[]{:S(2)}) collective-permute-start(f32[128,256]{1,0:T(8,128)S(1)} %collective-permute-done.28.refs_6_), channel_id=1, source_target_pairs={{0,1},{1,0},{2,3},{3,2},{4,5},{5,4},{6,7},{7,6},{8,9},{9,8},{10,11... | collective-permute-start | bytes 393224 | tf_op jit(solution)/shard_map/ppermute | solution.py:24
  86.6 5.1 %collective-permute-start.15 = (f32[128,256]{1,0:T(8,128)S(1)}, f32[128,256]{1,0:T(8,128)S(1)}, u32[]{:S(2)}, u32[]{:S(2)}) collective-permute-start(f32[128,256]{1,0:T(8,128)S(1)} %get-tuple-element.45.refs_0_), channel_id=1, source_target_pairs={{0,1},{1,0},{2,3},{3,2},{4,5},{5,4},{6,7},{7,6},{8,9},{9,8},{10,11... | collective-permute-start | bytes 393224 | tf_op jit(solution)/shard_map/ppermute | solution.py:24
  87.2 4.5 %collective-permute-start.17 = (f32[128,256]{1,0:T(8,128)S(1)}, f32[128,256]{1,0:T(8,128)S(1)}, u32[]{:S(2)}, u32[]{:S(2)}) collective-permute-start(f32[128,256]{1,0:T(8,128)S(1)} %collective-permute-done.16.refs_2_), channel_id=1, source_target_pairs={{0,1},{1,0},{2,3},{3,2},{4,5},{5,4},{6,7},{7,6},{8,9},{9,8},{10,11... | collective-permute-start | bytes 393224 | tf_op jit(solution)/shard_map/ppermute | solution.py:24
  87.3 4.4 %collective-permute-start.19 = (f32[128,256]{1,0:T(8,128)S(1)}, f32[128,256]{1,0:T(8,128)S(1)}, u32[]{:S(2)}, u32[]{:S(2)}) collective-permute-start(f32[128,256]{1,0:T(8,128)S(1)} %collective-permute-done.18.refs_4_), channel_id=1, source_target_pairs={{0,1},{1,0},{2,3},{3,2},{4,5},{5,4},{6,7},{7,6},{8,9},{9,8},{10,11... | collective-permute-start | bytes 393224 | tf_op jit(solution)/shard_map/ppermute | solution.py:24
  87.7 4.0 %collective-permute-start.21 = (f32[128,256]{1,0:T(8,128)S(1)}, f32[128,256]{1,0:T(8,128)S(1)}, u32[]{:S(2)}, u32[]{:S(2)}) collective-permute-start(f32[128,256]{1,0:T(8,128)S(1)} %collective-permute-done.20.refs_6_), channel_id=1, source_target_pairs={{0,1},{1,0},{2,3},{3,2},{4,5},{5,4},{6,7},{7,6},{8,9},{9,8},{10,11... | collective-permute-start | bytes 393224 | tf_op jit(solution)/shard_map/ppermute | solution.py:24
  90.1 9.2 %collective-permute-start.30 = (f32[512,128]{1,0:T(8,128)S(1)}, f32[512,128]{1,0:T(8,128)S(1)}, u32[]{:S(2)}, u32[]{:S(2)}) collective-permute-start(f32[512,128]{1,0:T(8,128)S(1)} %get-tuple-element.56), channel_id=1, source_target_pairs={{0,2},{1,3},{2,0},{3,1},{4,6},{5,7},{6,4},{7,5},{8,10},{9,11},{10,... | collective-permute-start | bytes 786440 | tf_op jit(solution)/shard_map/ppermute | solution.py:24
  93.1 11.4 %collective-permute-start.22 = (f32[512,128]{1,0:T(8,128)S(1)}, f32[512,128]{1,0:T(8,128)S(1)}, u32[]{:S(2)}, u32[]{:S(2)}) collective-permute-start(f32[512,128]{1,0:T(8,128)S(1)} %get-tuple-element.50), channel_id=1, source_target_pairs={{0,2},{1,3},{2,0},{3,1},{4,6},{5,7},{6,4},{7,5},{8,10},{9,11},{10,... | collective-permute-start | bytes 786440 | tf_op jit(solution)/shard_map/ppermute | solution.py:24

commit v2 on v1

v2 whole, which is shorter than its diff:
```python
import functools

import jax
import jax.numpy as jnp
from jax import lax
from jax.experimental import pallas as pl
from jax.experimental.pallas import tpu as pltpu
from jax.sharding import PartitionSpec as P

GP = 2048
f32, bf16 = jnp.float32, jnp.bfloat16
VMEM_LIMIT = 32 * 1024 * 1024
EXTRA = 8
CHUNKS = 2
FINE = 32
HALVES_COST, SCALE_COST, GREENS_COST, TOKEN_COST, BEHIND = (12, 3), 1, 3, 3.6, 0


def bits_of(size):
    return [1 << b for b in range(size.bit_length() - 1)][::-1]


def swap(value, axis, bit):
    size = lax.axis_size(axis)
    return lax.ppermute(value, axis, [(i, i ^ bit) for i in range(size)])


def split(value):
    high = value.astype(bf16)
    return high, (value - high.astype(f32)).astype(bf16)


def dot(a, b):
    return lax.dot_general(a, b, (((1,), (0,)), ((), ())), preferred_element_type=f32)


def column_kernel(T, place, occ, emp, *outs):
    piece = outs[0].shape[1]
    for s in range(T):
        lines = pl.ds(pl.multiple_of((place[0] ^ s) * piece, piece), piece)
        outs[s][...] = jnp.concatenate([occ[lines, :].T, emp[lines, :].T], 0)


def row_kernel(place, times, occ, emp, occ_energy, emp_energy, _, *outs):
    chunks, lines, breadth = outs[0].shape
    occ_n, n = occ.shape[1], lines - EXTRA
    for d in range(len(outs)):
        for c in range(chunks):
            first = (((place[2] // 2) ^ d) * chunks + c) * breadth
            at = pl.ds(pl.multiple_of(first, breadth), breadth)
            outs[d][c, 0:occ_n, :] = occ[at, :].T
            outs[d][c, occ_n:n, :] = emp[at, :].T
            outs[d][c, n:, :] = jnp.full((EXTRA, breadth), times[0], f32)
            outs[d][c, n : n + 1, 0:occ_n] = occ_energy[...]
            outs[d][c, n : n + 1, occ_n:n] = emp_energy[...]


def scale_kernel(chunk, T, C, counts, *refs):
    occ_r, emp_r = counts
    n = occ_r + emp_r
    k_occ = occ_r * T * C
    place, rows = refs[0], refs[1:5]
    s_high, s_low, flat, falls = refs[5:]
    q = place[2]
    breadth, half = flat.shape[1], T // 2
    lane = lax.broadcasted_iota(jnp.int32, (1, breadth), 1)
    instants = jnp.zeros((1, breadth), f32)
    for s in range(T):
        instants = jnp.where(lane == s, rows[2 * (s // half)][s % half, 0, 0, n + 1 : n + 2, :], instants)
    for s in range(T):
        for core in range(2):
            for d in range(C // 2):
                at = s * C + (q ^ (2 * d + core))
                block = rows[2 * (s // half) + core].at[s % half, d]
                occ_at = pl.ds(pl.multiple_of(at * occ_r, 8), occ_r)
                emp_at = pl.ds(pl.multiple_of(k_occ + at * emp_r, 8), emp_r)
                flat[occ_at, :] = block[chunk, 0:occ_r, :]
                flat[emp_at, :] = block[chunk, occ_r:n, :]
                levels = block[0, n : n + EXTRA, :].T[0:n, 0:1]
                decay = jnp.exp(-(levels * instants))
                falls[occ_at, :] = decay[0:occ_r]
                falls[emp_at, :] = decay[occ_r:n]
    step = 128
    for at in range(0, flat.shape[0], step):
        turned = flat[at : at + step, :].T
        decay = falls[at : at + step, :].T
        for t in range(T):
            high, low = split(turned * decay[t : t + 1, :])
            s_high[t * breadth : (t + 1) * breadth, at : at + step] = high
            s_low[t * breadth : (t + 1) * breadth, at : at + step] = low


def halves_kernel(slots, C, X, counts, waits, *refs):
    occ_c, emp_c = counts
    place, cols = refs[0], refs[1 : 1 + len(slots)]
    high, low, columns = refs[1 + len(slots) + waits :]
    x, q, piece = place[1], place[2], cols[0].shape[-1]
    size = columns.shape[0] // (X * (occ_c + emp_c))
    k_occ = occ_c * X * size
    for part, where in enumerate(slots):
        for i, (dx, dq, s) in enumerate(where):
            lanes = slice((dq // 2) * piece, (dq // 2) * piece + piece)
            at = s * X + (x ^ dx)
            columns[pl.ds(pl.multiple_of(at * occ_c, 8), occ_c), lanes] = cols[part][i, 0:occ_c, :]
            columns[pl.ds(pl.multiple_of(k_occ + at * emp_c, 8), emp_c), lanes] = cols[part][i, occ_c : occ_c + emp_c, :]
    line = lax.broadcasted_iota(jnp.int32, (piece, piece), 0)
    lane = lax.broadcasted_iota(jnp.int32, (piece, piece), 1)
    for d in range(C // 2):
        lanes = slice(d * piece, (d + 1) * piece)
        goal = jnp.where((q ^ (2 * d)) >= C // 2, piece - 1 - lane, lane)
        turn = jnp.where(line == goal, 1.0, 0.0).astype(bf16)
        a, b = split(columns[:, lanes])
        high[:, lanes] = dot(a, turn).astype(bf16)
        low[:, lanes] = dot(b, turn).astype(bf16)


def green_kernel(T, k_occ, *refs):
    place, weights, s_high, s_low = refs[:4]
    halves, outs = refs[4:-T], refs[-T:]
    k, breadth = place[0], outs[0].shape[0]
    groups = len(halves) // 2

    def green(first, size):
        total = None
        for g in range(groups):
            share = size // groups
            lines = slice(first // groups, first // groups + share)
            lanes = slice(first + g * share, first + (g + 1) * share)
            c_high, c_low = halves[2 * g][lines, :], halves[2 * g + 1][lines, :]
            a_high, a_low = s_high[:, lanes], s_low[:, lanes]
            term = dot(a_high, c_high) + dot(a_high, c_low) + dot(a_low, c_high)
            total = term if total is None else total + term
        return total

    product = green(0, k_occ) * green(k_occ, s_high.shape[1] - k_occ)
    for w in range(T):
        total = weights[k ^ w, k] * product[0:breadth, :]
        for t in range(1, T):
            total += weights[k ^ w, k ^ t] * product[t * breadth : (t + 1) * breadth, :]
        outs[w][...] = total


def token_kernel(_, out):
    out[...] = jnp.zeros_like(out)


def pack_kernel(T, *refs):
    for s in range(T):
        refs[-1][s] = refs[s][...]


def cost(us):
    return pl.CostEstimate(flops=int(us * 1e9), bytes_accessed=0, transcendentals=0)


def table_kernel(near, far, high, low):
    share = far.shape[1]
    for h in range(share):
        c, s = far[0, h : h + 1, :], far[1, h : h + 1, :]
        for odd in range(2):
            value = c * near[2 * odd] - s * near[2 * odd + 1]
            a, b = split(value)
            high[odd, h * FINE : (h + 1) * FINE, :] = a
            low[odd, h * FINE : (h + 1) * FINE, :] = b


def mode_kernel(T, waits, high, low, *refs):
    here, there = refs[:2]
    outs, both = refs[2 + waits : -1], refs[-1]
    _, breadth, width = here.shape
    step = width // 2 if width >= 256 else width
    groups = width // step
    at = 0
    for s in range(T):
        for d in range(groups):
            mine = here[s, :, d * step : (d + 1) * step]
            e = groups - 1 - d
            theirs = there[s ^ (T - 1), :, e * step : (e + 1) * step]
            for odd, value in enumerate((mine + theirs, mine - theirs)):
                a, b = split(value.T)
                both[odd, at : at + step, 0:breadth] = a
                both[odd, at : at + step, breadth:] = b
            at += step
    share = outs[0].shape[0] // 2
    for block, out in enumerate(outs):
        lines = slice(block * share, (block + 1) * share)
        for odd in range(2):
            twice = dot(high[odd, lines, :], both[odd])
            once = dot(low[odd, lines, :], both[odd, :, 0:breadth])
            out[pl.ds(odd, share, stride=2), :] = twice[:, :breadth] + twice[:, breadth:] + once


def place_kernel(first, place, *refs):
    pieces, out, done = refs[:-2], refs[-2], refs[-1]
    copies = []
    for i, (chunk, d) in enumerate(first):
        breadth = pieces[i].shape[1]
        at = ((place[2] // 2) ^ d) * CHUNKS + chunk
        copies.append(pltpu.make_async_copy(pieces[i], out.at[0, :, pl.ds(pl.multiple_of(at * breadth, breadth), breadth)], done.at[i]))
    for copy in copies:
        copy.start()
    for copy in copies:
        copy.wait()


def per_device(occ_rows, emp_rows, occ_cols, emp_cols, occ_energy, emp_energy, times, freq_weight):
    T, X, C = lax.axis_size("tm"), lax.axis_size("row"), lax.axis_size("col")
    k, x, q = lax.axis_index("tm"), lax.axis_index("row"), lax.axis_index("col")
    number_rows, number_cols = occ_rows.shape[0], occ_cols.shape[0]
    occ_r, emp_r, occ_c, emp_c = (a.shape[1] for a in (occ_rows, emp_rows, occ_cols, emp_cols))
    n, m = occ_r + emp_r, occ_c + emp_c
    H = C // 2
    rp, jp = number_rows // (H * CHUNKS), number_cols // T
    k_occ, k_emp = occ_r * T * C, emp_r * T * C
    high_bits = [("col", b) for b in bits_of(C) if b > 1]
    row_bits = [("row", b) for b in bits_of(X)]

    place = jnp.stack([k, x, q]).astype(jnp.int32)
    smem = pl.BlockSpec(memory_space=pltpu.SMEM)
    vmem = pl.BlockSpec(memory_space=pltpu.VMEM)
    hbm = pl.BlockSpec(memory_space=pl.ANY)
    params = pltpu.CompilerParams(vmem_limit_bytes=VMEM_LIMIT)

    pieces = pl.pallas_call(
        functools.partial(column_kernel, T),
        out_shape=[jax.ShapeDtypeStruct((m, jp), f32)] * T,
        in_specs=[smem] + [pl.BlockSpec()] * 2,
        out_specs=[vmem] * T,
        compiler_params=params,
        cost_estimate=cost(0),
        name="columns",
    )(place, occ_cols, emp_cols)
    col_slots = [pieces[0]] + [swap(pieces[s], "tm", s) for s in range(1, T)]

    row_pieces = pl.pallas_call(
        row_kernel,
        out_shape=[jax.ShapeDtypeStruct((CHUNKS, n + EXTRA, rp), f32)] * H,
        in_specs=[smem, smem] + [pl.BlockSpec()] * 4 + [hbm],
        out_specs=[vmem] * H,
        compiler_params=params,
        cost_estimate=cost(0),
        name="rows",
    )(place, times, occ_rows, emp_rows, occ_energy, emp_energy, pieces[0])
    own_rows = jnp.stack([row_pieces[0]] + [swap(row_pieces[d], "col", 2 * d) for d in range(1, H)])
    got_rows = {0: own_rows}
    for bit in bits_of(T):
        for s in list(got_rows):
            got_rows[s ^ bit] = swap(got_rows[s], "tm", bit)
    row_slots = []
    for first in range(0, T, T // 2):
        mine = jnp.stack([got_rows[s] for s in range(first, first + T // 2)])
        row_slots += [mine, swap(mine, "col", 1)]

    groups = [list(range(T))[: T // 2], list(range(T))[T // 2 :]]
    cuts = [[groups[0]], [groups[1][: T // 4], groups[1][T // 4 :]]]
    orders = [[row_bits + high_bits], [row_bits + high_bits, high_bits + row_bits]]
    cols, slots = [], []
    for group, parts, ways in zip(groups, cuts, orders):
        there, where = [], []
        for part, order in zip(parts, ways):
            values = [(jnp.stack([col_slots[s] for s in part]), [(0, 0, group.index(s)) for s in part])]
            for axis, bit in order:
                if len(values) > 1:
                    values = [(jnp.concatenate([v for v, _ in values], 0), sum((w for _, w in values), []))]
                value, at = values[0]
                far = [(dx ^ bit, dq, f) if axis == "row" else (dx, dq ^ bit, f) for dx, dq, f in at]
                values.append((swap(value, axis, bit), far))
            there += [v for v, _ in values]
            where += [w for _, w in values]
        cols.append(there)
        slots.append(where)

    wide = H * jp

    slot = jnp.arange(T, dtype=jnp.int32)[:, None, None]
    dq = 2 * jnp.arange(H, dtype=jnp.int32)[None, :, None]
    inner = jnp.arange(jp, dtype=jnp.int32)[None, None, :]
    source = q ^ dq
    lane = jnp.where(source >= C // 2, jp - 1 - inner, inner)
    column = (source * number_cols + (k ^ slot) * jp + lane).reshape(-1)
    odd_column = 2 * column + 1
    share = GP // C

    def angle(wave):
        phase = (odd_column[None, :] * wave[:, None]) % (4 * GP)
        return jnp.pi * phase.astype(f32) / (2.0 * GP)

    scale = jnp.sqrt(2.0 / GP)
    fine = 2 * jnp.arange(FINE, dtype=jnp.int32)
    per_block = share // (2 * FINE)
    blocks = q ^ (2 * jnp.arange(H, dtype=jnp.int32)[::-1])
    coarse = (blocks[:, None] * share + 2 * FINE * jnp.arange(per_block, dtype=jnp.int32)[None, :]).reshape(-1)
    even, odd, far = angle(fine), angle(fine + 1), angle(coarse)
    near = jnp.stack([scale * jnp.cos(even), scale * jnp.sin(even), scale * jnp.cos(odd), scale * jnp.sin(odd)])
    far = jnp.stack([jnp.cos(far), jnp.sin(far)])
    all_cols = T * wide
    t_high, t_low = pl.pallas_call(
        table_kernel,
        out_shape=[jax.ShapeDtypeStruct((2, H * share // 2, all_cols), bf16)] * 2,
        in_specs=[pl.BlockSpec()] * 2,
        out_specs=[vmem] * 2,
        compiler_params=params,
        cost_estimate=cost(0),
        name="cosines",
    )(near, far)

    halves, waits = [], [t_high, row_slots[1]]
    for g, group in enumerate(groups):
        got = pl.pallas_call(
            functools.partial(halves_kernel, slots[g], C, X, (occ_c, emp_c), len(waits)),
            out_shape=[jax.ShapeDtypeStruct(((k_occ + k_emp) // len(groups), wide), bf16)] * 2,
            in_specs=[smem] + [pl.BlockSpec()] * len(cols[g]) + [hbm] * len(waits),
            out_specs=[vmem] * 2,
            scratch_shapes=[pltpu.VMEM(((k_occ + k_emp) // len(groups), wide), f32)],
            compiler_params=params,
            cost_estimate=cost(HALVES_COST[g]),
            name="halves",
        )(place, *cols[g], *waits)
        halves += got
        waits = [got[0]]

    own = []
    for chunk in range(CHUNKS):
        scaled = pl.pallas_call(
            functools.partial(scale_kernel, chunk, T, C, (occ_r, emp_r)),
            out_shape=[jax.ShapeDtypeStruct((T * rp, k_occ + k_emp), bf16)] * 2,
            in_specs=[smem] + [pl.BlockSpec()] * len(row_slots),
            out_specs=[vmem] * 2,
            scratch_shapes=[pltpu.VMEM((k_occ + k_emp, rp), f32)] * 2,
            compiler_params=params,
            cost_estimate=cost(SCALE_COST),
            name="scale",
        )(place, *row_slots)
        series = pl.pallas_call(
            functools.partial(green_kernel, T, k_occ),
            out_shape=[jax.ShapeDtypeStruct((rp, wide), f32)] * T,
            in_specs=[smem, smem] + [vmem] * (2 + len(halves)),
            out_specs=[vmem] * T,
            compiler_params=params,
            cost_estimate=cost(GREENS_COST),
            name="greens",
        )(place, freq_weight, *scaled, *halves)
        here = [series[0]] + [None] * (T - 1)
        for s in range(T - 1, 0, -1):
            here[s] = swap(series[s], "tm", s)
        own.append(here)

    def assemble(parts, before):
        return pl.pallas_call(
            functools.partial(place_kernel, [at for at, _ in parts]),
            out_shape=jax.ShapeDtypeStruct((1, share, number_rows), f32),
            in_specs=[smem] + [hbm] * (len(parts) + len(before)),
            out_specs=hbm,
            scratch_shapes=[pltpu.SemaphoreType.DMA((len(parts),))],
            input_output_aliases={1 + len(parts): 0} if before else {},
            compiler_params=params,
            cost_estimate=cost(0),
            name="assemble",
        )(place, *[part for _, part in parts], *before)

    early, late = [], []
    for chunk in range(CHUNKS):
        behind = [own[chunk + 1][BEHIND]] if chunk + 1 < CHUNKS else []
        mine = pl.pallas_call(
            functools.partial(pack_kernel, T),
            out_shape=jax.ShapeDtypeStruct((T, rp, wide), f32),
            in_specs=[vmem] * T + [hbm] * len(behind),
            out_specs=vmem,
            compiler_params=params,
            cost_estimate=cost(0),
            name="pack",
        )(*own[chunk], *behind)
        waits = [
            pl.pallas_call(
                token_kernel,
                out_shape=jax.ShapeDtypeStruct((8, 128), f32),
                in_specs=[hbm],
                compiler_params=params,
                cost_estimate=cost(TOKEN_COST),
                name="token",
            )(part)
            for _, part in late
        ]
        made = pl.pallas_call(
            functools.partial(mode_kernel, T, len(waits)),
            out_shape=[jax.ShapeDtypeStruct((share, rp), f32)] * H,
            in_specs=[vmem] * 4 + [hbm] * len(waits),
            out_specs=[vmem] * H,
            scratch_shapes=[pltpu.VMEM((2, all_cols, 2 * rp), bf16)],
            compiler_params=params,
            cost_estimate=cost(0),
            name="modes",
        )(t_high, t_low, mine, swap(mine, "col", 1), *waits)
        early = early + late + [((chunk, 0), made[H - 1])]
        late = [((chunk, d), swap(made[H - 1 - d], "col", 2 * d)) for d in range(1, H)]
    return assemble(late, [assemble(early, [])])


def solution(mesh):
    return jax.shard_map(
        per_device,
        mesh=mesh,
        in_specs=(
            P("row", ("tm", "col")),
            P("row", ("tm", "col")),
            P("col", ("tm", "row")),
            P("col", ("tm", "row")),
            P(None, ("tm", "col")),
            P(None, ("tm", "col")),
            P("tm"),
            P(),
        ),
        out_specs=P("tm", "col", "row"),
        check_vma=False,
    )
```

time: 107 us -> 92.2 us (0.86)
  Pallas kernels: 11.8 us -> 20.5 us
  other arithmetic: 8.88 us -> 2.17 us
  local copies, waits for them, and re-layouts: 9 us -> 2.71 us
  waiting for transfers between devices: 40.8 us -> 35 us
  starting transfers between devices: 34.6 us -> 30.4 us
    pallas_call x5 -> x15, Pallas kernels: 10.8 us -> 19.6 us  [the longest x2 5.2 us: per_device(): pl.pallas_call(functools.partial(scale_kernel, chunk, T, C, (occ_r, emp_r...]
    ppermute x31 -> x25, waiting for transfers between devices: 40.8 us -> 35 us  [swap(): return lax.ppermute(value, axis, [(i, i ^ bit) for i in range(size)])]
    concatenate x6 -> x3, other arithmetic: 4.8 us -> 0.1 us  [per_device(): jnp.concatenate([v for v, _ in values], 0)]
    ppermute x31 -> x25, starting transfers between devices: 34.6 us -> 30.4 us  [swap(): return lax.ppermute(value, axis, [(i, i ^ bit) for i in range(size)])]
    exp x2 -> x0, other arithmetic: 1.43 us -> none  [decays(): return jnp.exp(-(instants[:, None] * energies.reshape(1, -1)))]
    mul x2 -> x0, local copies, waits for them, and re-layouts: 1.43 us -> none  [decays(): return jnp.exp(-(instants[:, None] * energies.reshape(1, -1)))]
    gather x4 -> x0, local copies, waits for them, and re-layouts: 1.31 us -> none  [per_device(): weights = freq_weight[k ^ step][:, k ^ step].reshape(-1)]
    unnamed x22 -> x14, local copies, waits for them, and re-layouts: 1.39 us -> 2.53 us
  transfers between devices with their start and end apart: 31 -> 25, of which waited for: 8 -> 11; matrix products, arithmetic and copies ran while one was open for 14% -> 3% of each run, Pallas kernels for 6% -> 13%
where the time goes in v2:
time: 92.2 us; the launch traced here: 92 us
  waiting for transfers between devices  35 us (38%)
  starting transfers between devices  30.4 us (33%)
  Pallas kernels  20.5 us (22%)
  local copies, waits for them, and re-layouts  2.71 us (3%)
  other arithmetic  2.17 us (2%)
  between operations  1.18 us (1%)
    ppermute x25, waiting for transfers between devices, swap(): return lax.ppermute(value, axis, [(i, i ^ bit) for i in range(size)])  35 us
    ppermute x25, starting transfers between devices, swap(): return lax.ppermute(value, axis, [(i, i ^ bit) for i in range(size)])  30.4 us
    pallas_call x2, Pallas kernels, per_device(): pl.pallas_call(functools.partial(scale_kernel, chunk, T, C, (occ_r, emp_r...  5.2 us
    pallas_call x2, Pallas kernels, per_device(): pl.pallas_call(functools.partial(green_kernel, T, k_occ), out_shape=[jax....  4.88 us
    pallas_call x2, Pallas kernels, per_device(): pl.pallas_call(functools.partial(mode_kernel, T, len(waits)), out_shape=[...  3.07 us
    pallas_call x2, Pallas kernels, assemble(): pl.pallas_call(functools.partial(place_kernel, [at for at, _ in parts]),...  2.71 us
    unnamed x14, local copies, waits for them, and re-layouts  2.53 us
    pallas_call x2, Pallas kernels, per_device(): pl.pallas_call(functools.partial(halves_kernel, slots[g], C, X, (occ_c, e...  2.07 us
  transfers between devices with their start and end apart: 25, of which 11 were waited for; matrix products, arithmetic and copies ran while one was open for 3% of the time, Pallas kernels for 13%

profile of v2, /device:TPU:0, one launch (start us, length us, event | category | flops | bytes accessed | tf_op | source)
XLA Modules:
  0.0 92.0 jit_solution(8886582864162428069)
XLA Ops:
  0.0 1.1 %copy.10.occ = f32[512,64]{1,0:T(8,128)S(1)} copy(f32[512,64]{0,1:T(8,128)} %param.10) | data formatting | bytes 262144 | tf_op args[2]
  1.1 1.2 %copy.11.emp = f32[512,192]{1,0:T(8,128)S(1)} copy(f32[512,192]{0,1:T(8,128)} %param.11) | data formatting | bytes 786432 | tf_op args[3]
  2.3 0.1 pad_add_fusion.place.refs_0_
  2.4 0.8 columns.1
  3.2 3.1 %collective-permute-start.6 = (f32[256,128]{1,0:T(8,128)S(1)}, f32[256,128]{1,0:T(8,128)S(1)}, u32[]{:S(2)}, u32[]{:S(2)}) collective-permute-start(f32[256,128]{1,0:T(8,128)S(1)} %get-tuple-element.40), channel_id=1, source_target_pairs={{0,8},{8,0},{16,24},{24,16},{1,9},{9,1},{17,25},{25,17},{2,10},{10... | collective-permute-start | bytes 393224 | tf_op jit(solution)/shard_map/ppermute | solution.py:25
  6.3 2.6 %collective-permute-start.9 = (f32[256,128]{1,0:T(8,128)S(1)}, f32[256,128]{1,0:T(8,128)S(1)}, u32[]{:S(2)}, u32[]{:S(2)}) collective-permute-start(f32[256,128]{1,0:T(8,128)S(1)} %get-tuple-element.43), channel_id=1, source_target_pairs={{0,16},{8,24},{16,0},{24,8},{1,17},{9,25},{17,1},{25,9},{2,18},{10... | collective-permute-start | bytes 393224 | tf_op jit(solution)/shard_map/ppermute | solution.py:25
  9.5 0.1 copy.12.occ
  9.7 0.1 copy.13.emp
  9.8 0.7 rows.1
  10.6 1.8 %collective-permute-start = (f32[2,136,128]{2,1,0:T(8,128)S(1)}, f32[2,136,128]{2,1,0:T(8,128)S(1)}, u32[]{:S(2)}, u32[]{:S(2)}) collective-permute-start(f32[2,136,128]{2,1,0:T(8,128)S(1)} %get-tuple-element.37), channel_id=1, source_target_pairs={{0,2},{1,3},{2,0},{3,1},{4,6},{5,7},{6,4},{7,5},{8,10},{9,11},{10,... | collective-permute-start | bytes 417800 | tf_op jit(solution)/shard_map/ppermute | solution.py:25
  12.4 0.1 rev.3
  12.5 0.1 iota_select_fusion
  12.6 0.1 broadcast_add_fusion
  12.7 0.1 multiply_add_fusion
  12.8 1.1 %cosine_multiply_fusion.1 = (f32[1,32,1024]{2,1,0:T(8,128)S(1)}, f32[1,32,1024]{2,1,0:T(8,128)S(1)}, f32[1,32,1024]{2,1,0:T(8,128)S(1)}, f32[1,32,1024]{2,1,0:T(8,128)S(1)}) fusion(s32[32]{0:T(128)S(1)} %get-tuple-element.73, s32[1024]{0:T(1024)S(1)} %bitcast.28, s32[32]{0:T(128)S(1)} %get-tuple-element.74), kind=kLoop, calls=%fused_computation.28 | loop fusion | flops 1048576 | bytes 528640 | tf_op jit(solution)/shard_map/mul | solution.py:294
  13.9 0.1 broadcast_add_fusion.1
  14.0 0.1 add.145
  14.0 0.0 collective-permute-done.6
  14.1 1.6 %collective-permute-start.7 = (f32[2,256,128]{2,1,0:T(8,128)S(1)}, f32[2,256,128]{2,1,0:T(8,128)S(1)}, u32[]{:S(2)}, u32[]{:S(2)}) collective-permute-start(f32[2,256,128]{2,1,0:T(8,128)S(1)} %pad_maximum_fusion.5), channel_id=1, source_target_pairs={{0,4},{4,0},{1,5},{5,1},{2,6},{6,2},{3,7},{7,3},{8,12},{12,8},{9,1... | collective-permute-start | bytes 786440 | tf_op jit(solution)/shard_map/ppermute | solution.py:25
  15.6 0.1 collective-permute-done
  15.8 1.0 %collective-permute-start.1 = (f32[2,2,136,128]{3,2,1,0:T(8,128)S(1)}, f32[2,2,136,128]{3,2,1,0:T(8,128)S(1)}, u32[]{:S(2)}, u32[]{:S(2)}) collective-permute-start(f32[2,2,136,128]{3,2,1,0:T(8,128)S(1)} %get-tuple-element.62), channel_id=1, source_target_pairs={{0,8},{8,0},{16,24},{24,16},{1,9},{9,1},{17,25},{25,17},{2,10},{10... | collective-permute-start | bytes 835592 | tf_op jit(solution)/shard_map/ppermute | solution.py:25
  16.7 0.3 fusion.10
  17.1 0.7 collective-permute-done.12
  17.8 1.5 %collective-permute-start.13 = (f32[1,256,128]{2,1,0:T(8,128)S(1)}, f32[1,256,128]{2,1,0:T(8,128)S(1)}, u32[]{:S(2)}, u32[]{:S(2)}) collective-permute-start(f32[1,256,128]{2,1,0:T(8,128)S(1)} %bitcast.26), channel_id=1, source_target_pairs={{0,2},{1,3},{2,0},{3,1},{4,6},{5,7},{6,4},{7,5},{8,10},{9,11},{10,... | collective-permute-start | bytes 393224 | tf_op jit(solution)/shard_map/ppermute | solution.py:25
  19.3 4.4 %collective-permute-start.3 = (f32[2,2,136,128]{3,2,1,0:T(8,128)S(1)}, f32[2,2,136,128]{3,2,1,0:T(8,128)S(1)}, u32[]{:S(2)}, u32[]{:S(2)}) collective-permute-start(f32[2,2,136,128]{3,2,1,0:T(8,128)S(1)} %get-tuple-element.62), channel_id=1, source_target_pairs={{0,16},{8,24},{16,0},{24,8},{1,17},{9,25},{17,1},{25,9},{2,18},{10... | collective-permute-start | bytes 835592 | tf_op jit(solution)/shard_map/ppermute | solution.py:25
  23.7 0.0 collective-permute-done.7
  23.8 0.6 collective-permute-start.8
  24.3 1.5 %collective-permute-done.1 = f32[2,2,136,128]{3,2,1,0:T(8,128)S(1)} collective-permute-done((f32[2,2,136,128]{3,2,1,0:T(8,128)S(1)}, f32[2,2,136,128]{3,2,1,0:T(8,128)S(1)}, u32[]{:S(2)}, u32[]{:S(2)}) %collective-permute-start.1) | collective-permute-done | bytes 278560 | tf_op jit(solution)/shard_map/ppermute | solution.py:25
  25.9 0.1 pad_maximum_fusion.refs_1_
  25.9 0.1 collective-permute-start.2
  26.1 0.0 collective-permute-done.9
  26.1 1.6 %collective-permute-start.10 = (f32[1,256,128]{2,1,0:T(8,128)S(1)}, f32[1,256,128]{2,1,0:T(8,128)S(1)}, u32[]{:S(2)}, u32[]{:S(2)}) collective-permute-start(f32[1,256,128]{2,1,0:T(8,128)S(1)} %bitcast.24), channel_id=1, source_target_pairs={{0,4},{4,0},{1,5},{5,1},{2,6},{6,2},{3,7},{7,3},{8,12},{12,8},{9,1... | collective-permute-start | bytes 393224 | tf_op jit(solution)/shard_map/ppermute | solution.py:25
  27.6 7.5 %collective-permute-done.3 = f32[2,2,136,128]{3,2,1,0:T(8,128)S(1)} collective-permute-done((f32[2,2,136,128]{3,2,1,0:T(8,128)S(1)}, f32[2,2,136,128]{3,2,1,0:T(8,128)S(1)}, u32[]{:S(2)}, u32[]{:S(2)}) %collective-permute-start.3) | collective-permute-done | bytes 278560 | tf_op jit(solution)/shard_map/ppermute | solution.py:25
  35.1 0.9 %cosines.1 = (bf16[2,512,1024]{2,1,0:T(8,128)(2,1)S(1)}, bf16[2,512,1024]{2,1,0:T(8,128)(2,1)S(1)}) custom-call(f32[4,32,1024]{2,1,0:T(8,128)S(1)} %pad_maximum_fusion.2.near, f32[2,16,1024]{2,1,0:T(8,128)S(1)} %pad_maximum_fusion.8.far), custom_call_target="tpu_custom_call" | custom-call | tf_op jit(solution)/shard_map/cosines/pallas_call | solution.py:297
  36.1 0.0 collective-permute-done.13
  36.1 1.6 %collective-permute-start.14 = (f32[2,256,128]{2,1,0:T(8,128)S(1)}, f32[2,256,128]{2,1,0:T(8,128)S(1)}, u32[]{:S(2)}, u32[]{:S(2)}) collective-permute-start(f32[2,256,128]{2,1,0:T(8,128)S(1)} %pad_maximum_fusion.7.refs_3_), channel_id=1, source_target_pairs={{0,4},{4,0},{1,5},{5,1},{2,6},{6,2},{3,7},{7,3},{8,12},{12,8},{9,1... | collective-permute-start | bytes 786440 | tf_op jit(solution)/shard_map/ppermute | solution.py:25
  37.7 0.6 collective-permute-start.11
  38.3 4.0 %collective-permute-done.4 = f32[2,2,136,128]{3,2,1,0:T(8,128)S(1)} collective-permute-done((f32[2,2,136,128]{3,2,1,0:T(8,128)S(1)}, f32[2,2,136,128]{3,2,1,0:T(8,128)S(1)}, u32[]{:S(2)}, u32[]{:S(2)}) %collective-permute-start.4) | collective-permute-done | bytes 278560 | tf_op jit(solution)/shard_map/ppermute | solution.py:25
  42.3 0.1 collective-permute-start.5
  42.4 1.0 %halves.2 = (bf16[1024,256]{1,0:T(8,128)(2,1)S(1)}, bf16[1024,256]{1,0:T(8,128)(2,1)S(1)}) custom-call(s32[3]{0:T(128)S(1)} %pad_add_fusion.place.refs_0_, f32[4,256,128]{2,1,0:T(8,128)S(1)} %pad_maximum_fusion.3.refs_1_, f32[4,256,128]{2,1,0:T(8,128)S(1)} %collective-permute-done.8.refs_2_, bf16[2,512,1024]{2,1,0:T(8,128)(2,1)S(1)} %get-tuple-element.33.refs_3_.high, ...), custom_call_target="tpu_custom_call" | custom-call | flops 12000000000 | tf_op jit(solution)/shard_map/halves/pallas_call | solution.py:309
  43.5 0.8 collective-permute-done.11.refs_2_
  44.3 1.0 %halves.3 = (bf16[1024,256]{1,0:T(8,128)(2,1)S(1)}, bf16[1024,256]{1,0:T(8,128)(2,1)S(1)}) custom-call(s32[3]{0:T(128)S(1)} %pad_add_fusion.place.refs_0_, f32[2,256,128]{2,1,0:T(8,128)S(1)} %pad_maximum_fusion.6.refs_1_, f32[2,256,128]{2,1,0:T(8,128)S(1)} %collective-permute-done.11.refs_2_, f32[2,256,128]{2,1,0:T(8,128)S(1)} %pad_maximum_fusion.7.refs_3_, ...), custom_call_target="tpu_custom_call" | custom-call | flops 3000000000 | tf_op jit(solution)/shard_map/halves/pallas_call | solution.py:309
  45.3 0.0 copy-start.2
  45.4 2.6 %scale.3 = (bf16[512,2048]{1,0:T(8,128)(2,1)S(1)}, bf16[512,2048]{1,0:T(8,128)(2,1)S(1)}) custom-call(s32[3]{0:T(128)S(1)} %pad_add_fusion.place.refs_0_, f32[2,2,2,136,128]{4,3,2,1,0:T(8,128)S(1)} %pad_maximum_fusion.refs_1_, f32[2,2,2,136,128]{4,3,2,1,0:T(8,128)S(1)} %collective-permute-done.2.refs_2_.refs_4_, ...), custom_call_target="tpu_custom_call" | custom-call | flops 1000000000 | tf_op jit(solution)/shard_map/scale/pallas_call | solution.py:324
  48.0 2.4 %greens.3 = (f32[128,256]{1,0:T(8,128)S(1)}, f32[128,256]{1,0:T(8,128)S(1)}, f32[128,256]{1,0:T(8,128)S(1)}, f32[128,256]{1,0:T(8,128)S(1)}) custom-call(s32[3]{0:T(128)S(1)} %pad_add_fusion.place.refs_0_, f32[4,4]{1,0:T(4,128)S(1)} %copy-done.2, bf16[512,2048]{1,0:T(8,128)(2,1)S(1)} %get-tuple-element.51.refs_2_, ...), custom_call_target="tpu_custom_call" | custom-call | flops 3000000000 | tf_op jit(solution)/shard_map/greens/pallas_call | solution.py:334
  50.4 1.9 %collective-permute-start.19 = (f32[128,256]{1,0:T(8,128)S(1)}, f32[128,256]{1,0:T(8,128)S(1)}, u32[]{:S(2)}, u32[]{:S(2)}) collective-permute-start(f32[128,256]{1,0:T(8,128)S(1)} %get-tuple-element.54), channel_id=1, source_target_pairs={{0,8},{8,0},{16,24},{24,16},{1,9},{9,1},{17,25},{25,17},{2,10},{10... | collective-permute-start | bytes 393224 | tf_op jit(solution)/shard_map/ppermute | solution.py:25
  52.3 2.5 %collective-permute-start.21 = (f32[128,256]{1,0:T(8,128)S(1)}, f32[128,256]{1,0:T(8,128)S(1)}, u32[]{:S(2)}, u32[]{:S(2)}) collective-permute-start(f32[128,256]{1,0:T(8,128)S(1)} %get-tuple-element.56), channel_id=1, source_target_pairs={{0,24},{8,16},{16,8},{24,0},{1,25},{9,17},{17,9},{25,1},{2,26},{10... | collective-permute-start | bytes 393224 | tf_op jit(solution)/shard_map/ppermute | solution.py:25
  54.9 2.6 %scale.2 = (bf16[512,2048]{1,0:T(8,128)(2,1)S(1)}, bf16[512,2048]{1,0:T(8,128)(2,1)S(1)}) custom-call(s32[3]{0:T(128)S(1)} %pad_add_fusion.place.refs_0_, f32[2,2,2,136,128]{4,3,2,1,0:T(8,128)S(1)} %pad_maximum_fusion.refs_1_, f32[2,2,2,136,128]{4,3,2,1,0:T(8,128)S(1)} %collective-permute-done.2.refs_2_.refs_4_, ...), custom_call_target="tpu_custom_call" | custom-call | flops 1000000000 | tf_op jit(solution)/shard_map/scale/pallas_call | solution.py:324
  57.5 2.4 %greens.2 = (f32[128,256]{1,0:T(8,128)S(1)}, f32[128,256]{1,0:T(8,128)S(1)}, f32[128,256]{1,0:T(8,128)S(1)}, f32[128,256]{1,0:T(8,128)S(1)}) custom-call(s32[3]{0:T(128)S(1)} %pad_add_fusion.place.refs_0_, f32[4,4]{1,0:T(4,128)S(1)} %copy-done.2, bf16[512,2048]{1,0:T(8,128)(2,1)S(1)} %get-tuple-element.38.refs_2_, ...), custom_call_target="tpu_custom_call" | custom-call | flops 3000000000 | tf_op jit(solution)/shard_map/greens/pallas_call | solution.py:334
  60.0 3.7 %collective-permute-done.20.refs_2_ = f32[128,256]{1,0:T(8,128)S(1)} collective-permute-done((f32[128,256]{1,0:T(8,128)S(1)}, f32[128,256]{1,0:T(8,128)S(1)}, u32[]{:S(2)}, u32[]{:S(2)}) %collective-permute-start.20) | collective-permute-done | bytes 131104 | tf_op jit(solution)/shard_map/ppermute | solution.py:25
  63.7 0.1 collective-permute-start.22
  63.7 2.0 %collective-permute-start.15 = (f32[128,256]{1,0:T(8,128)S(1)}, f32[128,256]{1,0:T(8,128)S(1)}, u32[]{:S(2)}, u32[]{:S(2)}) collective-permute-start(f32[128,256]{1,0:T(8,128)S(1)} %get-tuple-element.48), channel_id=1, source_target_pairs={{0,8},{8,0},{16,24},{24,16},{1,9},{9,1},{17,25},{25,17},{2,10},{10... | collective-permute-start | bytes 393224 | tf_op jit(solution)/shard_map/ppermute | solution.py:25
  65.8 2.4 %collective-permute-start.17 = (f32[128,256]{1,0:T(8,128)S(1)}, f32[128,256]{1,0:T(8,128)S(1)}, u32[]{:S(2)}, u32[]{:S(2)}) collective-permute-start(f32[128,256]{1,0:T(8,128)S(1)} %get-tuple-element.50), channel_id=1, source_target_pairs={{0,24},{8,16},{16,8},{24,0},{1,25},{9,17},{17,9},{25,1},{2,26},{10... | collective-permute-start | bytes 393224 | tf_op jit(solution)/shard_map/ppermute | solution.py:25
  68.2 1.6 %modes.2 = (f32[512,128]{1,0:T(8,128)S(1)}, f32[512,128]{1,0:T(8,128)S(1)}) custom-call(bf16[2,512,1024]{2,1,0:T(8,128)(2,1)S(1)} %get-tuple-element.33.refs_3_.high, bf16[2,512,1024]{2,1,0:T(8,128)(2,1)S(1)} %get-tuple-element.34.low, f32[4,128,256]{2,1,0:T(8,128)S(1)} %pack.3.refs_0_, f32[4,128,256]{2,1,0:T(8,128)S(1)} %collective-permute-done.22.refs_1_), custom_call_target="tpu_custom_call" | custom-call | tf_op jit(solution)/shard_map/modes/pallas_call | solution.py:384
  69.8 0.5 collective-permute-start.23
  70.3 0.9 %collective-permute-done.15.refs_1_ = f32[128,256]{1,0:T(8,128)S(1)} collective-permute-done((f32[128,256]{1,0:T(8,128)S(1)}, f32[128,256]{1,0:T(8,128)S(1)}, u32[]{:S(2)}, u32[]{:S(2)}) %collective-permute-start.15) | collective-permute-done | bytes 131104 | tf_op jit(solution)/shard_map/ppermute | solution.py:25
  71.3 7.4 %collective-permute-done.16.refs_2_ = f32[128,256]{1,0:T(8,128)S(1)} collective-permute-done((f32[128,256]{1,0:T(8,128)S(1)}, f32[128,256]{1,0:T(8,128)S(1)}, u32[]{:S(2)}, u32[]{:S(2)}) %collective-permute-start.16) | collective-permute-done | bytes 131104 | tf_op jit(solution)/shard_map/ppermute | solution.py:25
  78.7 0.1 collective-permute-start.18
  78.8 1.9 %collective-permute-done.18.refs_1_ = f32[4,128,256]{2,1,0:T(8,128)S(1)} collective-permute-done((f32[4,128,256]{2,1,0:T(8,128)S(1)}, f32[4,128,256]{2,1,0:T(8,128)S(1)}, u32[]{:S(2)}, u32[]{:S(2)}) %collective-permute-start.18) | collective-permute-done | bytes 524320 | tf_op jit(solution)/shard_map/ppermute | solution.py:25
  80.7 1.5 %modes.3 = (f32[512,128]{1,0:T(8,128)S(1)}, f32[512,128]{1,0:T(8,128)S(1)}) custom-call(bf16[2,512,1024]{2,1,0:T(8,128)(2,1)S(1)} %get-tuple-element.33.refs_3_.high, bf16[2,512,1024]{2,1,0:T(8,128)(2,1)S(1)} %get-tuple-element.34.low, f32[4,128,256]{2,1,0:T(8,128)S(1)} %pack.2.refs_0_, f32[4,128,256]{2,1,0:T(8,128)S(1)} %collective-permute-done.18.refs_1_, ...), custom_call_target="tpu_custom_call" | custom-call | tf_op jit(solution)/shard_map/modes/pallas_call | solution.py:384
  82.2 0.5 collective-permute-start.24
  82.7 1.4 %assemble.2.refs_1_ = f32[1,512,512]{2,1,0:T(8,128)} custom-call(s32[3]{0:T(128)S(1)} %pad_add_fusion.place.refs_0_, f32[512,128]{1,0:T(8,128)S(1)} %get-tuple-element.59.refs_0_, f32[512,128]{1,0:T(8,128)S(1)} %collective-permute-done.23._.refs_1_, f32[512,128]{1,0:T(8,128)S(1)} %get-tuple-element.60.refs_2_), custom_call_target="tpu_custom_call" | custom-call | tf_op jit(solution)/shard_map/assemble/pallas_call | solution.py:349
  84.1 6.4 %collective-permute-done.24.refs_0_ = f32[512,128]{1,0:T(8,128)S(1)} collective-permute-done((f32[512,128]{1,0:T(8,128)S(1)}, f32[512,128]{1,0:T(8,128)S(1)}, u32[]{:S(2)}, u32[]{:S(2)}) %collective-permute-start.24) | collective-permute-done | bytes 262176 | tf_op jit(solution)/shard_map/ppermute | solution.py:25
  90.6 1.3 %assemble.3 = f32[1,512,512]{2,1,0:T(8,128)} custom-call(s32[3]{0:T(128)S(1)} %pad_add_fusion.place.refs_0_, f32[512,128]{1,0:T(8,128)S(1)} %collective-permute-done.24.refs_0_, f32[1,512,512]{2,1,0:T(8,128)} %assemble.2.refs_1_), custom_call_target="tpu_custom_call", output_to_operand_aliasing={{}: (2, {})} | custom-call | tf_op jit(solution)/shard_map/assemble/pallas_call | solution.py:349
  (41 shorter events, 0.4 us)
Async XLA Ops:
  0.0 9.5 %copy-start.4 = (f32[512,32]{0,1:T(8,128)S(1)}, f32[512,32]{0,1:T(8,128)}, u32[]{:S(2)}) copy-start(f32[512,32]{0,1:T(8,128)} %param.8) | copy-start | bytes 196612
  0.0 9.7 %copy-start.3 = (f32[512,96]{0,1:T(8,128)S(1)}, f32[512,96]{0,1:T(8,128)}, u32[]{:S(2)}) copy-start(f32[512,96]{0,1:T(8,128)} %param.9) | copy-start | bytes 589828
  0.0 9.8 %copy-start.1 = (f32[1,96]{1,0:T(1,128)S(1)}, f32[1,96]{1,0:T(1,128)}, u32[]{:S(2)}) copy-start(f32[1,96]{1,0:T(1,128)} %emp_energy.1) | copy-start | bytes 1156
  0.0 9.8 %copy-start = (f32[1,32]{1,0:T(1,128)S(1)}, f32[1,32]{1,0:T(1,128)}, u32[]{:S(2)}) copy-start(f32[1,32]{1,0:T(1,128)} %occ_energy.1) | copy-start | bytes 388
  3.2 10.9 %collective-permute-start.6 = (f32[256,128]{1,0:T(8,128)S(1)}, f32[256,128]{1,0:T(8,128)S(1)}, u32[]{:S(2)}, u32[]{:S(2)}) collective-permute-start(f32[256,128]{1,0:T(8,128)S(1)} %get-tuple-element.40), channel_id=1, source_target_pairs={{0,8},{8,0},{16,24},{24,16},{1,9},{9,1},{17,25},{25,17},{2,10},{10... | collective-permute-start | bytes 393224 | tf_op jit(solution)/shard_map/ppermute | solution.py:25
  6.3 19.8 %collective-permute-start.9 = (f32[256,128]{1,0:T(8,128)S(1)}, f32[256,128]{1,0:T(8,128)S(1)}, u32[]{:S(2)}, u32[]{:S(2)}) collective-permute-start(f32[256,128]{1,0:T(8,128)S(1)} %get-tuple-element.43), channel_id=1, source_target_pairs={{0,16},{8,24},{16,0},{24,8},{1,17},{9,25},{17,1},{25,9},{2,18},{10... | collective-permute-start | bytes 393224 | tf_op jit(solution)/shard_map/ppermute | solution.py:25
  8.9 8.9 %collective-permute-start.12 = (f32[256,128]{1,0:T(8,128)S(1)}, f32[256,128]{1,0:T(8,128)S(1)}, u32[]{:S(2)}, u32[]{:S(2)}) collective-permute-start(f32[256,128]{1,0:T(8,128)S(1)} %get-tuple-element.44), channel_id=1, source_target_pairs={{0,24},{8,16},{16,8},{24,0},{1,25},{9,17},{17,9},{25,1},{2,26},{10... | collective-permute-start | bytes 393224 | tf_op jit(solution)/shard_map/ppermute | solution.py:25
  10.6 5.1 %collective-permute-start = (f32[2,136,128]{2,1,0:T(8,128)S(1)}, f32[2,136,128]{2,1,0:T(8,128)S(1)}, u32[]{:S(2)}, u32[]{:S(2)}) collective-permute-start(f32[2,136,128]{2,1,0:T(8,128)S(1)} %get-tuple-element.37), channel_id=1, source_target_pairs={{0,2},{1,3},{2,0},{3,1},{4,6},{5,7},{6,4},{7,5},{8,10},{9,11},{10,... | collective-permute-start | bytes 417800 | tf_op jit(solution)/shard_map/ppermute | solution.py:25
  14.1 9.6 %collective-permute-start.7 = (f32[2,256,128]{2,1,0:T(8,128)S(1)}, f32[2,256,128]{2,1,0:T(8,128)S(1)}, u32[]{:S(2)}, u32[]{:S(2)}) collective-permute-start(f32[2,256,128]{2,1,0:T(8,128)S(1)} %pad_maximum_fusion.5), channel_id=1, source_target_pairs={{0,4},{4,0},{1,5},{5,1},{2,6},{6,2},{3,7},{7,3},{8,12},{12,8},{9,1... | collective-permute-start | bytes 786440 | tf_op jit(solution)/shard_map/ppermute | solution.py:25
  15.8 10.1 %collective-permute-start.1 = (f32[2,2,136,128]{3,2,1,0:T(8,128)S(1)}, f32[2,2,136,128]{3,2,1,0:T(8,128)S(1)}, u32[]{:S(2)}, u32[]{:S(2)}) collective-permute-start(f32[2,2,136,128]{3,2,1,0:T(8,128)S(1)} %get-tuple-element.62), channel_id=1, source_target_pairs={{0,8},{8,0},{16,24},{24,16},{1,9},{9,1},{17,25},{25,17},{2,10},{10... | collective-permute-start | bytes 835592 | tf_op jit(solution)/shard_map/ppermute | solution.py:25
  17.8 18.3 %collective-permute-start.13 = (f32[1,256,128]{2,1,0:T(8,128)S(1)}, f32[1,256,128]{2,1,0:T(8,128)S(1)}, u32[]{:S(2)}, u32[]{:S(2)}) collective-permute-start(f32[1,256,128]{2,1,0:T(8,128)S(1)} %bitcast.26), channel_id=1, source_target_pairs={{0,2},{1,3},{2,0},{3,1},{4,6},{5,7},{6,4},{7,5},{8,10},{9,11},{10,... | collective-permute-start | bytes 393224 | tf_op jit(solution)/shard_map/ppermute | solution.py:25
  19.3 15.8 %collective-permute-start.3 = (f32[2,2,136,128]{3,2,1,0:T(8,128)S(1)}, f32[2,2,136,128]{3,2,1,0:T(8,128)S(1)}, u32[]{:S(2)}, u32[]{:S(2)}) collective-permute-start(f32[2,2,136,128]{3,2,1,0:T(8,128)S(1)} %get-tuple-element.62), channel_id=1, source_target_pairs={{0,16},{8,24},{16,0},{24,8},{1,17},{9,25},{17,1},{25,9},{2,18},{10... | collective-permute-start | bytes 835592 | tf_op jit(solution)/shard_map/ppermute | solution.py:25
  23.8 18.6 %collective-permute-start.8 = (f32[4,256,128]{2,1,0:T(8,128)S(1)}, f32[4,256,128]{2,1,0:T(8,128)S(1)}, u32[]{:S(2)}, u32[]{:S(2)}) collective-permute-start(f32[4,256,128]{2,1,0:T(8,128)S(1)} %pad_maximum_fusion.3.refs_1_), channel_id=1, source_target_pairs={{0,2},{1,3},{2,0},{3,1},{4,6},{5,7},{6,4},{7,5},{8,10},{9,11},{10,... | collective-permute-start | bytes 1572872 | tf_op jit(solution)/shard_map/ppermute | solution.py:25
  25.9 16.5 %collective-permute-start.2 = (f32[2,2,2,136,128]{4,3,2,1,0:T(8,128)S(1)}, f32[2,2,2,136,128]{4,3,2,1,0:T(8,128)S(1)}, u32[]{:S(2)}, u32[]{:S(2)}) collective-permute-start(f32[2,2,2,136,128]{4,3,2,1,0:T(8,128)S(1)} %pad_maximum_fusion.refs_1_), channel_id=1, source_target_pairs={{0,1},{1,0},{2,3},{3,2},{4,5},{5,4},{6,7},{7,6},{8,9},{9,8},{10,11... | collective-permute-start | bytes 1671176 | tf_op jit(solution)/shard_map/ppermute | solution.py:25
  26.1 11.6 %collective-permute-start.10 = (f32[1,256,128]{2,1,0:T(8,128)S(1)}, f32[1,256,128]{2,1,0:T(8,128)S(1)}, u32[]{:S(2)}, u32[]{:S(2)}) collective-permute-start(f32[1,256,128]{2,1,0:T(8,128)S(1)} %bitcast.24), channel_id=1, source_target_pairs={{0,4},{4,0},{1,5},{5,1},{2,6},{6,2},{3,7},{7,3},{8,12},{12,8},{9,1... | collective-permute-start | bytes 393224 | tf_op jit(solution)/shard_map/ppermute | solution.py:25
  35.1 7.2 %collective-permute-start.4 = (f32[2,2,136,128]{3,2,1,0:T(8,128)S(1)}, f32[2,2,136,128]{3,2,1,0:T(8,128)S(1)}, u32[]{:S(2)}, u32[]{:S(2)}) collective-permute-start(f32[2,2,136,128]{3,2,1,0:T(8,128)S(1)} %collective-permute-done.3), channel_id=1, source_target_pairs={{0,8},{8,0},{16,24},{24,16},{1,9},{9,1},{17,25},{25,17},{2,10},{10... | collective-permute-start | bytes 835592 | tf_op jit(solution)/shard_map/ppermute | solution.py:25
  36.1 7.4 %collective-permute-start.14 = (f32[2,256,128]{2,1,0:T(8,128)S(1)}, f32[2,256,128]{2,1,0:T(8,128)S(1)}, u32[]{:S(2)}, u32[]{:S(2)}) collective-permute-start(f32[2,256,128]{2,1,0:T(8,128)S(1)} %pad_maximum_fusion.7.refs_3_), channel_id=1, source_target_pairs={{0,4},{4,0},{1,5},{5,1},{2,6},{6,2},{3,7},{7,3},{8,12},{12,8},{9,1... | collective-permute-start | bytes 786440 | tf_op jit(solution)/shard_map/ppermute | solution.py:25
  37.7 6.6 %collective-permute-start.11 = (f32[2,256,128]{2,1,0:T(8,128)S(1)}, f32[2,256,128]{2,1,0:T(8,128)S(1)}, u32[]{:S(2)}, u32[]{:S(2)}) collective-permute-start(f32[2,256,128]{2,1,0:T(8,128)S(1)} %pad_maximum_fusion.6.refs_1_), channel_id=1, source_target_pairs={{0,2},{1,3},{2,0},{3,1},{4,6},{5,7},{6,4},{7,5},{8,10},{9,11},{10,... | collective-permute-start | bytes 786440 | tf_op jit(solution)/shard_map/ppermute | solution.py:25
  42.3 3.0 %collective-permute-start.5 = (f32[2,2,2,136,128]{4,3,2,1,0:T(8,128)S(1)}, f32[2,2,2,136,128]{4,3,2,1,0:T(8,128)S(1)}, u32[]{:S(2)}, u32[]{:S(2)}) collective-permute-start(f32[2,2,2,136,128]{4,3,2,1,0:T(8,128)S(1)} %pad_maximum_fusion.1.refs_3_), channel_id=1, source_target_pairs={{0,1},{1,0},{2,3},{3,2},{4,5},{5,4},{6,7},{7,6},{8,9},{9,8},{10,11... | collective-permute-start | bytes 1671176 | tf_op jit(solution)/shard_map/ppermute | solution.py:25
  45.3 2.6 %copy-start.2 = (f32[4,4]{1,0:T(4,128)S(1)}, f32[4,4]{1,0:T(4,128)}, u32[]{:S(2)}) copy-start(f32[4,4]{1,0:T(4,128)} %refs_1_.3) | copy-start | bytes 196
  50.4 9.5 %collective-permute-start.19 = (f32[128,256]{1,0:T(8,128)S(1)}, f32[128,256]{1,0:T(8,128)S(1)}, u32[]{:S(2)}, u32[]{:S(2)}) collective-permute-start(f32[128,256]{1,0:T(8,128)S(1)} %get-tuple-element.54), channel_id=1, source_target_pairs={{0,8},{8,0},{16,24},{24,16},{1,9},{9,1},{17,25},{25,17},{2,10},{10... | collective-permute-start | bytes 393224 | tf_op jit(solution)/shard_map/ppermute | solution.py:25
  52.3 11.3 %collective-permute-start.20 = (f32[128,256]{1,0:T(8,128)S(1)}, f32[128,256]{1,0:T(8,128)S(1)}, u32[]{:S(2)}, u32[]{:S(2)}) collective-permute-start(f32[128,256]{1,0:T(8,128)S(1)} %get-tuple-element.55), channel_id=1, source_target_pairs={{0,16},{8,24},{16,0},{24,8},{1,17},{9,25},{17,1},{25,9},{2,18},{10... | collective-permute-start | bytes 393224 | tf_op jit(solution)/shard_map/ppermute | solution.py:25
  52.3 11.3 %collective-permute-start.21 = (f32[128,256]{1,0:T(8,128)S(1)}, f32[128,256]{1,0:T(8,128)S(1)}, u32[]{:S(2)}, u32[]{:S(2)}) collective-permute-start(f32[128,256]{1,0:T(8,128)S(1)} %get-tuple-element.56), channel_id=1, source_target_pairs={{0,24},{8,16},{16,8},{24,0},{1,25},{9,17},{17,9},{25,1},{2,26},{10... | collective-permute-start | bytes 393224 | tf_op jit(solution)/shard_map/ppermute | solution.py:25
  63.7 4.6 %collective-permute-start.22 = (f32[4,128,256]{2,1,0:T(8,128)S(1)}, f32[4,128,256]{2,1,0:T(8,128)S(1)}, u32[]{:S(2)}, u32[]{:S(2)}) collective-permute-start(f32[4,128,256]{2,1,0:T(8,128)S(1)} %pack.3.refs_0_), channel_id=1, source_target_pairs={{0,1},{1,0},{2,3},{3,2},{4,5},{5,4},{6,7},{7,6},{8,9},{9,8},{10,11... | collective-permute-start | bytes 1572872 | tf_op jit(solution)/shard_map/ppermute | solution.py:25
  63.7 7.6 %collective-permute-start.15 = (f32[128,256]{1,0:T(8,128)S(1)}, f32[128,256]{1,0:T(8,128)S(1)}, u32[]{:S(2)}, u32[]{:S(2)}) collective-permute-start(f32[128,256]{1,0:T(8,128)S(1)} %get-tuple-element.48), channel_id=1, source_target_pairs={{0,8},{8,0},{16,24},{24,16},{1,9},{9,1},{17,25},{25,17},{2,10},{10... | collective-permute-start | bytes 393224 | tf_op jit(solution)/shard_map/ppermute | solution.py:25
  65.8 12.9 %collective-permute-start.16 = (f32[128,256]{1,0:T(8,128)S(1)}, f32[128,256]{1,0:T(8,128)S(1)}, u32[]{:S(2)}, u32[]{:S(2)}) collective-permute-start(f32[128,256]{1,0:T(8,128)S(1)} %get-tuple-element.49), channel_id=1, source_target_pairs={{0,16},{8,24},{16,0},{24,8},{1,17},{9,25},{17,1},{25,9},{2,18},{10... | collective-permute-start | bytes 393224 | tf_op jit(solution)/shard_map/ppermute | solution.py:25
  65.8 12.9 %collective-permute-start.17 = (f32[128,256]{1,0:T(8,128)S(1)}, f32[128,256]{1,0:T(8,128)S(1)}, u32[]{:S(2)}, u32[]{:S(2)}) collective-permute-start(f32[128,256]{1,0:T(8,128)S(1)} %get-tuple-element.50), channel_id=1, source_target_pairs={{0,24},{8,16},{16,8},{24,0},{1,25},{9,17},{17,9},{25,1},{2,26},{10... | collective-permute-start | bytes 393224 | tf_op jit(solution)/shard_map/ppermute | solution.py:25
  69.8 9.0 %collective-permute-start.23 = (f32[512,128]{1,0:T(8,128)S(1)}, f32[512,128]{1,0:T(8,128)S(1)}, u32[]{:S(2)}, u32[]{:S(2)}) collective-permute-start(f32[512,128]{1,0:T(8,128)S(1)} %get-tuple-element.57), channel_id=1, source_target_pairs={{0,2},{1,3},{2,0},{3,1},{4,6},{5,7},{6,4},{7,5},{8,10},{9,11},{10,... | collective-permute-start | bytes 786440 | tf_op jit(solution)/shard_map/ppermute | solution.py:25
  78.7 2.0 %collective-permute-start.18 = (f32[4,128,256]{2,1,0:T(8,128)S(1)}, f32[4,128,256]{2,1,0:T(8,128)S(1)}, u32[]{:S(2)}, u32[]{:S(2)}) collective-permute-start(f32[4,128,256]{2,1,0:T(8,128)S(1)} %pack.2.refs_0_), channel_id=1, source_target_pairs={{0,1},{1,0},{2,3},{3,2},{4,5},{5,4},{6,7},{7,6},{8,9},{9,8},{10,11... | collective-permute-start | bytes 1572872 | tf_op jit(solution)/shard_map/ppermute | solution.py:25
  82.2 8.4 %collective-permute-start.24 = (f32[512,128]{1,0:T(8,128)S(1)}, f32[512,128]{1,0:T(8,128)S(1)}, u32[]{:S(2)}, u32[]{:S(2)}) collective-permute-start(f32[512,128]{1,0:T(8,128)S(1)} %get-tuple-element.58), channel_id=1, source_target_pairs={{0,2},{1,3},{2,0},{3,1},{4,6},{5,7},{6,4},{7,5},{8,10},{9,11},{10,... | collective-permute-start | bytes 786440 | tf_op jit(solution)/shard_map/ppermute | solution.py:25

commit v3 on v2

--- a/solution.py
+++ b/solution.py
@@ -10,10 +10,11 @@
 GP = 2048
 f32, bf16 = jnp.float32, jnp.bfloat16
 VMEM_LIMIT = 32 * 1024 * 1024
+VMEM_ALL = 60 * 1024 * 1024
 EXTRA = 8
 CHUNKS = 2
 FINE = 32
-HALVES_COST, SCALE_COST, GREENS_COST, TOKEN_COST, BEHIND = (12, 3), 1, 3, 3.6, 0
+HALVES_COST, SCALE_COST, GREENS_COST, TOKEN_COST, BEHIND, GATE = (12, 8), (0, 0), 3, 3.6, 0, 1
 
 
 def bits_of(size):
@@ -34,49 +35,66 @@
     return lax.dot_general(a, b, (((1,), (0,)), ((), ())), preferred_element_type=f32)
 
 
-def column_kernel(T, place, occ, emp, *outs):
-    piece = outs[0].shape[1]
+def prepare_kernel(T, H, times, *refs):
+    sources, slices, blocks = refs[:6], refs[6 : 6 + T], refs[6 + T : 6 + T + H]
+    here, done = refs[6 + T + H : -1], refs[-1]
+    copies = [pltpu.make_async_copy(a, b, done.at[i]) for i, (a, b) in enumerate(zip(sources, here))]
+    for copy in copies:
+        copy.start()
+    for copy in copies:
+        copy.wait()
+    occ_c, emp_c, occ_r, emp_r, occ_energy, emp_energy = here
+    k, q = lax.axis_index("tm"), lax.axis_index("col")
+    n, piece = occ_c.shape[0], slices[0].shape[1]
     for s in range(T):
-        lines = pl.ds(pl.multiple_of((place[0] ^ s) * piece, piece), piece)
-        outs[s][...] = jnp.concatenate([occ[lines, :].T, emp[lines, :].T], 0)
-
-
-def row_kernel(place, times, occ, emp, occ_energy, emp_energy, _, *outs):
-    chunks, lines, breadth = outs[0].shape
-    occ_n, n = occ.shape[1], lines - EXTRA
-    for d in range(len(outs)):
+        for one in range(T) if piece % 128 else (None,):
+            @pl.when(True if one is None else (k ^ s) == one)
+            def _():
+                first = pl.multiple_of((k ^ s) * piece, piece) if one is None else one * piece
+                slices[s][0:n, :] = occ_c[:, pl.ds(first, piece)]
+                slices[s][n:-EXTRA, :] = emp_c[:, pl.ds(first, piece)]
+        slices[s][-EXTRA:, :] = jnp.full((EXTRA, piece), times[0], f32)
+    chunks, lines, breadth = blocks[0].shape
+    occ_n, n = occ_r.shape[0], lines - EXTRA
+    for d in range(H):
         for c in range(chunks):
-            first = (((place[2] // 2) ^ d) * chunks + c) * breadth
+            first = (((q // 2) ^ d) * chunks + c) * breadth
             at = pl.ds(pl.multiple_of(first, breadth), breadth)
-            outs[d][c, 0:occ_n, :] = occ[at, :].T
-            outs[d][c, occ_n:n, :] = emp[at, :].T
-            outs[d][c, n:, :] = jnp.full((EXTRA, breadth), times[0], f32)
-            outs[d][c, n : n + 1, 0:occ_n] = occ_energy[...]
-            outs[d][c, n : n + 1, occ_n:n] = emp_energy[...]
+            blocks[d][c, 0:occ_n, :] = occ_r[:, at]
+            blocks[d][c, occ_n:n, :] = emp_r[:, at]
+            blocks[d][c, n:, :] = jnp.zeros((EXTRA, breadth), f32)
+            blocks[d][c, n : n + 1, 0:occ_n] = occ_energy[...]
+            blocks[d][c, n : n + 1, occ_n:n] = emp_energy[...]
+
+
+def gate_kernel(waits, *refs):
+    pieces, out = refs[: -1 - waits], refs[-1]
+    for s, piece in enumerate(pieces):
+        out[s] = piece[0 : out.shape[1], :]
 
 
 def scale_kernel(chunk, T, C, counts, *refs):
     occ_r, emp_r = counts
     n = occ_r + emp_r
-    k_occ = occ_r * T * C
-    place, rows = refs[0], refs[1:5]
-    s_high, s_low, flat, falls = refs[5:]
+    place, rows, (s_high, s_low, flat, falls) = refs[0], refs[1:3], refs[-4:]
+    instant, slots = refs[3 : 3 + T], rows[0].shape[0]
+    k_occ = occ_r * slots * C
     q = place[2]
-    breadth, half = flat.shape[1], T // 2
+    breadth = flat.shape[1]
     lane = lax.broadcasted_iota(jnp.int32, (1, breadth), 1)
     instants = jnp.zeros((1, breadth), f32)
-    for s in range(T):
-        instants = jnp.where(lane == s, rows[2 * (s // half)][s % half, 0, 0, n + 1 : n + 2, :], instants)
-    for s in range(T):
+    for t in range(T):
+        instants = jnp.where(lane == t, instant[t][-1:, 0:1], instants)
+    for s in range(slots):
         for core in range(2):
             for d in range(C // 2):
                 at = s * C + (q ^ (2 * d + core))
-                block = rows[2 * (s // half) + core].at[s % half, d]
+                block = rows[core].at[s, d]
                 occ_at = pl.ds(pl.multiple_of(at * occ_r, 8), occ_r)
                 emp_at = pl.ds(pl.multiple_of(k_occ + at * emp_r, 8), emp_r)
                 flat[occ_at, :] = block[chunk, 0:occ_r, :]
                 flat[emp_at, :] = block[chunk, occ_r:n, :]
-                levels = block[0, n : n + EXTRA, :].T[0:n, 0:1]
+                levels = block[chunk, n : n + EXTRA, :].T[0:n, 0:1]
                 decay = jnp.exp(-(levels * instants))
                 falls[occ_at, :] = decay[0:occ_r]
                 falls[emp_at, :] = decay[occ_r:n]
@@ -114,25 +132,21 @@
         low[:, lanes] = dot(b, turn).astype(bf16)
 
 
-def green_kernel(T, k_occ, *refs):
-    place, weights, s_high, s_low = refs[:4]
-    halves, outs = refs[4:-T], refs[-T:]
+def green_kernel(T, groups, k_occ, *refs):
+    place, weights = refs[:2]
+    scaled, halves, outs = refs[2 : 2 + 2 * groups], refs[2 + 2 * groups : -T], refs[-T:]
     k, breadth = place[0], outs[0].shape[0]
-    groups = len(halves) // 2
-
-    def green(first, size):
+
+    def green(lines):
         total = None
         for g in range(groups):
-            share = size // groups
-            lines = slice(first // groups, first // groups + share)
-            lanes = slice(first + g * share, first + (g + 1) * share)
+            a_high, a_low = scaled[2 * g][:, lines], scaled[2 * g + 1][:, lines]
             c_high, c_low = halves[2 * g][lines, :], halves[2 * g + 1][lines, :]
-            a_high, a_low = s_high[:, lanes], s_low[:, lanes]
             term = dot(a_high, c_high) + dot(a_high, c_low) + dot(a_low, c_high)
             total = term if total is None else total + term
         return total
 
-    product = green(0, k_occ) * green(k_occ, s_high.shape[1] - k_occ)
+    product = green(slice(0, k_occ)) * green(slice(k_occ, scaled[0].shape[1]))
     for w in range(T):
         total = weights[k ^ w, k] * product[0:breadth, :]
         for t in range(1, T):
@@ -144,9 +158,9 @@
     out[...] = jnp.zeros_like(out)
 
 
-def pack_kernel(T, *refs):
-    for s in range(T):
-        refs[-1][s] = refs[s][...]
+def pack_kernel(order, *refs):
+    for i, s in enumerate(order):
+        refs[-1][s] = refs[i][...]
 
 
 def cost(us):
@@ -164,10 +178,10 @@
             low[odd, h * FINE : (h + 1) * FINE, :] = b
 
 
-def mode_kernel(T, waits, high, low, *refs):
+def fold_kernel(block, waits, high, low, *refs):
     here, there = refs[:2]
-    outs, both = refs[2 + waits : -1], refs[-1]
-    _, breadth, width = here.shape
+    out, both = refs[2 + waits :]
+    T, breadth, width = here.shape
     step = width // 2 if width >= 256 else width
     groups = width // step
     at = 0
@@ -181,13 +195,17 @@
                 both[odd, at : at + step, 0:breadth] = a
                 both[odd, at : at + step, breadth:] = b
             at += step
-    share = outs[0].shape[0] // 2
-    for block, out in enumerate(outs):
-        lines = slice(block * share, (block + 1) * share)
-        for odd in range(2):
-            twice = dot(high[odd, lines, :], both[odd])
-            once = dot(low[odd, lines, :], both[odd, :, 0:breadth])
-            out[pl.ds(odd, share, stride=2), :] = twice[:, :breadth] + twice[:, breadth:] + once
+    mode_kernel(block, 0, high, low, both, out)
+
+
+def mode_kernel(block, waits, high, low, both, *refs):
+    out = refs[-1]
+    share, breadth = out.shape[0] // 2, out.shape[1]
+    lines = slice(block * share, (block + 1) * share)
+    for odd in range(2):
+        twice = dot(high[odd, lines, :], both[odd])
+        once = dot(low[odd, lines, :], both[odd, :, 0:breadth])
+        out[pl.ds(odd, share, stride=2), :] = twice[:, :breadth] + twice[:, breadth:] + once
 
 
 def place_kernel(first, place, *refs):
@@ -221,50 +239,52 @@
     hbm = pl.BlockSpec(memory_space=pl.ANY)
     params = pltpu.CompilerParams(vmem_limit_bytes=VMEM_LIMIT)
 
-    pieces = pl.pallas_call(
-        functools.partial(column_kernel, T),
-        out_shape=[jax.ShapeDtypeStruct((m, jp), f32)] * T,
-        in_specs=[smem] + [pl.BlockSpec()] * 2,
-        out_specs=[vmem] * T,
-        compiler_params=params,
+    sources = [occ_cols.T, emp_cols.T, occ_rows.T, emp_rows.T, occ_energy, emp_energy]
+    prepared = pl.pallas_call(
+        functools.partial(prepare_kernel, T, H),
+        out_shape=[jax.ShapeDtypeStruct((m + EXTRA, jp), f32)] * T + [jax.ShapeDtypeStruct((CHUNKS, n + EXTRA, rp), f32)] * H,
+        in_specs=[smem] + [hbm] * len(sources),
+        out_specs=[vmem] * (T + H),
+        scratch_shapes=[pltpu.VMEM(a.shape, f32) for a in sources] + [pltpu.SemaphoreType.DMA((len(sources),))],
+        compiler_params=pltpu.CompilerParams(vmem_limit_bytes=VMEM_ALL),
         cost_estimate=cost(0),
-        name="columns",
-    )(place, occ_cols, emp_cols)
+        name="prepare",
+    )(times, *sources)
+    pieces, row_pieces = prepared[:T], prepared[T:]
     col_slots = [pieces[0]] + [swap(pieces[s], "tm", s) for s in range(1, T)]
-
-    row_pieces = pl.pallas_call(
-        row_kernel,
-        out_shape=[jax.ShapeDtypeStruct((CHUNKS, n + EXTRA, rp), f32)] * H,
-        in_specs=[smem, smem] + [pl.BlockSpec()] * 4 + [hbm],
-        out_specs=[vmem] * H,
-        compiler_params=params,
-        cost_estimate=cost(0),
-        name="rows",
-    )(place, times, occ_rows, emp_rows, occ_energy, emp_energy, pieces[0])
     own_rows = jnp.stack([row_pieces[0]] + [swap(row_pieces[d], "col", 2 * d) for d in range(1, H)])
     got_rows = {0: own_rows}
     for bit in bits_of(T):
         for s in list(got_rows):
             got_rows[s ^ bit] = swap(got_rows[s], "tm", bit)
-    row_slots = []
-    for first in range(0, T, T // 2):
-        mine = jnp.stack([got_rows[s] for s in range(first, first + T // 2)])
-        row_slots += [mine, swap(mine, "col", 1)]
+    early_rows = jnp.stack([got_rows[s] for s in range(T // 2)])
+    row_slots = [[early_rows, swap(early_rows, "col", 1)]]
 
     groups = [list(range(T))[: T // 2], list(range(T))[T // 2 :]]
     cuts = [[groups[0]], [groups[1][: T // 4], groups[1][T // 4 :]]]
     orders = [[row_bits + high_bits], [row_bits + high_bits, high_bits + row_bits]]
-    cols, slots = [], []
+    cols, slots, firsts = [], [], []
     for group, parts, ways in zip(groups, cuts, orders):
         there, where = [], []
         for part, order in zip(parts, ways):
-            values = [(jnp.stack([col_slots[s] for s in part]), [(0, 0, group.index(s)) for s in part])]
+            waits = firsts[:1] if GATE and group is groups[1] else []
+            value = pl.pallas_call(
+                functools.partial(gate_kernel, len(waits)),
+                out_shape=jax.ShapeDtypeStruct((len(part), m, jp), f32),
+                in_specs=[vmem] * len(part) + [hbm] * len(waits),
+                out_specs=vmem,
+                compiler_params=params,
+                cost_estimate=cost(0),
+                name="gate",
+            )(*[col_slots[s] for s in part], *waits)
+            values = [(value, [(0, 0, group.index(s)) for s in part])]
             for axis, bit in order:
                 if len(values) > 1:
                     values = [(jnp.concatenate([v for v, _ in values], 0), sum((w for _, w in values), []))]
                 value, at = values[0]
                 far = [(dx ^ bit, dq, f) if axis == "row" else (dx, dq ^ bit, f) for dx, dq, f in at]
                 values.append((swap(value, axis, bit), far))
+                firsts.append(values[-1][0])
             there += [v for v, _ in values]
             where += [w for _, w in values]
         cols.append(there)
@@ -304,7 +324,7 @@
         name="cosines",
     )(near, far)
 
-    halves, waits = [], [t_high, row_slots[1]]
+    halves, waits = [], [t_high]
     for g, group in enumerate(groups):
         got = pl.pallas_call(
             functools.partial(halves_kernel, slots[g], C, X, (occ_c, emp_c), len(waits)),
@@ -319,22 +339,36 @@
         halves += got
         waits = [got[0]]
 
-    own = []
+    own, instants = [], [slot[-EXTRA:] for slot in col_slots]
     for chunk in range(CHUNKS):
-        scaled = pl.pallas_call(
-            functools.partial(scale_kernel, chunk, T, C, (occ_r, emp_r)),
-            out_shape=[jax.ShapeDtypeStruct((T * rp, k_occ + k_emp), bf16)] * 2,
-            in_specs=[smem] + [pl.BlockSpec()] * len(row_slots),
-            out_specs=[vmem] * 2,
-            scratch_shapes=[pltpu.VMEM((k_occ + k_emp, rp), f32)] * 2,
-            compiler_params=params,
-            cost_estimate=cost(SCALE_COST),
-            name="scale",
-        )(place, *row_slots)
+        scaled = []
+        for g in range(len(groups)):
+            if len(row_slots) == g:
+                late_rows = pl.pallas_call(
+                    functools.partial(pack_kernel, range(T // 2)),
+                    out_shape=jax.ShapeDtypeStruct(early_rows.shape, f32),
+                    in_specs=[vmem] * (T // 2) + [hbm] * 2,
+                    out_specs=vmem,
+                    compiler_params=params,
+                    cost_estimate=cost(0),
+                    name="pack",
+                )(*[got_rows[s] for s in groups[g]], scaled[0], halves[0])
+                row_slots.append([late_rows, swap(late_rows, "col", 1)])
+            k_group = (k_occ + k_emp) // len(groups)
+            scaled += pl.pallas_call(
+                functools.partial(scale_kernel, chunk, T, C, (occ_r, emp_r)),
+                out_shape=[jax.ShapeDtypeStruct((T * rp, k_group), bf16)] * 2,
+                in_specs=[smem] + [pl.BlockSpec()] * 2 + [vmem] * T + [hbm] * len(own),
+                out_specs=[vmem] * 2,
+                scratch_shapes=[pltpu.VMEM((k_group, rp), f32)] * 2,
+                compiler_params=params,
+                cost_estimate=cost(SCALE_COST[g]),
+                name="scale",
+            )(place, *row_slots[g], *instants, *[here[0] for here in own])
         series = pl.pallas_call(
-            functools.partial(green_kernel, T, k_occ),
+            functools.partial(green_kernel, T, len(groups), k_occ // len(groups)),
             out_shape=[jax.ShapeDtypeStruct((rp, wide), f32)] * T,
-            in_specs=[smem, smem] + [vmem] * (2 + len(halves)),
+            in_specs=[smem, smem] + [vmem] * (len(scaled) + len(halves)),
             out_specs=[vmem] * T,
             compiler_params=params,
             cost_estimate=cost(GREENS_COST),
@@ -362,7 +396,7 @@
     for chunk in range(CHUNKS):
         behind = [own[chunk + 1][BEHIND]] if chunk + 1 < CHUNKS else []
         mine = pl.pallas_call(
-            functools.partial(pack_kernel, T),
+            functools.partial(pack_kernel, range(T)),
             out_shape=jax.ShapeDtypeStruct((T, rp, wide), f32),
             in_specs=[vmem] * T + [hbm] * len(behind),
             out_specs=vmem,
@@ -381,16 +415,29 @@
             )(part)
             for _, part in late
         ]
+        shape = jax.ShapeDtypeStruct((share, rp), f32)
         made = pl.pallas_call(
-            functools.partial(mode_kernel, T, len(waits)),
-            out_shape=[jax.ShapeDtypeStruct((share, rp), f32)] * H,
+            functools.partial(fold_kernel, 0, len(waits)),
+            out_shape=[shape, jax.ShapeDtypeStruct((2, all_cols, 2 * rp), bf16)],
             in_specs=[vmem] * 4 + [hbm] * len(waits),
-            out_specs=[vmem] * H,
-            scratch_shapes=[pltpu.VMEM((2, all_cols, 2 * rp), bf16)],
+            out_specs=[vmem] * 2,
             compiler_params=params,
             cost_estimate=cost(0),
             name="modes",
         )(t_high, t_low, mine, swap(mine, "col", 1), *waits)
+        made, both = [made[0]], made[1]
+        for block in range(1, H):
+            made.append(
+                pl.pallas_call(
+                    functools.partial(mode_kernel, block, 0),
+                    out_shape=shape,
+                    in_specs=[vmem] * 3,
+                    out_specs=vmem,
+                    compiler_params=params,
+                    cost_estimate=cost(0),
+                    name="modes",
+                )(t_high, t_low, both)
+            )
         early = early + late + [((chunk, 0), made[H - 1])]
         late = [((chunk, d), swap(made[H - 1 - d], "col", 2 * d)) for d in range(1, H)]
     return assemble(late, [assemble(early, [])])

time: 92.2 us -> 89.2 us (0.967)
  waiting for transfers between devices: 35 us -> 32.4 us
  Pallas kernels: 20.5 us -> 22.7 us
  starting transfers between devices: 30.4 us -> 28.9 us
    ppermute x25, waiting for transfers between devices: 35 us -> 32.4 us  [swap(): return lax.ppermute(value, axis, [(i, i ^ bit) for i in range(size)])]
    unnamed x14 -> x6, local copies, waits for them, and re-layouts: 2.53 us -> 0.91 us
    ppermute x25, starting transfers between devices: 30.4 us -> 28.9 us  [swap(): return lax.ppermute(value, axis, [(i, i ^ bit) for i in range(size)])]
    pallas_call x2 -> x4, Pallas kernels: 5.2 us -> 6.54 us  [per_device(): pl.pallas_call(functools.partial(scale_kernel, chunk, T, C, (occ_r, emp_r...]
    pallas_call x8 -> x13, Pallas kernels: 9.58 us -> 10.5 us  [the longest x2 4.89 us: per_device(): pl.pallas_call(functools.partial(green_kernel, T, len(groups), k_occ // l...]
  transfers between devices with their start and end apart: 25 -> 25, of which waited for: 11 -> 12; matrix products, arithmetic and copies ran while one was open for 3% -> 3% of each run, Pallas kernels for 13% -> 16%
where the time goes in v3:
time: 89.2 us; the launch traced here: 89.1 us
  waiting for transfers between devices  32.4 us (36%)
  starting transfers between devices  28.9 us (32%)
  Pallas kernels  22.7 us (25%)
  other arithmetic  2.04 us (2%)
  local copies, waits for them, and re-layouts  1.79 us (2%)
  between operations  1.21 us (1%)
    ppermute x25, waiting for transfers between devices, swap(): return lax.ppermute(value, axis, [(i, i ^ bit) for i in range(size)])  32.4 us
    ppermute x25, starting transfers between devices, swap(): return lax.ppermute(value, axis, [(i, i ^ bit) for i in range(size)])  28.9 us
    pallas_call x4, Pallas kernels, per_device(): pl.pallas_call(functools.partial(scale_kernel, chunk, T, C, (occ_r, emp_r...  6.54 us
    pallas_call x2, Pallas kernels, per_device(): pl.pallas_call(functools.partial(green_kernel, T, len(groups), k_occ // l...  4.89 us
    pallas_call x2, Pallas kernels, assemble(): pl.pallas_call(functools.partial(place_kernel, [at for at, _ in parts]),...  2.71 us
    pallas_call x1, Pallas kernels, per_device(): pl.pallas_call(functools.partial(prepare_kernel, T, H), out_shape=[jax.Sh...  2.09 us
    pallas_call x2, Pallas kernels, per_device(): pl.pallas_call(functools.partial(halves_kernel, slots[g], C, X, (occ_c, e...  2.07 us
    pallas_call x2, Pallas kernels, per_device(): pl.pallas_call(functools.partial(fold_kernel, 0, len(waits)), out_shape=[...  1.9 us
  transfers between devices with their start and end apart: 25, of which 12 were waited for; matrix products, arithmetic and copies ran while one was open for 3% of the time, Pallas kernels for 16%

profile of v3, /device:TPU:0, one launch (start us, length us, event | category | flops | bytes accessed | tf_op | source)
XLA Modules:
  0.0 89.1 jit_solution(11438304467124206842)
XLA Ops:
  0.7 2.1 %prepare.1 = (f32[264,128]{1,0:T(8,128)}, f32[264,128]{1,0:T(8,128)}, f32[264,128]{1,0:T(8,128)}, f32[264,128]{1,0:T(8,128)}, f32[2,136,128]{2,1,0:T(8,128)}, /*index=5*/f32[2,136,128]{2,1,0:T(8,128)}) custom-call(f32[1]{0:T(128)S(6)} %copy.11.times, f32[64,512]{1,0:T(8,128)} %bitcast.18, f32[192,512]{1,0:T(8,128)} %bitcast.13, f32[32,512]{1,0:T(8,128)} %bitcast.19, ...), custom_call_target="tpu_custom_call" | custom-call | tf_op jit(solution)/shard_map/prepare/pallas_call | solution.py:243
  2.8 0.0 copy-start.2
  2.8 3.1 %collective-permute-start.3 = (f32[264,128]{1,0:T(8,128)}, f32[264,128]{1,0:T(8,128)S(1)}, u32[]{:S(2)}, u32[]{:S(2)}) collective-permute-start(f32[264,128]{1,0:T(8,128)} %get-tuple-element.42), channel_id=1, source_target_pairs={{0,8},{8,0},{16,24},{24,16},{1,9},{9,1},{17,25},{25,17},{2,10},{10... | collective-permute-start | bytes 405512 | tf_op jit(solution)/shard_map/ppermute | solution.py:26
  5.9 2.6 %collective-permute-start.4 = (f32[264,128]{1,0:T(8,128)}, f32[264,128]{1,0:T(8,128)S(1)}, u32[]{:S(2)}, u32[]{:S(2)}) collective-permute-start(f32[264,128]{1,0:T(8,128)} %get-tuple-element.43), channel_id=1, source_target_pairs={{0,16},{8,24},{16,0},{24,8},{1,17},{9,25},{17,1},{25,9},{2,18},{10... | collective-permute-start | bytes 405512 | tf_op jit(solution)/shard_map/ppermute | solution.py:26
  8.4 1.7 %collective-permute-start = (f32[2,136,128]{2,1,0:T(8,128)}, f32[2,136,128]{2,1,0:T(8,128)S(1)}, u32[]{:S(2)}, u32[]{:S(2)}) collective-permute-start(f32[2,136,128]{2,1,0:T(8,128)} %get-tuple-element.40), channel_id=1, source_target_pairs={{0,2},{1,3},{2,0},{3,1},{4,6},{5,7},{6,4},{7,5},{8,10},{9,11},{10,... | collective-permute-start | bytes 417800 | tf_op jit(solution)/shard_map/ppermute | solution.py:26
  10.2 0.1 rev.3
  10.3 0.1 broadcast_add_fusion.1
  10.4 0.1 add.145
  10.5 0.1 iota_select_fusion
  10.6 0.1 broadcast_add_fusion
  10.6 0.1 multiply_add_fusion
  10.7 1.1 %cosine_multiply_fusion.1 = (f32[1,32,1024]{2,1,0:T(8,128)S(1)}, f32[1,32,1024]{2,1,0:T(8,128)S(1)}, f32[1,32,1024]{2,1,0:T(8,128)S(1)}, f32[1,32,1024]{2,1,0:T(8,128)S(1)}) fusion(s32[32]{0:T(128)S(1)} %get-tuple-element.81, s32[1024]{0:T(1024)S(1)} %bitcast.20, s32[32]{0:T(128)S(1)} %get-tuple-element.82), kind=kLoop, calls=%fused_computation.26 | loop fusion | flops 1048576 | bytes 528640 | tf_op jit(solution)/shard_map/mul | solution.py:314
  11.9 0.9 %copy-done = f32[264,128]{1,0:T(8,128)S(1)} copy-done((f32[264,128]{1,0:T(8,128)S(1)}, f32[264,128]{1,0:T(8,128)}, u32[]{:S(2)}) %copy-start) | copy-done | bytes 135192
  12.8 1.6 %collective-permute-start.8 = (f32[2,256,128]{2,1,0:T(8,128)S(1)}, f32[2,256,128]{2,1,0:T(8,128)S(1)}, u32[]{:S(2)}, u32[]{:S(2)}) collective-permute-start(f32[2,256,128]{2,1,0:T(8,128)S(1)} %gate.3), channel_id=1, source_target_pairs={{0,4},{4,0},{1,5},{5,1},{2,6},{6,2},{3,7},{7,3},{8,12},{12,8},{9,1... | collective-permute-start | bytes 786440 | tf_op jit(solution)/shard_map/ppermute | solution.py:26
  14.3 0.3 fusion.10
  14.8 0.7 collective-permute-start.1
  15.5 3.5 %collective-permute-start.6 = (f32[2,2,136,128]{3,2,1,0:T(8,128)S(1)}, f32[2,2,136,128]{3,2,1,0:T(8,128)S(1)}, u32[]{:S(2)}, u32[]{:S(2)}) collective-permute-start(f32[2,2,136,128]{3,2,1,0:T(8,128)S(1)} %get-tuple-element.70), channel_id=1, source_target_pairs={{0,16},{8,24},{16,0},{24,8},{1,17},{9,25},{17,1},{25,9},{2,18},{10... | collective-permute-start | bytes 835592 | tf_op jit(solution)/shard_map/ppermute | solution.py:26
  19.0 0.8 collective-permute-done.8.refs_1_
  19.9 0.6 collective-permute-start.9
  20.6 1.5 %collective-permute-start.13 = (f32[1,256,128]{2,1,0:T(8,128)S(1)}, f32[1,256,128]{2,1,0:T(8,128)S(1)}, u32[]{:S(2)}, u32[]{:S(2)}) collective-permute-start(f32[1,256,128]{2,1,0:T(8,128)S(1)} %gate.5), channel_id=1, source_target_pairs={{0,2},{1,3},{2,0},{3,1},{4,6},{5,7},{6,4},{7,5},{8,10},{9,11},{10,... | collective-permute-start | bytes 393224 | tf_op jit(solution)/shard_map/ppermute | solution.py:26
  22.1 0.1 pad_add_fusion.refs_0_.place
  22.1 0.7 slice.12.refs_3_
  22.8 0.9 %cosines.1 = (bf16[2,512,1024]{2,1,0:T(8,128)(2,1)S(1)}, bf16[2,512,1024]{2,1,0:T(8,128)(2,1)S(1)}) custom-call(f32[4,32,1024]{2,1,0:T(8,128)S(1)} %pad_maximum_fusion.1.near, f32[2,16,1024]{2,1,0:T(8,128)S(1)} %pad_maximum_fusion.6.far), custom_call_target="tpu_custom_call" | custom-call | tf_op jit(solution)/shard_map/cosines/pallas_call | solution.py:317
  23.8 1.6 %collective-permute-start.11 = (f32[1,256,128]{2,1,0:T(8,128)S(1)}, f32[1,256,128]{2,1,0:T(8,128)S(1)}, u32[]{:S(2)}, u32[]{:S(2)}) collective-permute-start(f32[1,256,128]{2,1,0:T(8,128)S(1)} %gate.4), channel_id=1, source_target_pairs={{0,4},{4,0},{1,5},{5,1},{2,6},{6,2},{3,7},{7,3},{8,12},{12,8},{9,1... | collective-permute-start | bytes 393224 | tf_op jit(solution)/shard_map/ppermute | solution.py:26
  25.4 2.1 %collective-permute-done.1 = f32[2,2,136,128]{3,2,1,0:T(8,128)S(1)} collective-permute-done((f32[2,2,136,128]{3,2,1,0:T(8,128)S(1)}, f32[2,2,136,128]{3,2,1,0:T(8,128)S(1)}, u32[]{:S(2)}, u32[]{:S(2)}) %collective-permute-start.1) | collective-permute-done | bytes 278560 | tf_op jit(solution)/shard_map/ppermute | solution.py:26
  27.5 0.1 collective-permute-start.2
  27.6 5.1 %collective-permute-done.6.refs_0_ = f32[2,2,136,128]{3,2,1,0:T(8,128)S(1)} collective-permute-done((f32[2,2,136,128]{3,2,1,0:T(8,128)S(1)}, f32[2,2,136,128]{3,2,1,0:T(8,128)S(1)}, u32[]{:S(2)}, u32[]{:S(2)}) %collective-permute-start.6) | collective-permute-done | bytes 278560 | tf_op jit(solution)/shard_map/ppermute | solution.py:26
  32.7 1.7 %collective-permute-done.13 = f32[1,256,128]{2,1,0:T(8,128)S(1)} collective-permute-done((f32[1,256,128]{2,1,0:T(8,128)S(1)}, f32[1,256,128]{2,1,0:T(8,128)S(1)}, u32[]{:S(2)}, u32[]{:S(2)}) %collective-permute-start.13) | collective-permute-done | bytes 131104 | tf_op jit(solution)/shard_map/ppermute | solution.py:26
  34.4 1.6 %collective-permute-start.14 = (f32[2,256,128]{2,1,0:T(8,128)S(1)}, f32[2,256,128]{2,1,0:T(8,128)S(1)}, u32[]{:S(2)}, u32[]{:S(2)}) collective-permute-start(f32[2,256,128]{2,1,0:T(8,128)S(1)} %pad_maximum_fusion.5.refs_3_), channel_id=1, source_target_pairs={{0,4},{4,0},{1,5},{5,1},{2,6},{6,2},{3,7},{7,3},{8,12},{12,8},{9,1... | collective-permute-start | bytes 786440 | tf_op jit(solution)/shard_map/ppermute | solution.py:26
  36.0 0.4 collective-permute-start.12
  36.4 1.0 %halves.2 = (bf16[1024,256]{1,0:T(8,128)(2,1)S(1)}, bf16[1024,256]{1,0:T(8,128)(2,1)S(1)}) custom-call(s32[3]{0:T(128)S(1)} %pad_add_fusion.refs_0_.place, f32[4,256,128]{2,1,0:T(8,128)S(1)} %pad_maximum_fusion.2.refs_1_, f32[4,256,128]{2,1,0:T(8,128)S(1)} %collective-permute-done.9.refs_2_, bf16[2,512,1024]{2,1,0:T(8,128)(2,1)S(1)} %get-tuple-element.37.refs_3_.high), custom_call_target="tpu_custom_call" | custom-call | flops 12000000000 | tf_op jit(solution)/shard_map/halves/pallas_call | solution.py:329
  37.4 1.6 %scale.4 = (bf16[512,1024]{1,0:T(8,128)(2,1)S(1)}, bf16[512,1024]{1,0:T(8,128)(2,1)S(1)}) custom-call(s32[3]{0:T(128)S(1)} %pad_add_fusion.refs_0_.place, f32[2,2,2,136,128]{4,3,2,1,0:T(8,128)S(1)} %pad_maximum_fusion.refs_1_, f32[2,2,2,136,128]{4,3,2,1,0:T(8,128)S(1)} %collective-permute-done.2.refs_2_, f32[8,128]{1,0:T(8,128)S(1)} %slice.12.refs_3_, ...), custom_call_target="tpu_custom_call" | custom-call | tf_op jit(solution)/shard_map/scale/pallas_call | solution.py:358
  39.0 0.9 %collective-permute-done.7.refs_1_ = f32[2,2,136,128]{3,2,1,0:T(8,128)S(1)} collective-permute-done((f32[2,2,136,128]{3,2,1,0:T(8,128)S(1)}, f32[2,2,136,128]{3,2,1,0:T(8,128)S(1)}, u32[]{:S(2)}, u32[]{:S(2)}) %collective-permute-start.7) | collective-permute-done | bytes 278560 | tf_op jit(solution)/shard_map/ppermute | solution.py:26
  40.0 0.0 copy-start.1
  40.0 0.1 collective-permute-start.10
  40.1 0.8 collective-permute-done.14.refs_4_
  40.9 1.6 %collective-permute-done.12.refs_2_ = f32[2,256,128]{2,1,0:T(8,128)S(1)} collective-permute-done((f32[2,256,128]{2,1,0:T(8,128)S(1)}, f32[2,256,128]{2,1,0:T(8,128)S(1)}, u32[]{:S(2)}, u32[]{:S(2)}) %collective-permute-start.12) | collective-permute-done | bytes 262176 | tf_op jit(solution)/shard_map/ppermute | solution.py:26
  42.5 1.0 %halves.3 = (bf16[1024,256]{1,0:T(8,128)(2,1)S(1)}, bf16[1024,256]{1,0:T(8,128)(2,1)S(1)}) custom-call(s32[3]{0:T(128)S(1)} %pad_add_fusion.refs_0_.place, f32[2,256,128]{2,1,0:T(8,128)S(1)} %pad_maximum_fusion.4.refs_1_, f32[2,256,128]{2,1,0:T(8,128)S(1)} %collective-permute-done.12.refs_2_, f32[2,256,128]{2,1,0:T(8,128)S(1)} %pad_maximum_fusion.5.refs_3_, ...), custom_call_target="tpu_custom_call" | custom-call | flops 8000000000 | tf_op jit(solution)/shard_map/halves/pallas_call | solution.py:329
  43.5 1.7 %scale.5 = (bf16[512,1024]{1,0:T(8,128)(2,1)S(1)}, bf16[512,1024]{1,0:T(8,128)(2,1)S(1)}) custom-call(s32[3]{0:T(128)S(1)} %pad_add_fusion.refs_0_.place, f32[2,2,2,136,128]{4,3,2,1,0:T(8,128)S(1)} %pack.3.refs_1_, f32[2,2,2,136,128]{4,3,2,1,0:T(8,128)S(1)} %collective-permute-done.10.refs_2_, f32[8,128]{1,0:T(8,128)S(1)} %slice.12.refs_3_, ...), custom_call_target="tpu_custom_call" | custom-call | tf_op jit(solution)/shard_map/scale/pallas_call | solution.py:358
  45.2 2.4 %greens.2 = (f32[128,256]{1,0:T(8,128)S(1)}, f32[128,256]{1,0:T(8,128)S(1)}, f32[128,256]{1,0:T(8,128)S(1)}, f32[128,256]{1,0:T(8,128)S(1)}) custom-call(s32[3]{0:T(128)S(1)} %pad_add_fusion.refs_0_.place, f32[4,4]{1,0:T(4,128)S(1)} %copy-done.1, bf16[512,1024]{1,0:T(8,128)(2,1)S(1)} %get-tuple-element.45.refs_2_, ...), custom_call_target="tpu_custom_call" | custom-call | flops 3000000000 | tf_op jit(solution)/shard_map/greens/pallas_call | solution.py:368
  47.6 0.6 collective-permute-start.19
  48.3 3.5 %collective-permute-start.20 = (f32[128,256]{1,0:T(8,128)S(1)}, f32[128,256]{1,0:T(8,128)S(1)}, u32[]{:S(2)}, u32[]{:S(2)}) collective-permute-start(f32[128,256]{1,0:T(8,128)S(1)} %get-tuple-element.63), channel_id=1, source_target_pairs={{0,16},{8,24},{16,0},{24,8},{1,17},{9,25},{17,1},{25,9},{2,18},{10... | collective-permute-start | bytes 393224 | tf_op jit(solution)/shard_map/ppermute | solution.py:26
  51.7 0.3 collective-permute-start.21
  52.1 1.6 %scale.7 = (bf16[512,1024]{1,0:T(8,128)(2,1)S(1)}, bf16[512,1024]{1,0:T(8,128)(2,1)S(1)}) custom-call(s32[3]{0:T(128)S(1)} %pad_add_fusion.refs_0_.place, f32[2,2,2,136,128]{4,3,2,1,0:T(8,128)S(1)} %pack.3.refs_1_, f32[2,2,2,136,128]{4,3,2,1,0:T(8,128)S(1)} %collective-permute-done.10.refs_2_, f32[8,128]{1,0:T(8,128)S(1)} %slice.12.refs_3_, ...), custom_call_target="tpu_custom_call" | custom-call | tf_op jit(solution)/shard_map/scale/pallas_call | solution.py:358
  53.8 1.7 %scale.6 = (bf16[512,1024]{1,0:T(8,128)(2,1)S(1)}, bf16[512,1024]{1,0:T(8,128)(2,1)S(1)}) custom-call(s32[3]{0:T(128)S(1)} %pad_add_fusion.refs_0_.place, f32[2,2,2,136,128]{4,3,2,1,0:T(8,128)S(1)} %pad_maximum_fusion.refs_1_, f32[2,2,2,136,128]{4,3,2,1,0:T(8,128)S(1)} %collective-permute-done.2.refs_2_, f32[8,128]{1,0:T(8,128)S(1)} %slice.12.refs_3_, ...), custom_call_target="tpu_custom_call" | custom-call | tf_op jit(solution)/shard_map/scale/pallas_call | solution.py:358
  55.4 2.5 %greens.3 = (f32[128,256]{1,0:T(8,128)S(1)}, f32[128,256]{1,0:T(8,128)S(1)}, f32[128,256]{1,0:T(8,128)S(1)}, f32[128,256]{1,0:T(8,128)S(1)}) custom-call(s32[3]{0:T(128)S(1)} %pad_add_fusion.refs_0_.place, f32[4,4]{1,0:T(4,128)S(1)} %copy-done.1, bf16[512,1024]{1,0:T(8,128)(2,1)S(1)} %get-tuple-element.54.refs_2_, ...), custom_call_target="tpu_custom_call" | custom-call | flops 3000000000 | tf_op jit(solution)/shard_map/greens/pallas_call | solution.py:368
  57.9 3.4 %collective-permute-done.20.refs_2_ = f32[128,256]{1,0:T(8,128)S(1)} collective-permute-done((f32[128,256]{1,0:T(8,128)S(1)}, f32[128,256]{1,0:T(8,128)S(1)}, u32[]{:S(2)}, u32[]{:S(2)}) %collective-permute-start.20) | collective-permute-done | bytes 131104 | tf_op jit(solution)/shard_map/ppermute | solution.py:26
  61.3 0.1 collective-permute-start.22
  61.4 2.0 %collective-permute-start.15 = (f32[128,256]{1,0:T(8,128)S(1)}, f32[128,256]{1,0:T(8,128)S(1)}, u32[]{:S(2)}, u32[]{:S(2)}) collective-permute-start(f32[128,256]{1,0:T(8,128)S(1)} %get-tuple-element.59), channel_id=1, source_target_pairs={{0,8},{8,0},{16,24},{24,16},{1,9},{9,1},{17,25},{25,17},{2,10},{10... | collective-permute-start | bytes 393224 | tf_op jit(solution)/shard_map/ppermute | solution.py:26
  63.4 1.1 %collective-permute-start.16 = (f32[128,256]{1,0:T(8,128)S(1)}, f32[128,256]{1,0:T(8,128)S(1)}, u32[]{:S(2)}, u32[]{:S(2)}) collective-permute-start(f32[128,256]{1,0:T(8,128)S(1)} %get-tuple-element.60), channel_id=1, source_target_pairs={{0,16},{8,24},{16,0},{24,8},{1,17},{9,25},{17,1},{25,9},{2,18},{10... | collective-permute-start | bytes 393224 | tf_op jit(solution)/shard_map/ppermute | solution.py:26
  64.5 1.4 %collective-permute-start.17 = (f32[128,256]{1,0:T(8,128)S(1)}, f32[128,256]{1,0:T(8,128)S(1)}, u32[]{:S(2)}, u32[]{:S(2)}) collective-permute-start(f32[128,256]{1,0:T(8,128)S(1)} %get-tuple-element.61), channel_id=1, source_target_pairs={{0,24},{8,16},{16,8},{24,0},{1,25},{9,17},{17,9},{25,1},{2,26},{10... | collective-permute-start | bytes 393224 | tf_op jit(solution)/shard_map/ppermute | solution.py:26
  65.9 1.1 %modes.4 = (f32[512,128]{1,0:T(8,128)S(1)}, bf16[2,1024,256]{2,1,0:T(8,128)(2,1)S(1)}) custom-call(bf16[2,512,1024]{2,1,0:T(8,128)(2,1)S(1)} %get-tuple-element.37.refs_3_.high, bf16[2,512,1024]{2,1,0:T(8,128)(2,1)S(1)} %get-tuple-element.38.low, f32[4,128,256]{2,1,0:T(8,128)S(1)} %pack.5.refs_0_, f32[4,128,256]{2,1,0:T(8,128)S(1)} %collective-permute-done.22.refs_1_), custom_call_target="tpu_custom_call" | custom-call | tf_op jit(solution)/shard_map/modes/pallas_call | solution.py:419
  67.0 0.4 collective-permute-start.23
  67.4 2.3 %collective-permute-done.15.refs_1_ = f32[128,256]{1,0:T(8,128)S(1)} collective-permute-done((f32[128,256]{1,0:T(8,128)S(1)}, f32[128,256]{1,0:T(8,128)S(1)}, u32[]{:S(2)}, u32[]{:S(2)}) %collective-permute-start.15) | collective-permute-done | bytes 131104 | tf_op jit(solution)/shard_map/ppermute | solution.py:26
  69.7 6.6 %collective-permute-done.16.refs_2_ = f32[128,256]{1,0:T(8,128)S(1)} collective-permute-done((f32[128,256]{1,0:T(8,128)S(1)}, f32[128,256]{1,0:T(8,128)S(1)}, u32[]{:S(2)}, u32[]{:S(2)}) %collective-permute-start.16) | collective-permute-done | bytes 131104 | tf_op jit(solution)/shard_map/ppermute | solution.py:26
  76.4 0.1 collective-permute-start.18
  76.5 1.9 %collective-permute-done.18.refs_1_ = f32[4,128,256]{2,1,0:T(8,128)S(1)} collective-permute-done((f32[4,128,256]{2,1,0:T(8,128)S(1)}, f32[4,128,256]{2,1,0:T(8,128)S(1)}, u32[]{:S(2)}, u32[]{:S(2)}) %collective-permute-start.18) | collective-permute-done | bytes 524320 | tf_op jit(solution)/shard_map/ppermute | solution.py:26
  78.4 0.8 modes.5
  79.2 0.4 collective-permute-start.24
  79.7 0.7 modes.6.refs_0_
  80.4 0.7 modes.7.refs_2_
  81.1 1.5 %assemble.2.refs_1_ = f32[1,512,512]{2,1,0:T(8,128)} custom-call(s32[3]{0:T(128)S(1)} %pad_add_fusion.refs_0_.place, f32[512,128]{1,0:T(8,128)S(1)} %modes.6.refs_0_, f32[512,128]{1,0:T(8,128)S(1)} %collective-permute-done.23._.refs_1_, f32[512,128]{1,0:T(8,128)S(1)} %modes.7.refs_2_), custom_call_target="tpu_custom_call" | custom-call | tf_op jit(solution)/shard_map/assemble/pallas_call | solution.py:383
  82.6 5.1 %collective-permute-done.24.refs_0_ = f32[512,128]{1,0:T(8,128)S(1)} collective-permute-done((f32[512,128]{1,0:T(8,128)S(1)}, f32[512,128]{1,0:T(8,128)S(1)}, u32[]{:S(2)}, u32[]{:S(2)}) %collective-permute-start.24) | collective-permute-done | bytes 262176 | tf_op jit(solution)/shard_map/ppermute | solution.py:26
  87.6 1.3 %assemble.3 = f32[1,512,512]{2,1,0:T(8,128)} custom-call(s32[3]{0:T(128)S(1)} %pad_add_fusion.refs_0_.place, f32[512,128]{1,0:T(8,128)S(1)} %collective-permute-done.24.refs_0_, f32[1,512,512]{2,1,0:T(8,128)} %assemble.2.refs_1_), custom_call_target="tpu_custom_call", output_to_operand_aliasing={{}: (2, {})} | custom-call | tf_op jit(solution)/shard_map/assemble/pallas_call | solution.py:383
  (42 shorter events, 0.4 us)
Async XLA Ops:
  2.8 12.0 %copy-start.2 = (f32[2,136,128]{2,1,0:T(8,128)S(1)}, f32[2,136,128]{2,1,0:T(8,128)}, u32[]{:S(2)}) copy-start(f32[2,136,128]{2,1,0:T(8,128)} %get-tuple-element.39) | copy-start | bytes 417796
  2.8 9.1 %collective-permute-start.3 = (f32[264,128]{1,0:T(8,128)}, f32[264,128]{1,0:T(8,128)S(1)}, u32[]{:S(2)}, u32[]{:S(2)}) collective-permute-start(f32[264,128]{1,0:T(8,128)} %get-tuple-element.42), channel_id=1, source_target_pairs={{0,8},{8,0},{16,24},{24,16},{1,9},{9,1},{17,25},{25,17},{2,10},{10... | collective-permute-start | bytes 405512 | tf_op jit(solution)/shard_map/ppermute | solution.py:26
  5.9 17.9 %collective-permute-start.4 = (f32[264,128]{1,0:T(8,128)}, f32[264,128]{1,0:T(8,128)S(1)}, u32[]{:S(2)}, u32[]{:S(2)}) collective-permute-start(f32[264,128]{1,0:T(8,128)} %get-tuple-element.43), channel_id=1, source_target_pairs={{0,16},{8,24},{16,0},{24,8},{1,17},{9,25},{17,1},{25,9},{2,18},{10... | collective-permute-start | bytes 405512 | tf_op jit(solution)/shard_map/ppermute | solution.py:26
  8.4 12.1 %collective-permute-start.5 = (f32[264,128]{1,0:T(8,128)}, f32[264,128]{1,0:T(8,128)S(1)}, u32[]{:S(2)}, u32[]{:S(2)}) collective-permute-start(f32[264,128]{1,0:T(8,128)} %get-tuple-element.44), channel_id=1, source_target_pairs={{0,24},{8,16},{16,8},{24,0},{1,25},{9,17},{17,9},{25,1},{2,26},{10... | collective-permute-start | bytes 405512 | tf_op jit(solution)/shard_map/ppermute | solution.py:26
  8.4 6.3 %collective-permute-start = (f32[2,136,128]{2,1,0:T(8,128)}, f32[2,136,128]{2,1,0:T(8,128)S(1)}, u32[]{:S(2)}, u32[]{:S(2)}) collective-permute-start(f32[2,136,128]{2,1,0:T(8,128)} %get-tuple-element.40), channel_id=1, source_target_pairs={{0,2},{1,3},{2,0},{3,1},{4,6},{5,7},{6,4},{7,5},{8,10},{9,11},{10,... | collective-permute-start | bytes 417800 | tf_op jit(solution)/shard_map/ppermute | solution.py:26
  11.8 0.9 %copy-start = (f32[264,128]{1,0:T(8,128)S(1)}, f32[264,128]{1,0:T(8,128)}, u32[]{:S(2)}) copy-start(f32[264,128]{1,0:T(8,128)} %get-tuple-element.41.refs_0_) | copy-start | bytes 405508
  12.8 7.1 %collective-permute-start.8 = (f32[2,256,128]{2,1,0:T(8,128)S(1)}, f32[2,256,128]{2,1,0:T(8,128)S(1)}, u32[]{:S(2)}, u32[]{:S(2)}) collective-permute-start(f32[2,256,128]{2,1,0:T(8,128)S(1)} %gate.3), channel_id=1, source_target_pairs={{0,4},{4,0},{1,5},{5,1},{2,6},{6,2},{3,7},{7,3},{8,12},{12,8},{9,1... | collective-permute-start | bytes 786440 | tf_op jit(solution)/shard_map/ppermute | solution.py:26
  14.8 12.7 %collective-permute-start.1 = (f32[2,2,136,128]{3,2,1,0:T(8,128)S(1)}, f32[2,2,136,128]{3,2,1,0:T(8,128)S(1)}, u32[]{:S(2)}, u32[]{:S(2)}) collective-permute-start(f32[2,2,136,128]{3,2,1,0:T(8,128)S(1)} %get-tuple-element.70), channel_id=1, source_target_pairs={{0,8},{8,0},{16,24},{24,16},{1,9},{9,1},{17,25},{25,17},{2,10},{10... | collective-permute-start | bytes 835592 | tf_op jit(solution)/shard_map/ppermute | solution.py:26
  15.5 17.2 %collective-permute-start.6 = (f32[2,2,136,128]{3,2,1,0:T(8,128)S(1)}, f32[2,2,136,128]{3,2,1,0:T(8,128)S(1)}, u32[]{:S(2)}, u32[]{:S(2)}) collective-permute-start(f32[2,2,136,128]{3,2,1,0:T(8,128)S(1)} %get-tuple-element.70), channel_id=1, source_target_pairs={{0,16},{8,24},{16,0},{24,8},{1,17},{9,25},{17,1},{25,9},{2,18},{10... | collective-permute-start | bytes 835592 | tf_op jit(solution)/shard_map/ppermute | solution.py:26
  19.9 16.5 %collective-permute-start.9 = (f32[4,256,128]{2,1,0:T(8,128)S(1)}, f32[4,256,128]{2,1,0:T(8,128)S(1)}, u32[]{:S(2)}, u32[]{:S(2)}) collective-permute-start(f32[4,256,128]{2,1,0:T(8,128)S(1)} %pad_maximum_fusion.2.refs_1_), channel_id=1, source_target_pairs={{0,2},{1,3},{2,0},{3,1},{4,6},{5,7},{6,4},{7,5},{8,10},{9,11},{10,... | collective-permute-start | bytes 1572872 | tf_op jit(solution)/shard_map/ppermute | solution.py:26
  20.6 13.9 %collective-permute-start.13 = (f32[1,256,128]{2,1,0:T(8,128)S(1)}, f32[1,256,128]{2,1,0:T(8,128)S(1)}, u32[]{:S(2)}, u32[]{:S(2)}) collective-permute-start(f32[1,256,128]{2,1,0:T(8,128)S(1)} %gate.5), channel_id=1, source_target_pairs={{0,2},{1,3},{2,0},{3,1},{4,6},{5,7},{6,4},{7,5},{8,10},{9,11},{10,... | collective-permute-start | bytes 393224 | tf_op jit(solution)/shard_map/ppermute | solution.py:26
  23.8 12.2 %collective-permute-start.11 = (f32[1,256,128]{2,1,0:T(8,128)S(1)}, f32[1,256,128]{2,1,0:T(8,128)S(1)}, u32[]{:S(2)}, u32[]{:S(2)}) collective-permute-start(f32[1,256,128]{2,1,0:T(8,128)S(1)} %gate.4), channel_id=1, source_target_pairs={{0,4},{4,0},{1,5},{5,1},{2,6},{6,2},{3,7},{7,3},{8,12},{12,8},{9,1... | collective-permute-start | bytes 393224 | tf_op jit(solution)/shard_map/ppermute | solution.py:26
  27.5 9.9 %collective-permute-start.2 = (f32[2,2,2,136,128]{4,3,2,1,0:T(8,128)S(1)}, f32[2,2,2,136,128]{4,3,2,1,0:T(8,128)S(1)}, u32[]{:S(2)}, u32[]{:S(2)}) collective-permute-start(f32[2,2,2,136,128]{4,3,2,1,0:T(8,128)S(1)} %pad_maximum_fusion.refs_1_), channel_id=1, source_target_pairs={{0,1},{1,0},{2,3},{3,2},{4,5},{5,4},{6,7},{7,6},{8,9},{9,8},{10,11... | collective-permute-start | bytes 1671176 | tf_op jit(solution)/shard_map/ppermute | solution.py:26
  32.7 7.3 %collective-permute-start.7 = (f32[2,2,136,128]{3,2,1,0:T(8,128)S(1)}, f32[2,2,136,128]{3,2,1,0:T(8,128)S(1)}, u32[]{:S(2)}, u32[]{:S(2)}) collective-permute-start(f32[2,2,136,128]{3,2,1,0:T(8,128)S(1)} %collective-permute-done.6.refs_0_), channel_id=1, source_target_pairs={{0,8},{8,0},{16,24},{24,16},{1,9},{9,1},{17,25},{25,17},{2,10},{10... | collective-permute-start | bytes 835592 | tf_op jit(solution)/shard_map/ppermute | solution.py:26
  34.4 6.4 %collective-permute-start.14 = (f32[2,256,128]{2,1,0:T(8,128)S(1)}, f32[2,256,128]{2,1,0:T(8,128)S(1)}, u32[]{:S(2)}, u32[]{:S(2)}) collective-permute-start(f32[2,256,128]{2,1,0:T(8,128)S(1)} %pad_maximum_fusion.5.refs_3_), channel_id=1, source_target_pairs={{0,4},{4,0},{1,5},{5,1},{2,6},{6,2},{3,7},{7,3},{8,12},{12,8},{9,1... | collective-permute-start | bytes 786440 | tf_op jit(solution)/shard_map/ppermute | solution.py:26
  36.0 6.4 %collective-permute-start.12 = (f32[2,256,128]{2,1,0:T(8,128)S(1)}, f32[2,256,128]{2,1,0:T(8,128)S(1)}, u32[]{:S(2)}, u32[]{:S(2)}) collective-permute-start(f32[2,256,128]{2,1,0:T(8,128)S(1)} %pad_maximum_fusion.4.refs_1_), channel_id=1, source_target_pairs={{0,2},{1,3},{2,0},{3,1},{4,6},{5,7},{6,4},{7,5},{8,10},{9,11},{10,... | collective-permute-start | bytes 786440 | tf_op jit(solution)/shard_map/ppermute | solution.py:26
  40.0 5.2 %copy-start.1 = (f32[4,4]{1,0:T(4,128)S(1)}, f32[4,4]{1,0:T(4,128)}, u32[]{:S(2)}) copy-start(f32[4,4]{1,0:T(4,128)} %refs_1_.3) | copy-start | bytes 196
  40.0 3.5 %collective-permute-start.10 = (f32[2,2,2,136,128]{4,3,2,1,0:T(8,128)S(1)}, f32[2,2,2,136,128]{4,3,2,1,0:T(8,128)S(1)}, u32[]{:S(2)}, u32[]{:S(2)}) collective-permute-start(f32[2,2,2,136,128]{4,3,2,1,0:T(8,128)S(1)} %pack.3.refs_1_), channel_id=1, source_target_pairs={{0,1},{1,0},{2,3},{3,2},{4,5},{5,4},{6,7},{7,6},{8,9},{9,8},{10,11... | collective-permute-start | bytes 1671176 | tf_op jit(solution)/shard_map/ppermute | solution.py:26
  47.6 10.2 %collective-permute-start.19 = (f32[128,256]{1,0:T(8,128)S(1)}, f32[128,256]{1,0:T(8,128)S(1)}, u32[]{:S(2)}, u32[]{:S(2)}) collective-permute-start(f32[128,256]{1,0:T(8,128)S(1)} %get-tuple-element.62), channel_id=1, source_target_pairs={{0,8},{8,0},{16,24},{24,16},{1,9},{9,1},{17,25},{25,17},{2,10},{10... | collective-permute-start | bytes 393224 | tf_op jit(solution)/shard_map/ppermute | solution.py:26
  48.3 13.0 %collective-permute-start.20 = (f32[128,256]{1,0:T(8,128)S(1)}, f32[128,256]{1,0:T(8,128)S(1)}, u32[]{:S(2)}, u32[]{:S(2)}) collective-permute-start(f32[128,256]{1,0:T(8,128)S(1)} %get-tuple-element.63), channel_id=1, source_target_pairs={{0,16},{8,24},{16,0},{24,8},{1,17},{9,25},{17,1},{25,9},{2,18},{10... | collective-permute-start | bytes 393224 | tf_op jit(solution)/shard_map/ppermute | solution.py:26
  51.7 9.5 %collective-permute-start.21 = (f32[128,256]{1,0:T(8,128)S(1)}, f32[128,256]{1,0:T(8,128)S(1)}, u32[]{:S(2)}, u32[]{:S(2)}) collective-permute-start(f32[128,256]{1,0:T(8,128)S(1)} %get-tuple-element.64), channel_id=1, source_target_pairs={{0,24},{8,16},{16,8},{24,0},{1,25},{9,17},{17,9},{25,1},{2,26},{10... | collective-permute-start | bytes 393224 | tf_op jit(solution)/shard_map/ppermute | solution.py:26
  61.3 4.6 %collective-permute-start.22 = (f32[4,128,256]{2,1,0:T(8,128)S(1)}, f32[4,128,256]{2,1,0:T(8,128)S(1)}, u32[]{:S(2)}, u32[]{:S(2)}) collective-permute-start(f32[4,128,256]{2,1,0:T(8,128)S(1)} %pack.5.refs_0_), channel_id=1, source_target_pairs={{0,1},{1,0},{2,3},{3,2},{4,5},{5,4},{6,7},{7,6},{8,9},{9,8},{10,11... | collective-permute-start | bytes 1572872 | tf_op jit(solution)/shard_map/ppermute | solution.py:26
  61.4 8.3 %collective-permute-start.15 = (f32[128,256]{1,0:T(8,128)S(1)}, f32[128,256]{1,0:T(8,128)S(1)}, u32[]{:S(2)}, u32[]{:S(2)}) collective-permute-start(f32[128,256]{1,0:T(8,128)S(1)} %get-tuple-element.59), channel_id=1, source_target_pairs={{0,8},{8,0},{16,24},{24,16},{1,9},{9,1},{17,25},{25,17},{2,10},{10... | collective-permute-start | bytes 393224 | tf_op jit(solution)/shard_map/ppermute | solution.py:26
  63.4 12.9 %collective-permute-start.16 = (f32[128,256]{1,0:T(8,128)S(1)}, f32[128,256]{1,0:T(8,128)S(1)}, u32[]{:S(2)}, u32[]{:S(2)}) collective-permute-start(f32[128,256]{1,0:T(8,128)S(1)} %get-tuple-element.60), channel_id=1, source_target_pairs={{0,16},{8,24},{16,0},{24,8},{1,17},{9,25},{17,1},{25,9},{2,18},{10... | collective-permute-start | bytes 393224 | tf_op jit(solution)/shard_map/ppermute | solution.py:26
  64.5 11.9 %collective-permute-start.17 = (f32[128,256]{1,0:T(8,128)S(1)}, f32[128,256]{1,0:T(8,128)S(1)}, u32[]{:S(2)}, u32[]{:S(2)}) collective-permute-start(f32[128,256]{1,0:T(8,128)S(1)} %get-tuple-element.61), channel_id=1, source_target_pairs={{0,24},{8,16},{16,8},{24,0},{1,25},{9,17},{17,9},{25,1},{2,26},{10... | collective-permute-start | bytes 393224 | tf_op jit(solution)/shard_map/ppermute | solution.py:26
  67.0 9.5 %collective-permute-start.23 = (f32[512,128]{1,0:T(8,128)S(1)}, f32[512,128]{1,0:T(8,128)S(1)}, u32[]{:S(2)}, u32[]{:S(2)}) collective-permute-start(f32[512,128]{1,0:T(8,128)S(1)} %get-tuple-element.65), channel_id=1, source_target_pairs={{0,2},{1,3},{2,0},{3,1},{4,6},{5,7},{6,4},{7,5},{8,10},{9,11},{10,... | collective-permute-start | bytes 786440 | tf_op jit(solution)/shard_map/ppermute | solution.py:26
  76.4 2.0 %collective-permute-start.18 = (f32[4,128,256]{2,1,0:T(8,128)S(1)}, f32[4,128,256]{2,1,0:T(8,128)S(1)}, u32[]{:S(2)}, u32[]{:S(2)}) collective-permute-start(f32[4,128,256]{2,1,0:T(8,128)S(1)} %pack.4.refs_0_), channel_id=1, source_target_pairs={{0,1},{1,0},{2,3},{3,2},{4,5},{5,4},{6,7},{7,6},{8,9},{9,8},{10,11... | collective-permute-start | bytes 1572872 | tf_op jit(solution)/shard_map/ppermute | solution.py:26
  79.2 8.4 %collective-permute-start.24 = (f32[512,128]{1,0:T(8,128)S(1)}, f32[512,128]{1,0:T(8,128)S(1)}, u32[]{:S(2)}, u32[]{:S(2)}) collective-permute-start(f32[512,128]{1,0:T(8,128)S(1)} %get-tuple-element.66), channel_id=1, source_target_pairs={{0,2},{1,3},{2,0},{3,1},{4,6},{5,7},{6,4},{7,5},{8,10},{9,11},{10,... | collective-permute-start | bytes 786440 | tf_op jit(solution)/shard_map/ppermute | solution.py:26

commit v4 on v3

--- a/solution.py
+++ b/solution.py
@@ -178,12 +178,11 @@
             low[odd, h * FINE : (h + 1) * FINE, :] = b
 
 
-def fold_kernel(block, waits, high, low, *refs):
+def fold_kernel(block, groups, waits, high, low, *refs):
     here, there = refs[:2]
     out, both = refs[2 + waits :]
     T, breadth, width = here.shape
-    step = width // 2 if width >= 256 else width
-    groups = width // step
+    step = width // groups
     at = 0
     for s in range(T):
         for d in range(groups):
@@ -417,7 +416,7 @@
         ]
         shape = jax.ShapeDtypeStruct((share, rp), f32)
         made = pl.pallas_call(
-            functools.partial(fold_kernel, 0, len(waits)),
+            functools.partial(fold_kernel, 0, H, len(waits)),
             out_shape=[shape, jax.ShapeDtypeStruct((2, all_cols, 2 * rp), bf16)],
             in_specs=[vmem] * 4 + [hbm] * len(waits),
             out_specs=[vmem] * 2,

time: 89.2 us -> 89.2 us (level)
  no operation moved by 1% of the time
where the time goes in v4:
time: 89.2 us; the launch traced here: 89.1 us
  waiting for transfers between devices  32.4 us (36%)
  starting transfers between devices  28.9 us (32%)
  Pallas kernels  22.7 us (25%)
  other arithmetic  2.04 us (2%)
  local copies, waits for them, and re-layouts  1.79 us (2%)
  between operations  1.21 us (1%)
    ppermute x25, waiting for transfers between devices, swap(): return lax.ppermute(value, axis, [(i, i ^ bit) for i in range(size)])  32.4 us
    ppermute x25, starting transfers between devices, swap(): return lax.ppermute(value, axis, [(i, i ^ bit) for i in range(size)])  28.9 us
    pallas_call x4, Pallas kernels, per_device(): pl.pallas_call(functools.partial(scale_kernel, chunk, T, C, (occ_r, emp_r...  6.54 us
    pallas_call x2, Pallas kernels, per_device(): pl.pallas_call(functools.partial(green_kernel, T, len(groups), k_occ // l...  4.89 us
    pallas_call x2, Pallas kernels, assemble(): pl.pallas_call(functools.partial(place_kernel, [at for at, _ in parts]),...  2.71 us
    pallas_call x1, Pallas kernels, per_device(): pl.pallas_call(functools.partial(prepare_kernel, T, H), out_shape=[jax.Sh...  2.09 us
    pallas_call x2, Pallas kernels, per_device(): pl.pallas_call(functools.partial(halves_kernel, slots[g], C, X, (occ_c, e...  2.07 us
    pallas_call x2, Pallas kernels, per_device(): pl.pallas_call(functools.partial(fold_kernel, 0, H, len(waits)), out_shap...  1.9 us
  transfers between devices with their start and end apart: 25, of which 12 were waited for; matrix products, arithmetic and copies ran while one was open for 3% of the time, Pallas kernels for 16%

profile of v4, /device:TPU:0, one launch (start us, length us, event | category | flops | bytes accessed | tf_op | source)
XLA Modules:
  0.0 89.1 jit_solution(11438304467124206842)
XLA Ops:
  0.7 2.1 %prepare.1 = (f32[264,128]{1,0:T(8,128)}, f32[264,128]{1,0:T(8,128)}, f32[264,128]{1,0:T(8,128)}, f32[264,128]{1,0:T(8,128)}, f32[2,136,128]{2,1,0:T(8,128)}, /*index=5*/f32[2,136,128]{2,1,0:T(8,128)}) custom-call(f32[1]{0:T(128)S(6)} %copy.11.times, f32[64,512]{1,0:T(8,128)} %bitcast.18, f32[192,512]{1,0:T(8,128)} %bitcast.13, f32[32,512]{1,0:T(8,128)} %bitcast.19, ...), custom_call_target="tpu_custom_call" | custom-call | tf_op jit(solution)/shard_map/prepare/pallas_call | solution.py:242
  2.8 0.0 copy-start.2
  2.8 3.1 %collective-permute-start.3 = (f32[264,128]{1,0:T(8,128)}, f32[264,128]{1,0:T(8,128)S(1)}, u32[]{:S(2)}, u32[]{:S(2)}) collective-permute-start(f32[264,128]{1,0:T(8,128)} %get-tuple-element.42), channel_id=1, source_target_pairs={{0,8},{8,0},{16,24},{24,16},{1,9},{9,1},{17,25},{25,17},{2,10},{10... | collective-permute-start | bytes 405512 | tf_op jit(solution)/shard_map/ppermute | solution.py:26
  5.9 2.6 %collective-permute-start.4 = (f32[264,128]{1,0:T(8,128)}, f32[264,128]{1,0:T(8,128)S(1)}, u32[]{:S(2)}, u32[]{:S(2)}) collective-permute-start(f32[264,128]{1,0:T(8,128)} %get-tuple-element.43), channel_id=1, source_target_pairs={{0,16},{8,24},{16,0},{24,8},{1,17},{9,25},{17,1},{25,9},{2,18},{10... | collective-permute-start | bytes 405512 | tf_op jit(solution)/shard_map/ppermute | solution.py:26
  8.4 1.7 %collective-permute-start = (f32[2,136,128]{2,1,0:T(8,128)}, f32[2,136,128]{2,1,0:T(8,128)S(1)}, u32[]{:S(2)}, u32[]{:S(2)}) collective-permute-start(f32[2,136,128]{2,1,0:T(8,128)} %get-tuple-element.40), channel_id=1, source_target_pairs={{0,2},{1,3},{2,0},{3,1},{4,6},{5,7},{6,4},{7,5},{8,10},{9,11},{10,... | collective-permute-start | bytes 417800 | tf_op jit(solution)/shard_map/ppermute | solution.py:26
  10.2 0.1 rev.3
  10.3 0.1 broadcast_add_fusion.1
  10.4 0.1 add.145
  10.5 0.1 iota_select_fusion
  10.6 0.1 broadcast_add_fusion
  10.6 0.1 multiply_add_fusion
  10.7 1.1 %cosine_multiply_fusion.1 = (f32[1,32,1024]{2,1,0:T(8,128)S(1)}, f32[1,32,1024]{2,1,0:T(8,128)S(1)}, f32[1,32,1024]{2,1,0:T(8,128)S(1)}, f32[1,32,1024]{2,1,0:T(8,128)S(1)}) fusion(s32[32]{0:T(128)S(1)} %get-tuple-element.81, s32[1024]{0:T(1024)S(1)} %bitcast.20, s32[32]{0:T(128)S(1)} %get-tuple-element.82), kind=kLoop, calls=%fused_computation.26 | loop fusion | flops 1048576 | bytes 528640 | tf_op jit(solution)/shard_map/mul | solution.py:313
  11.9 0.9 %copy-done = f32[264,128]{1,0:T(8,128)S(1)} copy-done((f32[264,128]{1,0:T(8,128)S(1)}, f32[264,128]{1,0:T(8,128)}, u32[]{:S(2)}) %copy-start) | copy-done | bytes 135192
  12.8 1.6 %collective-permute-start.8 = (f32[2,256,128]{2,1,0:T(8,128)S(1)}, f32[2,256,128]{2,1,0:T(8,128)S(1)}, u32[]{:S(2)}, u32[]{:S(2)}) collective-permute-start(f32[2,256,128]{2,1,0:T(8,128)S(1)} %gate.3), channel_id=1, source_target_pairs={{0,4},{4,0},{1,5},{5,1},{2,6},{6,2},{3,7},{7,3},{8,12},{12,8},{9,1... | collective-permute-start | bytes 786440 | tf_op jit(solution)/shard_map/ppermute | solution.py:26
  14.3 0.3 fusion.10
  14.8 0.7 collective-permute-start.1
  15.5 3.5 %collective-permute-start.6 = (f32[2,2,136,128]{3,2,1,0:T(8,128)S(1)}, f32[2,2,136,128]{3,2,1,0:T(8,128)S(1)}, u32[]{:S(2)}, u32[]{:S(2)}) collective-permute-start(f32[2,2,136,128]{3,2,1,0:T(8,128)S(1)} %get-tuple-element.70), channel_id=1, source_target_pairs={{0,16},{8,24},{16,0},{24,8},{1,17},{9,25},{17,1},{25,9},{2,18},{10... | collective-permute-start | bytes 835592 | tf_op jit(solution)/shard_map/ppermute | solution.py:26
  19.0 0.8 collective-permute-done.8.refs_1_
  19.9 0.6 collective-permute-start.9
  20.6 1.5 %collective-permute-start.13 = (f32[1,256,128]{2,1,0:T(8,128)S(1)}, f32[1,256,128]{2,1,0:T(8,128)S(1)}, u32[]{:S(2)}, u32[]{:S(2)}) collective-permute-start(f32[1,256,128]{2,1,0:T(8,128)S(1)} %gate.5), channel_id=1, source_target_pairs={{0,2},{1,3},{2,0},{3,1},{4,6},{5,7},{6,4},{7,5},{8,10},{9,11},{10,... | collective-permute-start | bytes 393224 | tf_op jit(solution)/shard_map/ppermute | solution.py:26
  22.1 0.1 pad_add_fusion.refs_0_.place
  22.1 0.7 slice.12.refs_3_
  22.8 0.9 %cosines.1 = (bf16[2,512,1024]{2,1,0:T(8,128)(2,1)S(1)}, bf16[2,512,1024]{2,1,0:T(8,128)(2,1)S(1)}) custom-call(f32[4,32,1024]{2,1,0:T(8,128)S(1)} %pad_maximum_fusion.1.near, f32[2,16,1024]{2,1,0:T(8,128)S(1)} %pad_maximum_fusion.6.far), custom_call_target="tpu_custom_call" | custom-call | tf_op jit(solution)/shard_map/cosines/pallas_call | solution.py:316
  23.8 1.6 %collective-permute-start.11 = (f32[1,256,128]{2,1,0:T(8,128)S(1)}, f32[1,256,128]{2,1,0:T(8,128)S(1)}, u32[]{:S(2)}, u32[]{:S(2)}) collective-permute-start(f32[1,256,128]{2,1,0:T(8,128)S(1)} %gate.4), channel_id=1, source_target_pairs={{0,4},{4,0},{1,5},{5,1},{2,6},{6,2},{3,7},{7,3},{8,12},{12,8},{9,1... | collective-permute-start | bytes 393224 | tf_op jit(solution)/shard_map/ppermute | solution.py:26
  25.4 2.1 %collective-permute-done.1 = f32[2,2,136,128]{3,2,1,0:T(8,128)S(1)} collective-permute-done((f32[2,2,136,128]{3,2,1,0:T(8,128)S(1)}, f32[2,2,136,128]{3,2,1,0:T(8,128)S(1)}, u32[]{:S(2)}, u32[]{:S(2)}) %collective-permute-start.1) | collective-permute-done | bytes 278560 | tf_op jit(solution)/shard_map/ppermute | solution.py:26
  27.5 0.1 collective-permute-start.2
  27.6 5.1 %collective-permute-done.6.refs_0_ = f32[2,2,136,128]{3,2,1,0:T(8,128)S(1)} collective-permute-done((f32[2,2,136,128]{3,2,1,0:T(8,128)S(1)}, f32[2,2,136,128]{3,2,1,0:T(8,128)S(1)}, u32[]{:S(2)}, u32[]{:S(2)}) %collective-permute-start.6) | collective-permute-done | bytes 278560 | tf_op jit(solution)/shard_map/ppermute | solution.py:26
  32.7 1.7 %collective-permute-done.13 = f32[1,256,128]{2,1,0:T(8,128)S(1)} collective-permute-done((f32[1,256,128]{2,1,0:T(8,128)S(1)}, f32[1,256,128]{2,1,0:T(8,128)S(1)}, u32[]{:S(2)}, u32[]{:S(2)}) %collective-permute-start.13) | collective-permute-done | bytes 131104 | tf_op jit(solution)/shard_map/ppermute | solution.py:26
  34.4 1.6 %collective-permute-start.14 = (f32[2,256,128]{2,1,0:T(8,128)S(1)}, f32[2,256,128]{2,1,0:T(8,128)S(1)}, u32[]{:S(2)}, u32[]{:S(2)}) collective-permute-start(f32[2,256,128]{2,1,0:T(8,128)S(1)} %pad_maximum_fusion.5.refs_3_), channel_id=1, source_target_pairs={{0,4},{4,0},{1,5},{5,1},{2,6},{6,2},{3,7},{7,3},{8,12},{12,8},{9,1... | collective-permute-start | bytes 786440 | tf_op jit(solution)/shard_map/ppermute | solution.py:26
  36.0 0.4 collective-permute-start.12
  36.4 1.0 %halves.2 = (bf16[1024,256]{1,0:T(8,128)(2,1)S(1)}, bf16[1024,256]{1,0:T(8,128)(2,1)S(1)}) custom-call(s32[3]{0:T(128)S(1)} %pad_add_fusion.refs_0_.place, f32[4,256,128]{2,1,0:T(8,128)S(1)} %pad_maximum_fusion.2.refs_1_, f32[4,256,128]{2,1,0:T(8,128)S(1)} %collective-permute-done.9.refs_2_, bf16[2,512,1024]{2,1,0:T(8,128)(2,1)S(1)} %get-tuple-element.37.refs_3_.high), custom_call_target="tpu_custom_call" | custom-call | flops 12000000000 | tf_op jit(solution)/shard_map/halves/pallas_call | solution.py:328
  37.4 1.6 %scale.4 = (bf16[512,1024]{1,0:T(8,128)(2,1)S(1)}, bf16[512,1024]{1,0:T(8,128)(2,1)S(1)}) custom-call(s32[3]{0:T(128)S(1)} %pad_add_fusion.refs_0_.place, f32[2,2,2,136,128]{4,3,2,1,0:T(8,128)S(1)} %pad_maximum_fusion.refs_1_, f32[2,2,2,136,128]{4,3,2,1,0:T(8,128)S(1)} %collective-permute-done.2.refs_2_, f32[8,128]{1,0:T(8,128)S(1)} %slice.12.refs_3_, ...), custom_call_target="tpu_custom_call" | custom-call | tf_op jit(solution)/shard_map/scale/pallas_call | solution.py:357
  39.0 0.9 %collective-permute-done.7.refs_1_ = f32[2,2,136,128]{3,2,1,0:T(8,128)S(1)} collective-permute-done((f32[2,2,136,128]{3,2,1,0:T(8,128)S(1)}, f32[2,2,136,128]{3,2,1,0:T(8,128)S(1)}, u32[]{:S(2)}, u32[]{:S(2)}) %collective-permute-start.7) | collective-permute-done | bytes 278560 | tf_op jit(solution)/shard_map/ppermute | solution.py:26
  40.0 0.0 copy-start.1
  40.0 0.1 collective-permute-start.10
  40.1 0.8 collective-permute-done.14.refs_4_
  40.9 1.6 %collective-permute-done.12.refs_2_ = f32[2,256,128]{2,1,0:T(8,128)S(1)} collective-permute-done((f32[2,256,128]{2,1,0:T(8,128)S(1)}, f32[2,256,128]{2,1,0:T(8,128)S(1)}, u32[]{:S(2)}, u32[]{:S(2)}) %collective-permute-start.12) | collective-permute-done | bytes 262176 | tf_op jit(solution)/shard_map/ppermute | solution.py:26
  42.5 1.0 %halves.3 = (bf16[1024,256]{1,0:T(8,128)(2,1)S(1)}, bf16[1024,256]{1,0:T(8,128)(2,1)S(1)}) custom-call(s32[3]{0:T(128)S(1)} %pad_add_fusion.refs_0_.place, f32[2,256,128]{2,1,0:T(8,128)S(1)} %pad_maximum_fusion.4.refs_1_, f32[2,256,128]{2,1,0:T(8,128)S(1)} %collective-permute-done.12.refs_2_, f32[2,256,128]{2,1,0:T(8,128)S(1)} %pad_maximum_fusion.5.refs_3_, ...), custom_call_target="tpu_custom_call" | custom-call | flops 8000000000 | tf_op jit(solution)/shard_map/halves/pallas_call | solution.py:328
  43.5 1.7 %scale.5 = (bf16[512,1024]{1,0:T(8,128)(2,1)S(1)}, bf16[512,1024]{1,0:T(8,128)(2,1)S(1)}) custom-call(s32[3]{0:T(128)S(1)} %pad_add_fusion.refs_0_.place, f32[2,2,2,136,128]{4,3,2,1,0:T(8,128)S(1)} %pack.3.refs_1_, f32[2,2,2,136,128]{4,3,2,1,0:T(8,128)S(1)} %collective-permute-done.10.refs_2_, f32[8,128]{1,0:T(8,128)S(1)} %slice.12.refs_3_, ...), custom_call_target="tpu_custom_call" | custom-call | tf_op jit(solution)/shard_map/scale/pallas_call | solution.py:357
  45.2 2.4 %greens.2 = (f32[128,256]{1,0:T(8,128)S(1)}, f32[128,256]{1,0:T(8,128)S(1)}, f32[128,256]{1,0:T(8,128)S(1)}, f32[128,256]{1,0:T(8,128)S(1)}) custom-call(s32[3]{0:T(128)S(1)} %pad_add_fusion.refs_0_.place, f32[4,4]{1,0:T(4,128)S(1)} %copy-done.1, bf16[512,1024]{1,0:T(8,128)(2,1)S(1)} %get-tuple-element.45.refs_2_, ...), custom_call_target="tpu_custom_call" | custom-call | flops 3000000000 | tf_op jit(solution)/shard_map/greens/pallas_call | solution.py:367
  47.6 0.6 collective-permute-start.19
  48.3 3.5 %collective-permute-start.20 = (f32[128,256]{1,0:T(8,128)S(1)}, f32[128,256]{1,0:T(8,128)S(1)}, u32[]{:S(2)}, u32[]{:S(2)}) collective-permute-start(f32[128,256]{1,0:T(8,128)S(1)} %get-tuple-element.63), channel_id=1, source_target_pairs={{0,16},{8,24},{16,0},{24,8},{1,17},{9,25},{17,1},{25,9},{2,18},{10... | collective-permute-start | bytes 393224 | tf_op jit(solution)/shard_map/ppermute | solution.py:26
  51.7 0.3 collective-permute-start.21
  52.1 1.6 %scale.7 = (bf16[512,1024]{1,0:T(8,128)(2,1)S(1)}, bf16[512,1024]{1,0:T(8,128)(2,1)S(1)}) custom-call(s32[3]{0:T(128)S(1)} %pad_add_fusion.refs_0_.place, f32[2,2,2,136,128]{4,3,2,1,0:T(8,128)S(1)} %pack.3.refs_1_, f32[2,2,2,136,128]{4,3,2,1,0:T(8,128)S(1)} %collective-permute-done.10.refs_2_, f32[8,128]{1,0:T(8,128)S(1)} %slice.12.refs_3_, ...), custom_call_target="tpu_custom_call" | custom-call | tf_op jit(solution)/shard_map/scale/pallas_call | solution.py:357
  53.8 1.7 %scale.6 = (bf16[512,1024]{1,0:T(8,128)(2,1)S(1)}, bf16[512,1024]{1,0:T(8,128)(2,1)S(1)}) custom-call(s32[3]{0:T(128)S(1)} %pad_add_fusion.refs_0_.place, f32[2,2,2,136,128]{4,3,2,1,0:T(8,128)S(1)} %pad_maximum_fusion.refs_1_, f32[2,2,2,136,128]{4,3,2,1,0:T(8,128)S(1)} %collective-permute-done.2.refs_2_, f32[8,128]{1,0:T(8,128)S(1)} %slice.12.refs_3_, ...), custom_call_target="tpu_custom_call" | custom-call | tf_op jit(solution)/shard_map/scale/pallas_call | solution.py:357
  55.4 2.5 %greens.3 = (f32[128,256]{1,0:T(8,128)S(1)}, f32[128,256]{1,0:T(8,128)S(1)}, f32[128,256]{1,0:T(8,128)S(1)}, f32[128,256]{1,0:T(8,128)S(1)}) custom-call(s32[3]{0:T(128)S(1)} %pad_add_fusion.refs_0_.place, f32[4,4]{1,0:T(4,128)S(1)} %copy-done.1, bf16[512,1024]{1,0:T(8,128)(2,1)S(1)} %get-tuple-element.54.refs_2_, ...), custom_call_target="tpu_custom_call" | custom-call | flops 3000000000 | tf_op jit(solution)/shard_map/greens/pallas_call | solution.py:367
  57.9 3.4 %collective-permute-done.20.refs_2_ = f32[128,256]{1,0:T(8,128)S(1)} collective-permute-done((f32[128,256]{1,0:T(8,128)S(1)}, f32[128,256]{1,0:T(8,128)S(1)}, u32[]{:S(2)}, u32[]{:S(2)}) %collective-permute-start.20) | collective-permute-done | bytes 131104 | tf_op jit(solution)/shard_map/ppermute | solution.py:26
  61.3 0.1 collective-permute-start.22
  61.4 2.0 %collective-permute-start.15 = (f32[128,256]{1,0:T(8,128)S(1)}, f32[128,256]{1,0:T(8,128)S(1)}, u32[]{:S(2)}, u32[]{:S(2)}) collective-permute-start(f32[128,256]{1,0:T(8,128)S(1)} %get-tuple-element.59), channel_id=1, source_target_pairs={{0,8},{8,0},{16,24},{24,16},{1,9},{9,1},{17,25},{25,17},{2,10},{10... | collective-permute-start | bytes 393224 | tf_op jit(solution)/shard_map/ppermute | solution.py:26
  63.4 1.1 %collective-permute-start.16 = (f32[128,256]{1,0:T(8,128)S(1)}, f32[128,256]{1,0:T(8,128)S(1)}, u32[]{:S(2)}, u32[]{:S(2)}) collective-permute-start(f32[128,256]{1,0:T(8,128)S(1)} %get-tuple-element.60), channel_id=1, source_target_pairs={{0,16},{8,24},{16,0},{24,8},{1,17},{9,25},{17,1},{25,9},{2,18},{10... | collective-permute-start | bytes 393224 | tf_op jit(solution)/shard_map/ppermute | solution.py:26
  64.5 1.4 %collective-permute-start.17 = (f32[128,256]{1,0:T(8,128)S(1)}, f32[128,256]{1,0:T(8,128)S(1)}, u32[]{:S(2)}, u32[]{:S(2)}) collective-permute-start(f32[128,256]{1,0:T(8,128)S(1)} %get-tuple-element.61), channel_id=1, source_target_pairs={{0,24},{8,16},{16,8},{24,0},{1,25},{9,17},{17,9},{25,1},{2,26},{10... | collective-permute-start | bytes 393224 | tf_op jit(solution)/shard_map/ppermute | solution.py:26
  65.9 1.1 %modes.4 = (f32[512,128]{1,0:T(8,128)S(1)}, bf16[2,1024,256]{2,1,0:T(8,128)(2,1)S(1)}) custom-call(bf16[2,512,1024]{2,1,0:T(8,128)(2,1)S(1)} %get-tuple-element.37.refs_3_.high, bf16[2,512,1024]{2,1,0:T(8,128)(2,1)S(1)} %get-tuple-element.38.low, f32[4,128,256]{2,1,0:T(8,128)S(1)} %pack.5.refs_0_, f32[4,128,256]{2,1,0:T(8,128)S(1)} %collective-permute-done.22.refs_1_), custom_call_target="tpu_custom_call" | custom-call | tf_op jit(solution)/shard_map/modes/pallas_call | solution.py:418
  67.0 0.4 collective-permute-start.23
  67.4 2.3 %collective-permute-done.15.refs_1_ = f32[128,256]{1,0:T(8,128)S(1)} collective-permute-done((f32[128,256]{1,0:T(8,128)S(1)}, f32[128,256]{1,0:T(8,128)S(1)}, u32[]{:S(2)}, u32[]{:S(2)}) %collective-permute-start.15) | collective-permute-done | bytes 131104 | tf_op jit(solution)/shard_map/ppermute | solution.py:26
  69.7 6.6 %collective-permute-done.16.refs_2_ = f32[128,256]{1,0:T(8,128)S(1)} collective-permute-done((f32[128,256]{1,0:T(8,128)S(1)}, f32[128,256]{1,0:T(8,128)S(1)}, u32[]{:S(2)}, u32[]{:S(2)}) %collective-permute-start.16) | collective-permute-done | bytes 131104 | tf_op jit(solution)/shard_map/ppermute | solution.py:26
  76.4 0.1 collective-permute-start.18
  76.5 1.9 %collective-permute-done.18.refs_1_ = f32[4,128,256]{2,1,0:T(8,128)S(1)} collective-permute-done((f32[4,128,256]{2,1,0:T(8,128)S(1)}, f32[4,128,256]{2,1,0:T(8,128)S(1)}, u32[]{:S(2)}, u32[]{:S(2)}) %collective-permute-start.18) | collective-permute-done | bytes 524320 | tf_op jit(solution)/shard_map/ppermute | solution.py:26
  78.4 0.8 modes.5
  79.2 0.4 collective-permute-start.24
  79.7 0.7 modes.6.refs_0_
  80.4 0.7 modes.7.refs_2_
  81.1 1.5 %assemble.2.refs_1_ = f32[1,512,512]{2,1,0:T(8,128)} custom-call(s32[3]{0:T(128)S(1)} %pad_add_fusion.refs_0_.place, f32[512,128]{1,0:T(8,128)S(1)} %modes.6.refs_0_, f32[512,128]{1,0:T(8,128)S(1)} %collective-permute-done.23._.refs_1_, f32[512,128]{1,0:T(8,128)S(1)} %modes.7.refs_2_), custom_call_target="tpu_custom_call" | custom-call | tf_op jit(solution)/shard_map/assemble/pallas_call | solution.py:382
  82.6 5.1 %collective-permute-done.24.refs_0_ = f32[512,128]{1,0:T(8,128)S(1)} collective-permute-done((f32[512,128]{1,0:T(8,128)S(1)}, f32[512,128]{1,0:T(8,128)S(1)}, u32[]{:S(2)}, u32[]{:S(2)}) %collective-permute-start.24) | collective-permute-done | bytes 262176 | tf_op jit(solution)/shard_map/ppermute | solution.py:26
  87.6 1.3 %assemble.3 = f32[1,512,512]{2,1,0:T(8,128)} custom-call(s32[3]{0:T(128)S(1)} %pad_add_fusion.refs_0_.place, f32[512,128]{1,0:T(8,128)S(1)} %collective-permute-done.24.refs_0_, f32[1,512,512]{2,1,0:T(8,128)} %assemble.2.refs_1_), custom_call_target="tpu_custom_call", output_to_operand_aliasing={{}: (2, {})} | custom-call | tf_op jit(solution)/shard_map/assemble/pallas_call | solution.py:382
  (42 shorter events, 0.4 us)
Async XLA Ops:
  2.8 12.0 %copy-start.2 = (f32[2,136,128]{2,1,0:T(8,128)S(1)}, f32[2,136,128]{2,1,0:T(8,128)}, u32[]{:S(2)}) copy-start(f32[2,136,128]{2,1,0:T(8,128)} %get-tuple-element.39) | copy-start | bytes 417796
  2.8 9.1 %collective-permute-start.3 = (f32[264,128]{1,0:T(8,128)}, f32[264,128]{1,0:T(8,128)S(1)}, u32[]{:S(2)}, u32[]{:S(2)}) collective-permute-start(f32[264,128]{1,0:T(8,128)} %get-tuple-element.42), channel_id=1, source_target_pairs={{0,8},{8,0},{16,24},{24,16},{1,9},{9,1},{17,25},{25,17},{2,10},{10... | collective-permute-start | bytes 405512 | tf_op jit(solution)/shard_map/ppermute | solution.py:26
  5.9 17.9 %collective-permute-start.4 = (f32[264,128]{1,0:T(8,128)}, f32[264,128]{1,0:T(8,128)S(1)}, u32[]{:S(2)}, u32[]{:S(2)}) collective-permute-start(f32[264,128]{1,0:T(8,128)} %get-tuple-element.43), channel_id=1, source_target_pairs={{0,16},{8,24},{16,0},{24,8},{1,17},{9,25},{17,1},{25,9},{2,18},{10... | collective-permute-start | bytes 405512 | tf_op jit(solution)/shard_map/ppermute | solution.py:26
  8.4 12.1 %collective-permute-start.5 = (f32[264,128]{1,0:T(8,128)}, f32[264,128]{1,0:T(8,128)S(1)}, u32[]{:S(2)}, u32[]{:S(2)}) collective-permute-start(f32[264,128]{1,0:T(8,128)} %get-tuple-element.44), channel_id=1, source_target_pairs={{0,24},{8,16},{16,8},{24,0},{1,25},{9,17},{17,9},{25,1},{2,26},{10... | collective-permute-start | bytes 405512 | tf_op jit(solution)/shard_map/ppermute | solution.py:26
  8.4 6.3 %collective-permute-start = (f32[2,136,128]{2,1,0:T(8,128)}, f32[2,136,128]{2,1,0:T(8,128)S(1)}, u32[]{:S(2)}, u32[]{:S(2)}) collective-permute-start(f32[2,136,128]{2,1,0:T(8,128)} %get-tuple-element.40), channel_id=1, source_target_pairs={{0,2},{1,3},{2,0},{3,1},{4,6},{5,7},{6,4},{7,5},{8,10},{9,11},{10,... | collective-permute-start | bytes 417800 | tf_op jit(solution)/shard_map/ppermute | solution.py:26
  11.8 0.9 %copy-start = (f32[264,128]{1,0:T(8,128)S(1)}, f32[264,128]{1,0:T(8,128)}, u32[]{:S(2)}) copy-start(f32[264,128]{1,0:T(8,128)} %get-tuple-element.41.refs_0_) | copy-start | bytes 405508
  12.8 7.1 %collective-permute-start.8 = (f32[2,256,128]{2,1,0:T(8,128)S(1)}, f32[2,256,128]{2,1,0:T(8,128)S(1)}, u32[]{:S(2)}, u32[]{:S(2)}) collective-permute-start(f32[2,256,128]{2,1,0:T(8,128)S(1)} %gate.3), channel_id=1, source_target_pairs={{0,4},{4,0},{1,5},{5,1},{2,6},{6,2},{3,7},{7,3},{8,12},{12,8},{9,1... | collective-permute-start | bytes 786440 | tf_op jit(solution)/shard_map/ppermute | solution.py:26
  14.8 12.7 %collective-permute-start.1 = (f32[2,2,136,128]{3,2,1,0:T(8,128)S(1)}, f32[2,2,136,128]{3,2,1,0:T(8,128)S(1)}, u32[]{:S(2)}, u32[]{:S(2)}) collective-permute-start(f32[2,2,136,128]{3,2,1,0:T(8,128)S(1)} %get-tuple-element.70), channel_id=1, source_target_pairs={{0,8},{8,0},{16,24},{24,16},{1,9},{9,1},{17,25},{25,17},{2,10},{10... | collective-permute-start | bytes 835592 | tf_op jit(solution)/shard_map/ppermute | solution.py:26
  15.5 17.2 %collective-permute-start.6 = (f32[2,2,136,128]{3,2,1,0:T(8,128)S(1)}, f32[2,2,136,128]{3,2,1,0:T(8,128)S(1)}, u32[]{:S(2)}, u32[]{:S(2)}) collective-permute-start(f32[2,2,136,128]{3,2,1,0:T(8,128)S(1)} %get-tuple-element.70), channel_id=1, source_target_pairs={{0,16},{8,24},{16,0},{24,8},{1,17},{9,25},{17,1},{25,9},{2,18},{10... | collective-permute-start | bytes 835592 | tf_op jit(solution)/shard_map/ppermute | solution.py:26
  19.9 16.5 %collective-permute-start.9 = (f32[4,256,128]{2,1,0:T(8,128)S(1)}, f32[4,256,128]{2,1,0:T(8,128)S(1)}, u32[]{:S(2)}, u32[]{:S(2)}) collective-permute-start(f32[4,256,128]{2,1,0:T(8,128)S(1)} %pad_maximum_fusion.2.refs_1_), channel_id=1, source_target_pairs={{0,2},{1,3},{2,0},{3,1},{4,6},{5,7},{6,4},{7,5},{8,10},{9,11},{10,... | collective-permute-start | bytes 1572872 | tf_op jit(solution)/shard_map/ppermute | solution.py:26
  20.6 13.9 %collective-permute-start.13 = (f32[1,256,128]{2,1,0:T(8,128)S(1)}, f32[1,256,128]{2,1,0:T(8,128)S(1)}, u32[]{:S(2)}, u32[]{:S(2)}) collective-permute-start(f32[1,256,128]{2,1,0:T(8,128)S(1)} %gate.5), channel_id=1, source_target_pairs={{0,2},{1,3},{2,0},{3,1},{4,6},{5,7},{6,4},{7,5},{8,10},{9,11},{10,... | collective-permute-start | bytes 393224 | tf_op jit(solution)/shard_map/ppermute | solution.py:26
  23.8 12.2 %collective-permute-start.11 = (f32[1,256,128]{2,1,0:T(8,128)S(1)}, f32[1,256,128]{2,1,0:T(8,128)S(1)}, u32[]{:S(2)}, u32[]{:S(2)}) collective-permute-start(f32[1,256,128]{2,1,0:T(8,128)S(1)} %gate.4), channel_id=1, source_target_pairs={{0,4},{4,0},{1,5},{5,1},{2,6},{6,2},{3,7},{7,3},{8,12},{12,8},{9,1... | collective-permute-start | bytes 393224 | tf_op jit(solution)/shard_map/ppermute | solution.py:26
  27.5 9.9 %collective-permute-start.2 = (f32[2,2,2,136,128]{4,3,2,1,0:T(8,128)S(1)}, f32[2,2,2,136,128]{4,3,2,1,0:T(8,128)S(1)}, u32[]{:S(2)}, u32[]{:S(2)}) collective-permute-start(f32[2,2,2,136,128]{4,3,2,1,0:T(8,128)S(1)} %pad_maximum_fusion.refs_1_), channel_id=1, source_target_pairs={{0,1},{1,0},{2,3},{3,2},{4,5},{5,4},{6,7},{7,6},{8,9},{9,8},{10,11... | collective-permute-start | bytes 1671176 | tf_op jit(solution)/shard_map/ppermute | solution.py:26
  32.7 7.3 %collective-permute-start.7 = (f32[2,2,136,128]{3,2,1,0:T(8,128)S(1)}, f32[2,2,136,128]{3,2,1,0:T(8,128)S(1)}, u32[]{:S(2)}, u32[]{:S(2)}) collective-permute-start(f32[2,2,136,128]{3,2,1,0:T(8,128)S(1)} %collective-permute-done.6.refs_0_), channel_id=1, source_target_pairs={{0,8},{8,0},{16,24},{24,16},{1,9},{9,1},{17,25},{25,17},{2,10},{10... | collective-permute-start | bytes 835592 | tf_op jit(solution)/shard_map/ppermute | solution.py:26
  34.4 6.4 %collective-permute-start.14 = (f32[2,256,128]{2,1,0:T(8,128)S(1)}, f32[2,256,128]{2,1,0:T(8,128)S(1)}, u32[]{:S(2)}, u32[]{:S(2)}) collective-permute-start(f32[2,256,128]{2,1,0:T(8,128)S(1)} %pad_maximum_fusion.5.refs_3_), channel_id=1, source_target_pairs={{0,4},{4,0},{1,5},{5,1},{2,6},{6,2},{3,7},{7,3},{8,12},{12,8},{9,1... | collective-permute-start | bytes 786440 | tf_op jit(solution)/shard_map/ppermute | solution.py:26
  36.0 6.4 %collective-permute-start.12 = (f32[2,256,128]{2,1,0:T(8,128)S(1)}, f32[2,256,128]{2,1,0:T(8,128)S(1)}, u32[]{:S(2)}, u32[]{:S(2)}) collective-permute-start(f32[2,256,128]{2,1,0:T(8,128)S(1)} %pad_maximum_fusion.4.refs_1_), channel_id=1, source_target_pairs={{0,2},{1,3},{2,0},{3,1},{4,6},{5,7},{6,4},{7,5},{8,10},{9,11},{10,... | collective-permute-start | bytes 786440 | tf_op jit(solution)/shard_map/ppermute | solution.py:26
  40.0 5.2 %copy-start.1 = (f32[4,4]{1,0:T(4,128)S(1)}, f32[4,4]{1,0:T(4,128)}, u32[]{:S(2)}) copy-start(f32[4,4]{1,0:T(4,128)} %refs_1_.3) | copy-start | bytes 196
  40.0 3.5 %collective-permute-start.10 = (f32[2,2,2,136,128]{4,3,2,1,0:T(8,128)S(1)}, f32[2,2,2,136,128]{4,3,2,1,0:T(8,128)S(1)}, u32[]{:S(2)}, u32[]{:S(2)}) collective-permute-start(f32[2,2,2,136,128]{4,3,2,1,0:T(8,128)S(1)} %pack.3.refs_1_), channel_id=1, source_target_pairs={{0,1},{1,0},{2,3},{3,2},{4,5},{5,4},{6,7},{7,6},{8,9},{9,8},{10,11... | collective-permute-start | bytes 1671176 | tf_op jit(solution)/shard_map/ppermute | solution.py:26
  47.6 10.2 %collective-permute-start.19 = (f32[128,256]{1,0:T(8,128)S(1)}, f32[128,256]{1,0:T(8,128)S(1)}, u32[]{:S(2)}, u32[]{:S(2)}) collective-permute-start(f32[128,256]{1,0:T(8,128)S(1)} %get-tuple-element.62), channel_id=1, source_target_pairs={{0,8},{8,0},{16,24},{24,16},{1,9},{9,1},{17,25},{25,17},{2,10},{10... | collective-permute-start | bytes 393224 | tf_op jit(solution)/shard_map/ppermute | solution.py:26
  48.3 13.0 %collective-permute-start.20 = (f32[128,256]{1,0:T(8,128)S(1)}, f32[128,256]{1,0:T(8,128)S(1)}, u32[]{:S(2)}, u32[]{:S(2)}) collective-permute-start(f32[128,256]{1,0:T(8,128)S(1)} %get-tuple-element.63), channel_id=1, source_target_pairs={{0,16},{8,24},{16,0},{24,8},{1,17},{9,25},{17,1},{25,9},{2,18},{10... | collective-permute-start | bytes 393224 | tf_op jit(solution)/shard_map/ppermute | solution.py:26
  51.7 9.5 %collective-permute-start.21 = (f32[128,256]{1,0:T(8,128)S(1)}, f32[128,256]{1,0:T(8,128)S(1)}, u32[]{:S(2)}, u32[]{:S(2)}) collective-permute-start(f32[128,256]{1,0:T(8,128)S(1)} %get-tuple-element.64), channel_id=1, source_target_pairs={{0,24},{8,16},{16,8},{24,0},{1,25},{9,17},{17,9},{25,1},{2,26},{10... | collective-permute-start | bytes 393224 | tf_op jit(solution)/shard_map/ppermute | solution.py:26
  61.3 4.6 %collective-permute-start.22 = (f32[4,128,256]{2,1,0:T(8,128)S(1)}, f32[4,128,256]{2,1,0:T(8,128)S(1)}, u32[]{:S(2)}, u32[]{:S(2)}) collective-permute-start(f32[4,128,256]{2,1,0:T(8,128)S(1)} %pack.5.refs_0_), channel_id=1, source_target_pairs={{0,1},{1,0},{2,3},{3,2},{4,5},{5,4},{6,7},{7,6},{8,9},{9,8},{10,11... | collective-permute-start | bytes 1572872 | tf_op jit(solution)/shard_map/ppermute | solution.py:26
  61.4 8.3 %collective-permute-start.15 = (f32[128,256]{1,0:T(8,128)S(1)}, f32[128,256]{1,0:T(8,128)S(1)}, u32[]{:S(2)}, u32[]{:S(2)}) collective-permute-start(f32[128,256]{1,0:T(8,128)S(1)} %get-tuple-element.59), channel_id=1, source_target_pairs={{0,8},{8,0},{16,24},{24,16},{1,9},{9,1},{17,25},{25,17},{2,10},{10... | collective-permute-start | bytes 393224 | tf_op jit(solution)/shard_map/ppermute | solution.py:26
  63.4 12.9 %collective-permute-start.16 = (f32[128,256]{1,0:T(8,128)S(1)}, f32[128,256]{1,0:T(8,128)S(1)}, u32[]{:S(2)}, u32[]{:S(2)}) collective-permute-start(f32[128,256]{1,0:T(8,128)S(1)} %get-tuple-element.60), channel_id=1, source_target_pairs={{0,16},{8,24},{16,0},{24,8},{1,17},{9,25},{17,1},{25,9},{2,18},{10... | collective-permute-start | bytes 393224 | tf_op jit(solution)/shard_map/ppermute | solution.py:26
  64.5 11.9 %collective-permute-start.17 = (f32[128,256]{1,0:T(8,128)S(1)}, f32[128,256]{1,0:T(8,128)S(1)}, u32[]{:S(2)}, u32[]{:S(2)}) collective-permute-start(f32[128,256]{1,0:T(8,128)S(1)} %get-tuple-element.61), channel_id=1, source_target_pairs={{0,24},{8,16},{16,8},{24,0},{1,25},{9,17},{17,9},{25,1},{2,26},{10... | collective-permute-start | bytes 393224 | tf_op jit(solution)/shard_map/ppermute | solution.py:26
  67.0 9.5 %collective-permute-start.23 = (f32[512,128]{1,0:T(8,128)S(1)}, f32[512,128]{1,0:T(8,128)S(1)}, u32[]{:S(2)}, u32[]{:S(2)}) collective-permute-start(f32[512,128]{1,0:T(8,128)S(1)} %get-tuple-element.65), channel_id=1, source_target_pairs={{0,2},{1,3},{2,0},{3,1},{4,6},{5,7},{6,4},{7,5},{8,10},{9,11},{10,... | collective-permute-start | bytes 786440 | tf_op jit(solution)/shard_map/ppermute | solution.py:26
  76.4 2.0 %collective-permute-start.18 = (f32[4,128,256]{2,1,0:T(8,128)S(1)}, f32[4,128,256]{2,1,0:T(8,128)S(1)}, u32[]{:S(2)}, u32[]{:S(2)}) collective-permute-start(f32[4,128,256]{2,1,0:T(8,128)S(1)} %pack.4.refs_0_), channel_id=1, source_target_pairs={{0,1},{1,0},{2,3},{3,2},{4,5},{5,4},{6,7},{7,6},{8,9},{9,8},{10,11... | collective-permute-start | bytes 1572872 | tf_op jit(solution)/shard_map/ppermute | solution.py:26
  79.2 8.4 %collective-permute-start.24 = (f32[512,128]{1,0:T(8,128)S(1)}, f32[512,128]{1,0:T(8,128)S(1)}, u32[]{:S(2)}, u32[]{:S(2)}) collective-permute-start(f32[512,128]{1,0:T(8,128)S(1)} %get-tuple-element.66), channel_id=1, source_target_pairs={{0,2},{1,3},{2,0},{3,1},{4,6},{5,7},{6,4},{7,5},{8,10},{9,11},{10,... | collective-permute-start | bytes 786440 | tf_op jit(solution)/shard_map/ppermute | solution.py:26

commit v5 on v4

--- a/solution.py
+++ b/solution.py
@@ -14,7 +14,7 @@
 EXTRA = 8
 CHUNKS = 2
 FINE = 32
-HALVES_COST, SCALE_COST, GREENS_COST, TOKEN_COST, BEHIND, GATE = (12, 8), (0, 0), 3, 3.6, 0, 1
+HALVES_COST, SCALE_COST, GREENS_COST, TOKEN_COST, BEHIND, GATE, PARTS = (12, 8), (0, 0), 3, 0.7, 1, 1, 1
 
 
 def bits_of(size):
@@ -178,17 +178,18 @@
             low[odd, h * FINE : (h + 1) * FINE, :] = b
 
 
-def fold_kernel(block, groups, waits, high, low, *refs):
-    here, there = refs[:2]
-    out, both = refs[2 + waits :]
-    T, breadth, width = here.shape
+def fold_kernel(block, groups, packs, waits, high, low, *refs):
+    here = [refs[2 * i].at[s] for i in range(packs) for s in range(refs[2 * i].shape[0])]
+    there = [refs[2 * i + 1].at[s] for i in range(packs) for s in range(refs[2 * i + 1].shape[0])]
+    out, both = refs[2 * packs + waits :]
+    T, (breadth, width) = len(here), here[0].shape
     step = width // groups
     at = 0
     for s in range(T):
         for d in range(groups):
-            mine = here[s, :, d * step : (d + 1) * step]
+            mine = here[s][:, d * step : (d + 1) * step]
             e = groups - 1 - d
-            theirs = there[s ^ (T - 1), :, e * step : (e + 1) * step]
+            theirs = there[s ^ (T - 1)][:, e * step : (e + 1) * step]
             for odd, value in enumerate((mine + theirs, mine - theirs)):
                 a, b = split(value.T)
                 both[odd, at : at + step, 0:breadth] = a
@@ -394,15 +395,19 @@
     early, late = [], []
     for chunk in range(CHUNKS):
         behind = [own[chunk + 1][BEHIND]] if chunk + 1 < CHUNKS else []
-        mine = pl.pallas_call(
-            functools.partial(pack_kernel, range(T)),
-            out_shape=jax.ShapeDtypeStruct((T, rp, wide), f32),
-            in_specs=[vmem] * T + [hbm] * len(behind),
-            out_specs=vmem,
-            compiler_params=params,
-            cost_estimate=cost(0),
-            name="pack",
-        )(*own[chunk], *behind)
+        packed = []
+        for group in groups if PARTS and chunk == CHUNKS - 1 else [range(T)]:
+            mine = pl.pallas_call(
+                functools.partial(pack_kernel, range(len(group))),
+                out_shape=jax.ShapeDtypeStruct((len(group), rp, wide), f32),
+                in_specs=[vmem] * len(group) + [hbm] * len(behind),
+                out_specs=vmem,
+                compiler_params=params,
+                cost_estimate=cost(0),
+                name="pack",
+            )(*[own[chunk][s] for s in group], *behind)
+            packed += [mine, swap(mine, "col", 1)]
+            behind = packed[-1:]
         waits = [
             pl.pallas_call(
                 token_kernel,
@@ -416,14 +421,14 @@
         ]
         shape = jax.ShapeDtypeStruct((share, rp), f32)
         made = pl.pallas_call(
-            functools.partial(fold_kernel, 0, H, len(waits)),
+            functools.partial(fold_kernel, 0, H, len(packed) // 2, len(waits)),
             out_shape=[shape, jax.ShapeDtypeStruct((2, all_cols, 2 * rp), bf16)],
-            in_specs=[vmem] * 4 + [hbm] * len(waits),
+            in_specs=[vmem] * (2 + len(packed)) + [hbm] * len(waits),
             out_specs=[vmem] * 2,
             compiler_params=params,
             cost_estimate=cost(0),
             name="modes",
-        )(t_high, t_low, mine, swap(mine, "col", 1), *waits)
+        )(t_high, t_low, *packed, *waits)
         made, both = [made[0]], made[1]
         for block in range(1, H):
             made.append(

time: 89.2 us -> 89.1 us (level)
  waiting for transfers between devices: 32.4 us -> 30.5 us
  starting transfers between devices: 28.9 us -> 30.6 us
    ppermute x25 -> x26, waiting for transfers between devices: 32.4 us -> 30.5 us  [swap(): return lax.ppermute(value, axis, [(i, i ^ bit) for i in range(size)])]
    ppermute x25 -> x26, starting transfers between devices: 28.9 us -> 30.6 us  [swap(): return lax.ppermute(value, axis, [(i, i ^ bit) for i in range(size)])]
    pallas_call x4 -> x5, Pallas kernels: 1.97 us -> 1.98 us  [the longest x2 1.91 us: per_device(): pl.pallas_call(functools.partial(fold_kernel, 0, H, len(packed) // 2, len...]
  transfers between devices with their start and end apart: 25 -> 26, of which waited for: 12 -> 12; matrix products, arithmetic and copies ran while one was open for 3% -> 3% of each run, Pallas kernels for 16% -> 16%
where the time goes in v5:
time: 89.1 us; the launch traced here: 88.9 us
  starting transfers between devices  30.6 us (34%)
  waiting for transfers between devices  30.5 us (34%)
  Pallas kernels  22.7 us (25%)
  other arithmetic  2.04 us (2%)
  local copies, waits for them, and re-layouts  1.78 us (2%)
  between operations  1.21 us (1%)
    ppermute x26, starting transfers between devices, swap(): return lax.ppermute(value, axis, [(i, i ^ bit) for i in range(size)])  30.6 us
    ppermute x26, waiting for transfers between devices, swap(): return lax.ppermute(value, axis, [(i, i ^ bit) for i in range(size)])  30.5 us
    pallas_call x4, Pallas kernels, per_device(): pl.pallas_call(functools.partial(scale_kernel, chunk, T, C, (occ_r, emp_r...  6.54 us
    pallas_call x2, Pallas kernels, per_device(): pl.pallas_call(functools.partial(green_kernel, T, len(groups), k_occ // l...  4.89 us
    pallas_call x2, Pallas kernels, assemble(): pl.pallas_call(functools.partial(place_kernel, [at for at, _ in parts]),...  2.71 us
    pallas_call x1, Pallas kernels, per_device(): pl.pallas_call(functools.partial(prepare_kernel, T, H), out_shape=[jax.Sh...  2.09 us
    pallas_call x2, Pallas kernels, per_device(): pl.pallas_call(functools.partial(halves_kernel, slots[g], C, X, (occ_c, e...  2.07 us
    pallas_call x2, Pallas kernels, per_device(): pl.pallas_call(functools.partial(fold_kernel, 0, H, len(packed) // 2, len...  1.91 us
  transfers between devices with their start and end apart: 26, of which 12 were waited for; matrix products, arithmetic and copies ran while one was open for 3% of the time, Pallas kernels for 16%

profile of v5, /device:TPU:0, one launch (start us, length us, event | category | flops | bytes accessed | tf_op | source)
XLA Modules:
  0.0 88.9 jit_solution(6939100860831399233)
XLA Ops:
  0.7 2.1 %prepare.1 = (f32[264,128]{1,0:T(8,128)}, f32[264,128]{1,0:T(8,128)}, f32[264,128]{1,0:T(8,128)}, f32[264,128]{1,0:T(8,128)}, f32[2,136,128]{2,1,0:T(8,128)}, /*index=5*/f32[2,136,128]{2,1,0:T(8,128)}) custom-call(f32[1]{0:T(128)S(6)} %copy.11.times, f32[64,512]{1,0:T(8,128)} %bitcast.18, f32[192,512]{1,0:T(8,128)} %bitcast.13, f32[32,512]{1,0:T(8,128)} %bitcast.19, ...), custom_call_target="tpu_custom_call" | custom-call | tf_op jit(solution)/shard_map/prepare/pallas_call | solution.py:243
  2.8 0.0 copy-start.2
  2.8 3.1 %collective-permute-start.3 = (f32[264,128]{1,0:T(8,128)}, f32[264,128]{1,0:T(8,128)S(1)}, u32[]{:S(2)}, u32[]{:S(2)}) collective-permute-start(f32[264,128]{1,0:T(8,128)} %get-tuple-element.42), channel_id=1, source_target_pairs={{0,8},{8,0},{16,24},{24,16},{1,9},{9,1},{17,25},{25,17},{2,10},{10... | collective-permute-start | bytes 405512 | tf_op jit(solution)/shard_map/ppermute | solution.py:26
  5.9 2.6 %collective-permute-start.4 = (f32[264,128]{1,0:T(8,128)}, f32[264,128]{1,0:T(8,128)S(1)}, u32[]{:S(2)}, u32[]{:S(2)}) collective-permute-start(f32[264,128]{1,0:T(8,128)} %get-tuple-element.43), channel_id=1, source_target_pairs={{0,16},{8,24},{16,0},{24,8},{1,17},{9,25},{17,1},{25,9},{2,18},{10... | collective-permute-start | bytes 405512 | tf_op jit(solution)/shard_map/ppermute | solution.py:26
  8.4 1.7 %collective-permute-start = (f32[2,136,128]{2,1,0:T(8,128)}, f32[2,136,128]{2,1,0:T(8,128)S(1)}, u32[]{:S(2)}, u32[]{:S(2)}) collective-permute-start(f32[2,136,128]{2,1,0:T(8,128)} %get-tuple-element.40), channel_id=1, source_target_pairs={{0,2},{1,3},{2,0},{3,1},{4,6},{5,7},{6,4},{7,5},{8,10},{9,11},{10,... | collective-permute-start | bytes 417800 | tf_op jit(solution)/shard_map/ppermute | solution.py:26
  10.2 0.1 rev.3
  10.3 0.1 broadcast_add_fusion.1
  10.4 0.1 add.145
  10.5 0.1 iota_select_fusion
  10.6 0.1 broadcast_add_fusion
  10.6 0.1 multiply_add_fusion
  10.7 1.1 %cosine_multiply_fusion.1 = (f32[1,32,1024]{2,1,0:T(8,128)S(1)}, f32[1,32,1024]{2,1,0:T(8,128)S(1)}, f32[1,32,1024]{2,1,0:T(8,128)S(1)}, f32[1,32,1024]{2,1,0:T(8,128)S(1)}) fusion(s32[32]{0:T(128)S(1)} %get-tuple-element.81, s32[1024]{0:T(1024)S(1)} %bitcast.20, s32[32]{0:T(128)S(1)} %get-tuple-element.82), kind=kLoop, calls=%fused_computation.26 | loop fusion | flops 1048576 | bytes 528640 | tf_op jit(solution)/shard_map/mul | solution.py:314
  11.9 0.9 %copy-done = f32[264,128]{1,0:T(8,128)S(1)} copy-done((f32[264,128]{1,0:T(8,128)S(1)}, f32[264,128]{1,0:T(8,128)}, u32[]{:S(2)}) %copy-start) | copy-done | bytes 135192
  12.8 1.6 %collective-permute-start.8 = (f32[2,256,128]{2,1,0:T(8,128)S(1)}, f32[2,256,128]{2,1,0:T(8,128)S(1)}, u32[]{:S(2)}, u32[]{:S(2)}) collective-permute-start(f32[2,256,128]{2,1,0:T(8,128)S(1)} %gate.3), channel_id=1, source_target_pairs={{0,4},{4,0},{1,5},{5,1},{2,6},{6,2},{3,7},{7,3},{8,12},{12,8},{9,1... | collective-permute-start | bytes 786440 | tf_op jit(solution)/shard_map/ppermute | solution.py:26
  14.3 0.3 fusion.10
  14.8 0.7 collective-permute-start.1
  15.5 3.5 %collective-permute-start.6 = (f32[2,2,136,128]{3,2,1,0:T(8,128)S(1)}, f32[2,2,136,128]{3,2,1,0:T(8,128)S(1)}, u32[]{:S(2)}, u32[]{:S(2)}) collective-permute-start(f32[2,2,136,128]{3,2,1,0:T(8,128)S(1)} %get-tuple-element.70), channel_id=1, source_target_pairs={{0,16},{8,24},{16,0},{24,8},{1,17},{9,25},{17,1},{25,9},{2,18},{10... | collective-permute-start | bytes 835592 | tf_op jit(solution)/shard_map/ppermute | solution.py:26
  19.0 0.8 collective-permute-done.8.refs_1_
  19.9 0.6 collective-permute-start.9
  20.6 1.5 %collective-permute-start.13 = (f32[1,256,128]{2,1,0:T(8,128)S(1)}, f32[1,256,128]{2,1,0:T(8,128)S(1)}, u32[]{:S(2)}, u32[]{:S(2)}) collective-permute-start(f32[1,256,128]{2,1,0:T(8,128)S(1)} %gate.5), channel_id=1, source_target_pairs={{0,2},{1,3},{2,0},{3,1},{4,6},{5,7},{6,4},{7,5},{8,10},{9,11},{10,... | collective-permute-start | bytes 393224 | tf_op jit(solution)/shard_map/ppermute | solution.py:26
  22.1 0.1 pad_add_fusion.refs_0_.place
  22.1 0.7 slice.12.refs_3_
  22.8 0.9 %cosines.1 = (bf16[2,512,1024]{2,1,0:T(8,128)(2,1)S(1)}, bf16[2,512,1024]{2,1,0:T(8,128)(2,1)S(1)}) custom-call(f32[4,32,1024]{2,1,0:T(8,128)S(1)} %pad_maximum_fusion.1.near, f32[2,16,1024]{2,1,0:T(8,128)S(1)} %pad_maximum_fusion.6.far), custom_call_target="tpu_custom_call" | custom-call | tf_op jit(solution)/shard_map/cosines/pallas_call | solution.py:317
  23.8 1.6 %collective-permute-start.11 = (f32[1,256,128]{2,1,0:T(8,128)S(1)}, f32[1,256,128]{2,1,0:T(8,128)S(1)}, u32[]{:S(2)}, u32[]{:S(2)}) collective-permute-start(f32[1,256,128]{2,1,0:T(8,128)S(1)} %gate.4), channel_id=1, source_target_pairs={{0,4},{4,0},{1,5},{5,1},{2,6},{6,2},{3,7},{7,3},{8,12},{12,8},{9,1... | collective-permute-start | bytes 393224 | tf_op jit(solution)/shard_map/ppermute | solution.py:26
  25.4 2.1 %collective-permute-done.1 = f32[2,2,136,128]{3,2,1,0:T(8,128)S(1)} collective-permute-done((f32[2,2,136,128]{3,2,1,0:T(8,128)S(1)}, f32[2,2,136,128]{3,2,1,0:T(8,128)S(1)}, u32[]{:S(2)}, u32[]{:S(2)}) %collective-permute-start.1) | collective-permute-done | bytes 278560 | tf_op jit(solution)/shard_map/ppermute | solution.py:26
  27.5 0.1 collective-permute-start.2
  27.6 5.1 %collective-permute-done.6.refs_0_ = f32[2,2,136,128]{3,2,1,0:T(8,128)S(1)} collective-permute-done((f32[2,2,136,128]{3,2,1,0:T(8,128)S(1)}, f32[2,2,136,128]{3,2,1,0:T(8,128)S(1)}, u32[]{:S(2)}, u32[]{:S(2)}) %collective-permute-start.6) | collective-permute-done | bytes 278560 | tf_op jit(solution)/shard_map/ppermute | solution.py:26
  32.7 1.7 %collective-permute-done.13 = f32[1,256,128]{2,1,0:T(8,128)S(1)} collective-permute-done((f32[1,256,128]{2,1,0:T(8,128)S(1)}, f32[1,256,128]{2,1,0:T(8,128)S(1)}, u32[]{:S(2)}, u32[]{:S(2)}) %collective-permute-start.13) | collective-permute-done | bytes 131104 | tf_op jit(solution)/shard_map/ppermute | solution.py:26
  34.5 1.6 %collective-permute-start.14 = (f32[2,256,128]{2,1,0:T(8,128)S(1)}, f32[2,256,128]{2,1,0:T(8,128)S(1)}, u32[]{:S(2)}, u32[]{:S(2)}) collective-permute-start(f32[2,256,128]{2,1,0:T(8,128)S(1)} %pad_maximum_fusion.5.refs_3_), channel_id=1, source_target_pairs={{0,4},{4,0},{1,5},{5,1},{2,6},{6,2},{3,7},{7,3},{8,12},{12,8},{9,1... | collective-permute-start | bytes 786440 | tf_op jit(solution)/shard_map/ppermute | solution.py:26
  36.0 0.4 collective-permute-start.12
  36.4 1.0 %halves.2 = (bf16[1024,256]{1,0:T(8,128)(2,1)S(1)}, bf16[1024,256]{1,0:T(8,128)(2,1)S(1)}) custom-call(s32[3]{0:T(128)S(1)} %pad_add_fusion.refs_0_.place, f32[4,256,128]{2,1,0:T(8,128)S(1)} %pad_maximum_fusion.2.refs_1_, f32[4,256,128]{2,1,0:T(8,128)S(1)} %collective-permute-done.9.refs_2_, bf16[2,512,1024]{2,1,0:T(8,128)(2,1)S(1)} %get-tuple-element.37.refs_3_.high), custom_call_target="tpu_custom_call" | custom-call | flops 12000000000 | tf_op jit(solution)/shard_map/halves/pallas_call | solution.py:329
  37.4 1.6 %scale.4 = (bf16[512,1024]{1,0:T(8,128)(2,1)S(1)}, bf16[512,1024]{1,0:T(8,128)(2,1)S(1)}) custom-call(s32[3]{0:T(128)S(1)} %pad_add_fusion.refs_0_.place, f32[2,2,2,136,128]{4,3,2,1,0:T(8,128)S(1)} %pad_maximum_fusion.refs_1_, f32[2,2,2,136,128]{4,3,2,1,0:T(8,128)S(1)} %collective-permute-done.2.refs_2_, f32[8,128]{1,0:T(8,128)S(1)} %slice.12.refs_3_, ...), custom_call_target="tpu_custom_call" | custom-call | tf_op jit(solution)/shard_map/scale/pallas_call | solution.py:358
  39.0 0.9 %collective-permute-done.7.refs_1_ = f32[2,2,136,128]{3,2,1,0:T(8,128)S(1)} collective-permute-done((f32[2,2,136,128]{3,2,1,0:T(8,128)S(1)}, f32[2,2,136,128]{3,2,1,0:T(8,128)S(1)}, u32[]{:S(2)}, u32[]{:S(2)}) %collective-permute-start.7) | collective-permute-done | bytes 278560 | tf_op jit(solution)/shard_map/ppermute | solution.py:26
  40.0 0.1 collective-permute-start.10
  40.1 0.8 collective-permute-done.14.refs_4_
  40.9 1.6 %collective-permute-done.12.refs_2_ = f32[2,256,128]{2,1,0:T(8,128)S(1)} collective-permute-done((f32[2,256,128]{2,1,0:T(8,128)S(1)}, f32[2,256,128]{2,1,0:T(8,128)S(1)}, u32[]{:S(2)}, u32[]{:S(2)}) %collective-permute-start.12) | collective-permute-done | bytes 262176 | tf_op jit(solution)/shard_map/ppermute | solution.py:26
  42.5 1.0 %halves.3 = (bf16[1024,256]{1,0:T(8,128)(2,1)S(1)}, bf16[1024,256]{1,0:T(8,128)(2,1)S(1)}) custom-call(s32[3]{0:T(128)S(1)} %pad_add_fusion.refs_0_.place, f32[2,256,128]{2,1,0:T(8,128)S(1)} %pad_maximum_fusion.4.refs_1_, f32[2,256,128]{2,1,0:T(8,128)S(1)} %collective-permute-done.12.refs_2_, f32[2,256,128]{2,1,0:T(8,128)S(1)} %pad_maximum_fusion.5.refs_3_, ...), custom_call_target="tpu_custom_call" | custom-call | flops 8000000000 | tf_op jit(solution)/shard_map/halves/pallas_call | solution.py:329
  43.5 1.7 %scale.5 = (bf16[512,1024]{1,0:T(8,128)(2,1)S(1)}, bf16[512,1024]{1,0:T(8,128)(2,1)S(1)}) custom-call(s32[3]{0:T(128)S(1)} %pad_add_fusion.refs_0_.place, f32[2,2,2,136,128]{4,3,2,1,0:T(8,128)S(1)} %pack.4.refs_1_, f32[2,2,2,136,128]{4,3,2,1,0:T(8,128)S(1)} %collective-permute-done.10.refs_2_, f32[8,128]{1,0:T(8,128)S(1)} %slice.12.refs_3_, ...), custom_call_target="tpu_custom_call" | custom-call | tf_op jit(solution)/shard_map/scale/pallas_call | solution.py:358
  45.2 2.4 %greens.2 = (f32[128,256]{1,0:T(8,128)S(1)}, f32[128,256]{1,0:T(8,128)S(1)}, f32[128,256]{1,0:T(8,128)S(1)}, f32[128,256]{1,0:T(8,128)S(1)}) custom-call(s32[3]{0:T(128)S(1)} %pad_add_fusion.refs_0_.place, f32[4,4]{1,0:T(4,128)S(1)} %copy-done.1, bf16[512,1024]{1,0:T(8,128)(2,1)S(1)} %get-tuple-element.45.refs_2_, ...), custom_call_target="tpu_custom_call" | custom-call | flops 3000000000 | tf_op jit(solution)/shard_map/greens/pallas_call | solution.py:368
  47.6 0.6 collective-permute-start.20
  48.3 3.5 %collective-permute-start.21 = (f32[128,256]{1,0:T(8,128)S(1)}, f32[128,256]{1,0:T(8,128)S(1)}, u32[]{:S(2)}, u32[]{:S(2)}) collective-permute-start(f32[128,256]{1,0:T(8,128)S(1)} %get-tuple-element.63), channel_id=1, source_target_pairs={{0,16},{8,24},{16,0},{24,8},{1,17},{9,25},{17,1},{25,9},{2,18},{10... | collective-permute-start | bytes 393224 | tf_op jit(solution)/shard_map/ppermute | solution.py:26
  51.7 0.3 collective-permute-start.22
  52.1 1.6 %scale.7 = (bf16[512,1024]{1,0:T(8,128)(2,1)S(1)}, bf16[512,1024]{1,0:T(8,128)(2,1)S(1)}) custom-call(s32[3]{0:T(128)S(1)} %pad_add_fusion.refs_0_.place, f32[2,2,2,136,128]{4,3,2,1,0:T(8,128)S(1)} %pack.4.refs_1_, f32[2,2,2,136,128]{4,3,2,1,0:T(8,128)S(1)} %collective-permute-done.10.refs_2_, f32[8,128]{1,0:T(8,128)S(1)} %slice.12.refs_3_, ...), custom_call_target="tpu_custom_call" | custom-call | tf_op jit(solution)/shard_map/scale/pallas_call | solution.py:358
  53.8 1.7 %scale.6 = (bf16[512,1024]{1,0:T(8,128)(2,1)S(1)}, bf16[512,1024]{1,0:T(8,128)(2,1)S(1)}) custom-call(s32[3]{0:T(128)S(1)} %pad_add_fusion.refs_0_.place, f32[2,2,2,136,128]{4,3,2,1,0:T(8,128)S(1)} %pad_maximum_fusion.refs_1_, f32[2,2,2,136,128]{4,3,2,1,0:T(8,128)S(1)} %collective-permute-done.2.refs_2_, f32[8,128]{1,0:T(8,128)S(1)} %slice.12.refs_3_, ...), custom_call_target="tpu_custom_call" | custom-call | tf_op jit(solution)/shard_map/scale/pallas_call | solution.py:358
  55.4 2.5 %greens.3 = (f32[128,256]{1,0:T(8,128)S(1)}, f32[128,256]{1,0:T(8,128)S(1)}, f32[128,256]{1,0:T(8,128)S(1)}, f32[128,256]{1,0:T(8,128)S(1)}) custom-call(s32[3]{0:T(128)S(1)} %pad_add_fusion.refs_0_.place, f32[4,4]{1,0:T(4,128)S(1)} %copy-done.1, bf16[512,1024]{1,0:T(8,128)(2,1)S(1)} %get-tuple-element.54.refs_2_, ...), custom_call_target="tpu_custom_call" | custom-call | flops 3000000000 | tf_op jit(solution)/shard_map/greens/pallas_call | solution.py:368
  57.9 0.3 collective-permute-start.15
  58.2 3.1 %collective-permute-done.21.refs_2_ = f32[128,256]{1,0:T(8,128)S(1)} collective-permute-done((f32[128,256]{1,0:T(8,128)S(1)}, f32[128,256]{1,0:T(8,128)S(1)}, u32[]{:S(2)}, u32[]{:S(2)}) %collective-permute-start.21) | collective-permute-done | bytes 131104 | tf_op jit(solution)/shard_map/ppermute | solution.py:26
  61.3 1.9 %collective-permute-done.15.refs_1_.refs_4_ = f32[128,256]{1,0:T(8,128)S(1)} collective-permute-done((f32[128,256]{1,0:T(8,128)S(1)}, f32[128,256]{1,0:T(8,128)S(1)}, u32[]{:S(2)}, u32[]{:S(2)}) %collective-permute-start.15) | collective-permute-done | bytes 131104 | tf_op jit(solution)/shard_map/ppermute | solution.py:26
  63.3 0.1 collective-permute-start.23
  63.4 0.6 collective-permute-start.16
  63.9 1.7 %collective-permute-start.17 = (f32[128,256]{1,0:T(8,128)S(1)}, f32[128,256]{1,0:T(8,128)S(1)}, u32[]{:S(2)}, u32[]{:S(2)}) collective-permute-start(f32[128,256]{1,0:T(8,128)S(1)} %get-tuple-element.60), channel_id=1, source_target_pairs={{0,16},{8,24},{16,0},{24,8},{1,17},{9,25},{17,1},{25,9},{2,18},{10... | collective-permute-start | bytes 393224 | tf_op jit(solution)/shard_map/ppermute | solution.py:26
  65.6 1.5 %collective-permute-start.18 = (f32[128,256]{1,0:T(8,128)S(1)}, f32[128,256]{1,0:T(8,128)S(1)}, u32[]{:S(2)}, u32[]{:S(2)}) collective-permute-start(f32[128,256]{1,0:T(8,128)S(1)} %get-tuple-element.61), channel_id=1, source_target_pairs={{0,24},{8,16},{16,8},{24,0},{1,25},{9,17},{17,9},{25,1},{2,26},{10... | collective-permute-start | bytes 393224 | tf_op jit(solution)/shard_map/ppermute | solution.py:26
  67.1 1.1 %modes.4 = (f32[512,128]{1,0:T(8,128)S(1)}, bf16[2,1024,256]{2,1,0:T(8,128)(2,1)S(1)}) custom-call(bf16[2,512,1024]{2,1,0:T(8,128)(2,1)S(1)} %get-tuple-element.37.refs_3_.high, bf16[2,512,1024]{2,1,0:T(8,128)(2,1)S(1)} %get-tuple-element.38.low, f32[4,128,256]{2,1,0:T(8,128)S(1)} %pack.7.refs_0_, f32[4,128,256]{2,1,0:T(8,128)S(1)} %collective-permute-done.23.refs_1_), custom_call_target="tpu_custom_call" | custom-call | tf_op jit(solution)/shard_map/modes/pallas_call | solution.py:423
  68.1 1.7 %collective-permute-start.24 = (f32[512,128]{1,0:T(8,128)S(1)}, f32[512,128]{1,0:T(8,128)S(1)}, u32[]{:S(2)}, u32[]{:S(2)}) collective-permute-start(f32[512,128]{1,0:T(8,128)S(1)} %get-tuple-element.65), channel_id=1, source_target_pairs={{0,2},{1,3},{2,0},{3,1},{4,6},{5,7},{6,4},{7,5},{8,10},{9,11},{10,... | collective-permute-start | bytes 786440 | tf_op jit(solution)/shard_map/ppermute | solution.py:26
  69.9 6.6 %collective-permute-done.17.refs_0_ = f32[128,256]{1,0:T(8,128)S(1)} collective-permute-done((f32[128,256]{1,0:T(8,128)S(1)}, f32[128,256]{1,0:T(8,128)S(1)}, u32[]{:S(2)}, u32[]{:S(2)}) %collective-permute-start.17) | collective-permute-done | bytes 131104 | tf_op jit(solution)/shard_map/ppermute | solution.py:26
  76.6 0.1 collective-permute-start.19
  76.7 1.5 %collective-permute-done.19.refs_3_ = f32[2,128,256]{2,1,0:T(8,128)S(1)} collective-permute-done((f32[2,128,256]{2,1,0:T(8,128)S(1)}, f32[2,128,256]{2,1,0:T(8,128)S(1)}, u32[]{:S(2)}, u32[]{:S(2)}) %collective-permute-start.19) | collective-permute-done | bytes 262176 | tf_op jit(solution)/shard_map/ppermute | solution.py:26
  78.2 0.9 modes.5
  79.0 1.3 %collective-permute-start.25 = (f32[512,128]{1,0:T(8,128)S(1)}, f32[512,128]{1,0:T(8,128)S(1)}, u32[]{:S(2)}, u32[]{:S(2)}) collective-permute-start(f32[512,128]{1,0:T(8,128)S(1)} %get-tuple-element.66), channel_id=1, source_target_pairs={{0,2},{1,3},{2,0},{3,1},{4,6},{5,7},{6,4},{7,5},{8,10},{9,11},{10,... | collective-permute-start | bytes 786440 | tf_op jit(solution)/shard_map/ppermute | solution.py:26
  80.4 0.7 modes.6.refs_0_
  81.1 0.7 modes.7.refs_2_
  81.8 1.5 %assemble.2.refs_1_ = f32[1,512,512]{2,1,0:T(8,128)} custom-call(s32[3]{0:T(128)S(1)} %pad_add_fusion.refs_0_.place, f32[512,128]{1,0:T(8,128)S(1)} %modes.6.refs_0_, f32[512,128]{1,0:T(8,128)S(1)} %collective-permute-done.24._.refs_1_, f32[512,128]{1,0:T(8,128)S(1)} %modes.7.refs_2_), custom_call_target="tpu_custom_call" | custom-call | tf_op jit(solution)/shard_map/assemble/pallas_call | solution.py:383
  83.3 4.2 %collective-permute-done.25.refs_0_ = f32[512,128]{1,0:T(8,128)S(1)} collective-permute-done((f32[512,128]{1,0:T(8,128)S(1)}, f32[512,128]{1,0:T(8,128)S(1)}, u32[]{:S(2)}, u32[]{:S(2)}) %collective-permute-start.25) | collective-permute-done | bytes 262176 | tf_op jit(solution)/shard_map/ppermute | solution.py:26
  87.4 1.3 %assemble.3 = f32[1,512,512]{2,1,0:T(8,128)} custom-call(s32[3]{0:T(128)S(1)} %pad_add_fusion.refs_0_.place, f32[512,128]{1,0:T(8,128)S(1)} %collective-permute-done.25.refs_0_, f32[1,512,512]{2,1,0:T(8,128)} %assemble.2.refs_1_), custom_call_target="tpu_custom_call", output_to_operand_aliasing={{}: (2, {})} | custom-call | tf_op jit(solution)/shard_map/assemble/pallas_call | solution.py:383
  (45 shorter events, 0.4 us)
Async XLA Ops:
  2.8 12.0 %copy-start.2 = (f32[2,136,128]{2,1,0:T(8,128)S(1)}, f32[2,136,128]{2,1,0:T(8,128)}, u32[]{:S(2)}) copy-start(f32[2,136,128]{2,1,0:T(8,128)} %get-tuple-element.39) | copy-start | bytes 417796
  2.8 9.1 %collective-permute-start.3 = (f32[264,128]{1,0:T(8,128)}, f32[264,128]{1,0:T(8,128)S(1)}, u32[]{:S(2)}, u32[]{:S(2)}) collective-permute-start(f32[264,128]{1,0:T(8,128)} %get-tuple-element.42), channel_id=1, source_target_pairs={{0,8},{8,0},{16,24},{24,16},{1,9},{9,1},{17,25},{25,17},{2,10},{10... | collective-permute-start | bytes 405512 | tf_op jit(solution)/shard_map/ppermute | solution.py:26
  5.9 17.9 %collective-permute-start.4 = (f32[264,128]{1,0:T(8,128)}, f32[264,128]{1,0:T(8,128)S(1)}, u32[]{:S(2)}, u32[]{:S(2)}) collective-permute-start(f32[264,128]{1,0:T(8,128)} %get-tuple-element.43), channel_id=1, source_target_pairs={{0,16},{8,24},{16,0},{24,8},{1,17},{9,25},{17,1},{25,9},{2,18},{10... | collective-permute-start | bytes 405512 | tf_op jit(solution)/shard_map/ppermute | solution.py:26
  8.4 12.1 %collective-permute-start.5 = (f32[264,128]{1,0:T(8,128)}, f32[264,128]{1,0:T(8,128)S(1)}, u32[]{:S(2)}, u32[]{:S(2)}) collective-permute-start(f32[264,128]{1,0:T(8,128)} %get-tuple-element.44), channel_id=1, source_target_pairs={{0,24},{8,16},{16,8},{24,0},{1,25},{9,17},{17,9},{25,1},{2,26},{10... | collective-permute-start | bytes 405512 | tf_op jit(solution)/shard_map/ppermute | solution.py:26
  8.4 6.3 %collective-permute-start = (f32[2,136,128]{2,1,0:T(8,128)}, f32[2,136,128]{2,1,0:T(8,128)S(1)}, u32[]{:S(2)}, u32[]{:S(2)}) collective-permute-start(f32[2,136,128]{2,1,0:T(8,128)} %get-tuple-element.40), channel_id=1, source_target_pairs={{0,2},{1,3},{2,0},{3,1},{4,6},{5,7},{6,4},{7,5},{8,10},{9,11},{10,... | collective-permute-start | bytes 417800 | tf_op jit(solution)/shard_map/ppermute | solution.py:26
  11.8 0.9 %copy-start = (f32[264,128]{1,0:T(8,128)S(1)}, f32[264,128]{1,0:T(8,128)}, u32[]{:S(2)}) copy-start(f32[264,128]{1,0:T(8,128)} %get-tuple-element.41.refs_0_) | copy-start | bytes 405508
  12.8 7.1 %collective-permute-start.8 = (f32[2,256,128]{2,1,0:T(8,128)S(1)}, f32[2,256,128]{2,1,0:T(8,128)S(1)}, u32[]{:S(2)}, u32[]{:S(2)}) collective-permute-start(f32[2,256,128]{2,1,0:T(8,128)S(1)} %gate.3), channel_id=1, source_target_pairs={{0,4},{4,0},{1,5},{5,1},{2,6},{6,2},{3,7},{7,3},{8,12},{12,8},{9,1... | collective-permute-start | bytes 786440 | tf_op jit(solution)/shard_map/ppermute | solution.py:26
  14.8 12.7 %collective-permute-start.1 = (f32[2,2,136,128]{3,2,1,0:T(8,128)S(1)}, f32[2,2,136,128]{3,2,1,0:T(8,128)S(1)}, u32[]{:S(2)}, u32[]{:S(2)}) collective-permute-start(f32[2,2,136,128]{3,2,1,0:T(8,128)S(1)} %get-tuple-element.70), channel_id=1, source_target_pairs={{0,8},{8,0},{16,24},{24,16},{1,9},{9,1},{17,25},{25,17},{2,10},{10... | collective-permute-start | bytes 835592 | tf_op jit(solution)/shard_map/ppermute | solution.py:26
  15.5 17.2 %collective-permute-start.6 = (f32[2,2,136,128]{3,2,1,0:T(8,128)S(1)}, f32[2,2,136,128]{3,2,1,0:T(8,128)S(1)}, u32[]{:S(2)}, u32[]{:S(2)}) collective-permute-start(f32[2,2,136,128]{3,2,1,0:T(8,128)S(1)} %get-tuple-element.70), channel_id=1, source_target_pairs={{0,16},{8,24},{16,0},{24,8},{1,17},{9,25},{17,1},{25,9},{2,18},{10... | collective-permute-start | bytes 835592 | tf_op jit(solution)/shard_map/ppermute | solution.py:26
  19.9 16.5 %collective-permute-start.9 = (f32[4,256,128]{2,1,0:T(8,128)S(1)}, f32[4,256,128]{2,1,0:T(8,128)S(1)}, u32[]{:S(2)}, u32[]{:S(2)}) collective-permute-start(f32[4,256,128]{2,1,0:T(8,128)S(1)} %pad_maximum_fusion.2.refs_1_), channel_id=1, source_target_pairs={{0,2},{1,3},{2,0},{3,1},{4,6},{5,7},{6,4},{7,5},{8,10},{9,11},{10,... | collective-permute-start | bytes 1572872 | tf_op jit(solution)/shard_map/ppermute | solution.py:26
  20.6 13.9 %collective-permute-start.13 = (f32[1,256,128]{2,1,0:T(8,128)S(1)}, f32[1,256,128]{2,1,0:T(8,128)S(1)}, u32[]{:S(2)}, u32[]{:S(2)}) collective-permute-start(f32[1,256,128]{2,1,0:T(8,128)S(1)} %gate.5), channel_id=1, source_target_pairs={{0,2},{1,3},{2,0},{3,1},{4,6},{5,7},{6,4},{7,5},{8,10},{9,11},{10,... | collective-permute-start | bytes 393224 | tf_op jit(solution)/shard_map/ppermute | solution.py:26
  23.8 12.2 %collective-permute-start.11 = (f32[1,256,128]{2,1,0:T(8,128)S(1)}, f32[1,256,128]{2,1,0:T(8,128)S(1)}, u32[]{:S(2)}, u32[]{:S(2)}) collective-permute-start(f32[1,256,128]{2,1,0:T(8,128)S(1)} %gate.4), channel_id=1, source_target_pairs={{0,4},{4,0},{1,5},{5,1},{2,6},{6,2},{3,7},{7,3},{8,12},{12,8},{9,1... | collective-permute-start | bytes 393224 | tf_op jit(solution)/shard_map/ppermute | solution.py:26
  27.5 9.9 %collective-permute-start.2 = (f32[2,2,2,136,128]{4,3,2,1,0:T(8,128)S(1)}, f32[2,2,2,136,128]{4,3,2,1,0:T(8,128)S(1)}, u32[]{:S(2)}, u32[]{:S(2)}) collective-permute-start(f32[2,2,2,136,128]{4,3,2,1,0:T(8,128)S(1)} %pad_maximum_fusion.refs_1_), channel_id=1, source_target_pairs={{0,1},{1,0},{2,3},{3,2},{4,5},{5,4},{6,7},{7,6},{8,9},{9,8},{10,11... | collective-permute-start | bytes 1671176 | tf_op jit(solution)/shard_map/ppermute | solution.py:26
  32.7 7.3 %collective-permute-start.7 = (f32[2,2,136,128]{3,2,1,0:T(8,128)S(1)}, f32[2,2,136,128]{3,2,1,0:T(8,128)S(1)}, u32[]{:S(2)}, u32[]{:S(2)}) collective-permute-start(f32[2,2,136,128]{3,2,1,0:T(8,128)S(1)} %collective-permute-done.6.refs_0_), channel_id=1, source_target_pairs={{0,8},{8,0},{16,24},{24,16},{1,9},{9,1},{17,25},{25,17},{2,10},{10... | collective-permute-start | bytes 835592 | tf_op jit(solution)/shard_map/ppermute | solution.py:26
  34.5 6.4 %collective-permute-start.14 = (f32[2,256,128]{2,1,0:T(8,128)S(1)}, f32[2,256,128]{2,1,0:T(8,128)S(1)}, u32[]{:S(2)}, u32[]{:S(2)}) collective-permute-start(f32[2,256,128]{2,1,0:T(8,128)S(1)} %pad_maximum_fusion.5.refs_3_), channel_id=1, source_target_pairs={{0,4},{4,0},{1,5},{5,1},{2,6},{6,2},{3,7},{7,3},{8,12},{12,8},{9,1... | collective-permute-start | bytes 786440 | tf_op jit(solution)/shard_map/ppermute | solution.py:26
  36.0 6.4 %collective-permute-start.12 = (f32[2,256,128]{2,1,0:T(8,128)S(1)}, f32[2,256,128]{2,1,0:T(8,128)S(1)}, u32[]{:S(2)}, u32[]{:S(2)}) collective-permute-start(f32[2,256,128]{2,1,0:T(8,128)S(1)} %pad_maximum_fusion.4.refs_1_), channel_id=1, source_target_pairs={{0,2},{1,3},{2,0},{3,1},{4,6},{5,7},{6,4},{7,5},{8,10},{9,11},{10,... | collective-permute-start | bytes 786440 | tf_op jit(solution)/shard_map/ppermute | solution.py:26
  40.0 5.2 %copy-start.1 = (f32[4,4]{1,0:T(4,128)S(1)}, f32[4,4]{1,0:T(4,128)}, u32[]{:S(2)}) copy-start(f32[4,4]{1,0:T(4,128)} %refs_1_.3) | copy-start | bytes 196
  40.0 3.5 %collective-permute-start.10 = (f32[2,2,2,136,128]{4,3,2,1,0:T(8,128)S(1)}, f32[2,2,2,136,128]{4,3,2,1,0:T(8,128)S(1)}, u32[]{:S(2)}, u32[]{:S(2)}) collective-permute-start(f32[2,2,2,136,128]{4,3,2,1,0:T(8,128)S(1)} %pack.4.refs_1_), channel_id=1, source_target_pairs={{0,1},{1,0},{2,3},{3,2},{4,5},{5,4},{6,7},{7,6},{8,9},{9,8},{10,11... | collective-permute-start | bytes 1671176 | tf_op jit(solution)/shard_map/ppermute | solution.py:26
  47.6 10.5 %collective-permute-start.20 = (f32[128,256]{1,0:T(8,128)S(1)}, f32[128,256]{1,0:T(8,128)S(1)}, u32[]{:S(2)}, u32[]{:S(2)}) collective-permute-start(f32[128,256]{1,0:T(8,128)S(1)} %get-tuple-element.62), channel_id=1, source_target_pairs={{0,8},{8,0},{16,24},{24,16},{1,9},{9,1},{17,25},{25,17},{2,10},{10... | collective-permute-start | bytes 393224 | tf_op jit(solution)/shard_map/ppermute | solution.py:26
  48.3 13.0 %collective-permute-start.21 = (f32[128,256]{1,0:T(8,128)S(1)}, f32[128,256]{1,0:T(8,128)S(1)}, u32[]{:S(2)}, u32[]{:S(2)}) collective-permute-start(f32[128,256]{1,0:T(8,128)S(1)} %get-tuple-element.63), channel_id=1, source_target_pairs={{0,16},{8,24},{16,0},{24,8},{1,17},{9,25},{17,1},{25,9},{2,18},{10... | collective-permute-start | bytes 393224 | tf_op jit(solution)/shard_map/ppermute | solution.py:26
  51.7 9.5 %collective-permute-start.22 = (f32[128,256]{1,0:T(8,128)S(1)}, f32[128,256]{1,0:T(8,128)S(1)}, u32[]{:S(2)}, u32[]{:S(2)}) collective-permute-start(f32[128,256]{1,0:T(8,128)S(1)} %get-tuple-element.64), channel_id=1, source_target_pairs={{0,24},{8,16},{16,8},{24,0},{1,25},{9,17},{17,9},{25,1},{2,26},{10... | collective-permute-start | bytes 393224 | tf_op jit(solution)/shard_map/ppermute | solution.py:26
  57.9 5.4 %collective-permute-start.15 = (f32[128,256]{1,0:T(8,128)S(1)}, f32[128,256]{1,0:T(8,128)S(1)}, u32[]{:S(2)}, u32[]{:S(2)}) collective-permute-start(f32[128,256]{1,0:T(8,128)S(1)} %get-tuple-element.59), channel_id=1, source_target_pairs={{0,8},{8,0},{16,24},{24,16},{1,9},{9,1},{17,25},{25,17},{2,10},{10... | collective-permute-start | bytes 393224 | tf_op jit(solution)/shard_map/ppermute | solution.py:26
  63.3 3.8 %collective-permute-start.23 = (f32[4,128,256]{2,1,0:T(8,128)S(1)}, f32[4,128,256]{2,1,0:T(8,128)S(1)}, u32[]{:S(2)}, u32[]{:S(2)}) collective-permute-start(f32[4,128,256]{2,1,0:T(8,128)S(1)} %pack.7.refs_0_), channel_id=1, source_target_pairs={{0,1},{1,0},{2,3},{3,2},{4,5},{5,4},{6,7},{7,6},{8,9},{9,8},{10,11... | collective-permute-start | bytes 1572872 | tf_op jit(solution)/shard_map/ppermute | solution.py:26
  63.4 13.2 %collective-permute-start.16 = (f32[2,128,256]{2,1,0:T(8,128)S(1)}, f32[2,128,256]{2,1,0:T(8,128)S(1)}, u32[]{:S(2)}, u32[]{:S(2)}) collective-permute-start(f32[2,128,256]{2,1,0:T(8,128)S(1)} %pack.5.refs_0_), channel_id=1, source_target_pairs={{0,1},{1,0},{2,3},{3,2},{4,5},{5,4},{6,7},{7,6},{8,9},{9,8},{10,11... | collective-permute-start | bytes 786440 | tf_op jit(solution)/shard_map/ppermute | solution.py:26
  63.9 12.6 %collective-permute-start.17 = (f32[128,256]{1,0:T(8,128)S(1)}, f32[128,256]{1,0:T(8,128)S(1)}, u32[]{:S(2)}, u32[]{:S(2)}) collective-permute-start(f32[128,256]{1,0:T(8,128)S(1)} %get-tuple-element.60), channel_id=1, source_target_pairs={{0,16},{8,24},{16,0},{24,8},{1,17},{9,25},{17,1},{25,9},{2,18},{10... | collective-permute-start | bytes 393224 | tf_op jit(solution)/shard_map/ppermute | solution.py:26
  65.6 10.9 %collective-permute-start.18 = (f32[128,256]{1,0:T(8,128)S(1)}, f32[128,256]{1,0:T(8,128)S(1)}, u32[]{:S(2)}, u32[]{:S(2)}) collective-permute-start(f32[128,256]{1,0:T(8,128)S(1)} %get-tuple-element.61), channel_id=1, source_target_pairs={{0,24},{8,16},{16,8},{24,0},{1,25},{9,17},{17,9},{25,1},{2,26},{10... | collective-permute-start | bytes 393224 | tf_op jit(solution)/shard_map/ppermute | solution.py:26
  68.1 8.5 %collective-permute-start.24 = (f32[512,128]{1,0:T(8,128)S(1)}, f32[512,128]{1,0:T(8,128)S(1)}, u32[]{:S(2)}, u32[]{:S(2)}) collective-permute-start(f32[512,128]{1,0:T(8,128)S(1)} %get-tuple-element.65), channel_id=1, source_target_pairs={{0,2},{1,3},{2,0},{3,1},{4,6},{5,7},{6,4},{7,5},{8,10},{9,11},{10,... | collective-permute-start | bytes 786440 | tf_op jit(solution)/shard_map/ppermute | solution.py:26
  76.6 1.6 %collective-permute-start.19 = (f32[2,128,256]{2,1,0:T(8,128)S(1)}, f32[2,128,256]{2,1,0:T(8,128)S(1)}, u32[]{:S(2)}, u32[]{:S(2)}) collective-permute-start(f32[2,128,256]{2,1,0:T(8,128)S(1)} %pack.6.refs_2_), channel_id=1, source_target_pairs={{0,1},{1,0},{2,3},{3,2},{4,5},{5,4},{6,7},{7,6},{8,9},{9,8},{10,11... | collective-permute-start | bytes 786440 | tf_op jit(solution)/shard_map/ppermute | solution.py:26
  79.0 8.4 %collective-permute-start.25 = (f32[512,128]{1,0:T(8,128)S(1)}, f32[512,128]{1,0:T(8,128)S(1)}, u32[]{:S(2)}, u32[]{:S(2)}) collective-permute-start(f32[512,128]{1,0:T(8,128)S(1)} %get-tuple-element.66), channel_id=1, source_target_pairs={{0,2},{1,3},{2,0},{3,1},{4,6},{5,7},{6,4},{7,5},{8,10},{9,11},{10,... | collective-permute-start | bytes 786440 | tf_op jit(solution)/shard_map/ppermute | solution.py:26
